TPU v7x, 128 devices: a whole 4x4x4 slice. The times are simulated.
128 devices in a mesh: grp: 4 (over y), slab: 32 (over x, z, core).
Axes of the slice: x: 4, y: 4, z: 4, core: 2. Of those that a mesh axis runs over, the one named last changes fastest.
Arguments:
- right_side: float32 [256, 256, 256], P(('grp', 'slab')), may hold values from -8 to 8
- conductivity: float32 [256, 256, 256], P(('grp', 'slab')), may hold values from 0.1 to 10
Outputs:
- iterate: float32 [256, 256, 256], P(('grp', 'slab'))
- final_defect: float32 [256, 256, 256], P(('grp', 'slab'))
All inputs are finite; a program needn't handle non-finite values.
Results may differ from a plain program's by a relative error of at most 0.00016.
Values sent between devices are 32-bit elements; how exact they have to be, the bound alone decides.
No kernel may reach another device: no remote copies, remote signals or barrier semaphores. Data moves between devices by JAX's collectives and lax.ppermute only.
A program may use at most 128 MiB of HBM per device.

v0:
```python
import jax
import jax.numpy as jnp
from jax import lax
from jax.sharding import PartitionSpec as P

KF = 2
KC = 4


LOWER = 0.25
UPPER = 2.0
SHIFTS = ((1, 0, 0), (-1, 0, 0), (0, 1, 0), (0, -1, 0), (0, 0, 1), (0, 0, -1))


def extended(block, sides, width):
    for axis, dim in sides:
        count = lax.axis_size(axis)
        forward = [(i, i + 1) for i in range(count - 1)]
        backward = [(target, source) for source, target in forward]
        low = lax.ppermute(
            lax.slice_in_dim(block, block.shape[dim] - width, None, axis=dim), axis, forward
        )
        high = lax.ppermute(lax.slice_in_dim(block, 0, width, axis=dim), axis, backward)
        block = jnp.concatenate([low, block, high], axis=dim)
    return block


def shifted(padded, offz, offx, offy):
    return padded[
        1 + offz : padded.shape[0] - 1 + offz,
        1 + offx : padded.shape[1] - 1 + offx,
        1 + offy : padded.shape[2] - 1 + offy,
    ]


def pad_sides(field):
    return jnp.pad(field, ((0, 0), (1, 1), (1, 1)))


def operate(field_zpad, coef_pad, weight):
    full = pad_sides(field_zpad)
    center = shifted(full, 0, 0, 0)
    coef_mid = shifted(coef_pad, 0, 0, 0)
    total = jnp.zeros(center.shape, jnp.float32)
    for offset in SHIFTS:
        face = 0.5 * (coef_mid + shifted(coef_pad, *offset))
        total = total + face * (center - shifted(full, *offset))
    return weight * total


def diagonal_of(coef_pad, weight):
    coef_mid = shifted(coef_pad, 0, 0, 0)
    total = jnp.zeros(coef_mid.shape, jnp.float32)
    for offset in SHIFTS:
        total = total + 0.5 * (coef_mid + shifted(coef_pad, *offset))
    return weight * total


def restrict(field):
    planes, rows, cols = field.shape
    return jnp.mean(field.reshape(planes // 2, 2, rows // 2, 2, cols // 2, 2), axis=(1, 3, 5))


def prolong(field):
    return jnp.repeat(jnp.repeat(jnp.repeat(field, 2, axis=0), 2, axis=1), 2, axis=2)


def chebyshev(start, source, apply_op, inv_diag, count):
    center_val = (UPPER + LOWER) / 2.0
    half_width = (UPPER - LOWER) / 2.0
    ratio_val = center_val / half_width
    rho_now = 1.0 / ratio_val
    current = start
    update = inv_diag * (source - apply_op(current)) / center_val
    current = current + update
    for sweep_index in range(count - 1):
        rho_new = 1.0 / (2.0 * ratio_val - rho_now)
        update = rho_new * rho_now * update + 2.0 * rho_new / half_width * inv_diag * (
            source - apply_op(current)
        )
        current = current + update
        rho_now = rho_new
    return current


def local(right_side, conductivity):
    coef_rows = extended(conductivity, ((("grp", "slab"), 0),), 1)
    fine_coef = pad_sides(coef_rows)

    def fine_apply(field):
        return operate(extended(field, ((("grp", "slab"), 0),), 1), fine_coef, 1.0)

    inv_fine = 1.0 / diagonal_of(fine_coef, 1.0)
    coarse_local = restrict(conductivity)
    own_planes = coarse_local.shape[0]
    group_coef = lax.all_gather(coarse_local, "slab", axis=0, tiled=True)
    group_rows = extended(group_coef, (("grp", 0),), 1)
    coarse_coef = pad_sides(group_rows)

    def coarse_apply(field):
        return operate(extended(field, (("grp", 0),), 1), coarse_coef, 0.25)

    coarse_diag = diagonal_of(coarse_coef, 0.25)
    inv_coarse = 1.0 / coarse_diag
    column_diag = jnp.sum(coarse_diag, axis=0)
    iterate = jnp.zeros(right_side.shape, jnp.float32)
    iterate = chebyshev(iterate, right_side, fine_apply, inv_fine, KF)
    defect = right_side - fine_apply(iterate)
    group_rhs = lax.all_gather(restrict(defect), "slab", axis=0, tiled=True)
    group_corr = chebyshev(
        jnp.zeros(group_rhs.shape, jnp.float32), group_rhs, coarse_apply, inv_coarse, KC
    )
    column_defect = jnp.sum(group_rhs - coarse_apply(group_corr), axis=0)
    group_corr = group_corr + (column_defect / column_diag)[None, :, :]
    first_plane = lax.axis_index("slab") * own_planes
    correction = lax.dynamic_slice_in_dim(group_corr, first_plane, own_planes, 0)
    iterate = iterate + prolong(correction)
    iterate = chebyshev(iterate, right_side, fine_apply, inv_fine, KF)
    final_defect = right_side - fine_apply(iterate)
    return (iterate, final_defect)


def solution(mesh):
    placed = (P(("grp", "slab"), None, None), P(("grp", "slab"), None, None))
    return jax.shard_map(
        local,
        mesh=mesh,
        in_specs=placed,
        out_specs=(P(("grp", "slab"), None, None), P(("grp", "slab"), None, None)),
        check_vma=False,
    )
```

profile of v0, /device:TPU:24, one launch (start us, length us, event | category | flops | bytes accessed | tf_op | source)
XLA Modules:
  0.0 354.1 jit_solution(15073669002580579363)
XLA Ops:
  8.3 7.8 %collective-permute-start = (f32[1,256,256]{2,1,0:T(8,128)S(1)}, f32[1,256,256]{2,1,0:T(8,128)S(1)}, u32[]{:S(2)}, u32[]{:S(2)}) collective-permute-start(f32[1,256,256]{2,1,0:T(8,128)S(1)} %get-tuple-element.44), channel_id=1, source_target_pairs={{1,0},{2,1},{3,2},{4,3},{5,4},{6,5},{7,6},{8,7},{9,8},{10,9},{11,1... | collective-permute-start | bytes 786440 | tf_op jit(solution)/shard_map/ppermute | solution.py:23
  18.0 7.9 %collective-permute-start.2 = (f32[1,256,256]{2,1,0:T(8,128)S(1)}, f32[1,256,256]{2,1,0:T(8,128)S(1)}, u32[]{:S(2)}, u32[]{:S(2)}) collective-permute-start(f32[1,256,256]{2,1,0:T(8,128)S(1)} %broadcast.95), channel_id=1, source_target_pairs={{1,0},{2,1},{3,2},{4,3},{5,4},{6,5},{7,6},{8,7},{9,8},{10,9},{11,1... | collective-permute-start | bytes 786440 | tf_op jit(solution)/shard_map/ppermute | solution.py:23
  29.7 8.0 %collective-permute-done.3 = f32[1,256,256]{2,1,0:T(8,128)S(1)} collective-permute-done((f32[1,256,256]{2,1,0:T(8,128)S(1)}, f32[1,256,256]{2,1,0:T(8,128)S(1)}, u32[]{:S(2)}, u32[]{:S(2)}) %collective-permute-start.3) | collective-permute-done | bytes 262176 | tf_op jit(solution)/shard_map/ppermute | solution.py:20
  40.6 18.1 %reduce_sum.43 = f32[128,2,128,2]{3,2,1,0:T(8,128)} reshape(f32[256,256]{1,0:T(8,128)S(1)} %get-tuple-element.38) | data formatting | bytes 524288 | tf_op jit(solution)/shard_map/reduce_sum | solution.py:61
  58.7 8.0 %reduce_sum.52 = f32[128,128]{1,0:T(8,128)S(1)} reduce(f32[128,2,128,2]{3,2,1,0:T(8,128)} %reduce_sum.43, f32[]{:T(128)} %constant.17.clone.1), dimensions={1,3}, to_apply=%region_1.2 | reduce | flops 49152 | bytes 327684 | tf_op jit(solution)/shard_map/reduce_sum | solution.py:61
  73.4 8.5 %collective-permute-done.5 = f32[1,256,256]{2,1,0:T(8,128)S(1)} collective-permute-done((f32[1,256,256]{2,1,0:T(8,128)S(1)}, f32[1,256,256]{2,1,0:T(8,128)S(1)}, u32[]{:S(2)}, u32[]{:S(2)}) %collective-permute-start.5) | collective-permute-done | bytes 262176 | tf_op jit(solution)/shard_map/ppermute | solution.py:20
  86.8 2.6 collective-permute-start.9
  90.6 8.1 %collective-permute-done.9 = f32[1,256,256]{2,1,0:T(8,128)S(1)} collective-permute-done((f32[1,256,256]{2,1,0:T(8,128)S(1)}, f32[1,256,256]{2,1,0:T(8,128)S(1)}, u32[]{:S(2)}, u32[]{:S(2)}) %collective-permute-start.9) | collective-permute-done | bytes 262176 | tf_op jit(solution)/shard_map/ppermute | solution.py:20
  99.9 18.1 %reduce_sum.54 = f32[128,2,128,2]{3,2,1,0:T(8,128)} reshape(f32[256,256]{1,0:T(8,128)S(1)} %fusion.161) | data formatting | bytes 524288 | tf_op jit(solution)/shard_map/reduce_sum | solution.py:61
  118.0 8.0 %reduce_sum.55 = f32[128,128]{1,0:T(8,128)S(1)} reduce(f32[128,2,128,2]{3,2,1,0:T(8,128)} %reduce_sum.54, f32[]{:T(128)} %constant.17.clone.1), dimensions={1,3}, to_apply=%region_3.4 | reduce | flops 49152 | bytes 327684 | tf_op jit(solution)/shard_map/reduce_sum | solution.py:61
  132.5 5.2 %collective-permute-start.6 = (f32[1,128,128]{2,1,0:T(8,128)S(1)}, f32[1,128,128]{2,1,0:T(8,128)S(1)}, u32[]{:S(2)}, u32[]{:S(2)}) collective-permute-start(f32[1,128,128]{2,1,0:T(8,128)S(1)} %get-tuple-element.30), channel_id=1, source_target_pairs={{32,0},{64,32},{96,64},{33,1},{65,33},{97,65},{34,2},{66,34},{98,6... | collective-permute-start | bytes 196616 | tf_op jit(solution)/shard_map/ppermute | solution.py:23
  138.0 4.3 %select_maximum_fusion.8 = f32[34,130,130]{2,1,0:T(8,128)} fusion(f32[1,128,128]{2,1,0:T(8,128)S(1)} %collective-permute-done.10, f32[32,128,128]{2,1,0:T(8,128)S(1)} %broadcast_in_dim.21, f32[1,128,128]{2,1,0:T(8,128)S(1)} %collective-permute-done.11), kind=kLoop, calls=%fused_computation.12 | loop fusion | flops 8619000 | bytes 4526624 | tf_op jit(solution)/shard_map/concatenate | solution.py:24
  142.3 4.4 %select_maximum_fusion.10 = f32[34,130,130]{2,1,0:T(8,128)} fusion(f32[1,128,128]{2,1,0:T(8,128)S(1)} %collective-permute-done.6, f32[32,128,128]{2,1,0:T(8,128)S(1)} %bitcast.26, f32[1,128,128]{2,1,0:T(8,128)S(1)} %collective-permute-done.7), kind=kLoop, calls=%fused_computation.14 | loop fusion | flops 8619000 | bytes 4526624 | tf_op jit(solution)/shard_map/concatenate | solution.py:24
  146.7 20.1 %all-gather.7.cloned.1.call-done = f32[4096,128]{1,0:T(8,128)} async-done(((f32[128,128]{1,0:T(8,128)}), f32[4096,128]{1,0:T(8,128)}) %all-gather.7.cloned.1.call-update) | async-done | bytes 2097168 | tf_op jit(solution)/shard_map/all_gather | solution.py:109
  166.8 18.7 %broadcast_multiply_fusion = (f32[32,128,128]{2,1,0:T(8,128)}, f32[32,128,128]{2,1,0:T(8,128)}, f32[32,128,128]{2,1,0:T(8,128)}, f32[32,128,128]{2,1,0:T(8,128)}...) fusion(f32[34,130,130]{2,1,0:T(8,128)} %select_maximum_fusion.8, f32[1,128,128]{2,1,0:T(8,128)S(1)} %collective-permute-done.11, ...), kind=kLoop, calls=%fused_computation.169 | loop fusion | flops 22020096 | bytes 35913728 | tf_op jit(solution)/shard_map/div | solution.py:74
  186.4 2.7 collective-permute-start.12
  191.1 4.6 %collective-permute-done.13 = f32[1,128,128]{2,1,0:T(8,128)S(1)} collective-permute-done((f32[1,128,128]{2,1,0:T(8,128)S(1)}, f32[1,128,128]{2,1,0:T(8,128)S(1)}, u32[]{:S(2)}, u32[]{:S(2)}) %collective-permute-start.13) | collective-permute-done | bytes 65568 | tf_op jit(solution)/shard_map/ppermute | solution.py:20
  195.6 5.5 %select_maximum_fusion.6 = f32[34,130,130]{2,1,0:T(8,128)} fusion(f32[1,128,128]{2,1,0:T(8,128)S(1)} %collective-permute-done.12, f32[32,128,128]{2,1,0:T(8,128)} %get-tuple-element.8, f32[1,128,128]{2,1,0:T(8,128)S(1)} %collective-permute-done.13), kind=kLoop, calls=%fused_computation.10 | loop fusion | flops 8619000 | bytes 4526624 | tf_op jit(solution)/shard_map/concatenate | solution.py:24
  201.1 14.4 %fusion.98 = (f32[32,128,128]{2,1,0:T(8,128)}, f32[32,128,128]{2,1,0:T(8,128)}) fusion(f32[32,128,128]{2,1,0:T(8,128)} %get-tuple-element.9, f32[32,128,128]{2,1,0:T(8,128)} %get-tuple-element.13, f32[32,128,128]{2,1,0:T(8,128)} %get-tuple-element.8, f32[34,130,130]{2,1,0:T(8,128)} %select_maximum_fusion.6, f32[32,128,128]{2,1,0:T(8,128)S(1)} %copy-done.5, ...), kind=kLoop, calls=%fused_computation.170 | loop fusion | flops 20971520 | bytes 29622272 | tf_op jit(solution)/shard_map/add | solution.py:81
  220.7 4.3 %collective-permute-done.15 = f32[1,128,128]{2,1,0:T(8,128)S(1)} collective-permute-done((f32[1,128,128]{2,1,0:T(8,128)S(1)}, f32[1,128,128]{2,1,0:T(8,128)S(1)}, u32[]{:S(2)}, u32[]{:S(2)}) %collective-permute-start.15) | collective-permute-done | bytes 65568 | tf_op jit(solution)/shard_map/ppermute | solution.py:20
  225.0 5.5 %select_maximum_fusion.4 = f32[34,130,130]{2,1,0:T(8,128)} fusion(f32[1,128,128]{2,1,0:T(8,128)S(1)} %collective-permute-done.14, f32[32,128,128]{2,1,0:T(8,128)} %get-tuple-element.6, f32[1,128,128]{2,1,0:T(8,128)S(1)} %collective-permute-done.15), kind=kLoop, calls=%fused_computation.8 | loop fusion | flops 8619000 | bytes 4526624 | tf_op jit(solution)/shard_map/concatenate | solution.py:24
  230.5 15.3 %fusion.99 = (f32[32,128,128]{2,1,0:T(8,128)}, f32[32,128,128]{2,1,0:T(8,128)}) fusion(f32[32,128,128]{2,1,0:T(8,128)} %get-tuple-element.7, f32[32,128,128]{2,1,0:T(8,128)} %get-tuple-element.9, f32[32,128,128]{2,1,0:T(8,128)} %get-tuple-element.13, f32[32,128,128]{2,1,0:T(8,128)} %get-tuple-element.6, f32[34,130,130]{2,1,0:T(8,128)} %select_maximum_fusion.4, ...), kind=kLoop, calls=%fused_computation.171 | loop fusion | flops 21495808 | bytes 31719424 | tf_op jit(solution)/shard_map/add | solution.py:81
  250.9 4.3 %collective-permute-done.17 = f32[1,128,128]{2,1,0:T(8,128)S(1)} collective-permute-done((f32[1,128,128]{2,1,0:T(8,128)S(1)}, f32[1,128,128]{2,1,0:T(8,128)S(1)}, u32[]{:S(2)}, u32[]{:S(2)}) %collective-permute-start.17) | collective-permute-done | bytes 65568 | tf_op jit(solution)/shard_map/ppermute | solution.py:20
  255.2 5.5 %select_maximum_fusion.2 = f32[34,130,130]{2,1,0:T(8,128)} fusion(f32[1,128,128]{2,1,0:T(8,128)S(1)} %collective-permute-done.16, f32[32,128,128]{2,1,0:T(8,128)} %get-tuple-element.4, f32[1,128,128]{2,1,0:T(8,128)S(1)} %collective-permute-done.17), kind=kLoop, calls=%fused_computation.6 | loop fusion | flops 8619000 | bytes 4526624 | tf_op jit(solution)/shard_map/concatenate | solution.py:24
  260.7 13.3 %fusion.37 = f32[32,128,128]{2,1,0:T(8,128)} fusion(f32[32,128,128]{2,1,0:T(8,128)} %get-tuple-element.4, f32[32,128,128]{2,1,0:T(8,128)} %get-tuple-element.13, f32[34,130,130]{2,1,0:T(8,128)} %select_maximum_fusion.2, f32[32,128,128]{2,1,0:T(8,128)S(1)} %copy-done.6, f32[32,128,128]{2,1,0:T(8,128)S(1)} %copy-done.4, f32[32,128,128]{2,1,0:T(8,128)S(1)} %copy-done.2, ...), kind=kLoop, calls=%fused_computation.66 | loop fusion | flops 20447232 | bytes 27525120 | tf_op jit(solution)/shard_map/add | solution.py:81
  279.5 3.6 %collective-permute-done.19 = f32[1,128,128]{2,1,0:T(8,128)S(1)} collective-permute-done((f32[1,128,128]{2,1,0:T(8,128)S(1)}, f32[1,128,128]{2,1,0:T(8,128)S(1)}, u32[]{:S(2)}, u32[]{:S(2)}) %collective-permute-start.19) | collective-permute-done | bytes 65568 | tf_op jit(solution)/shard_map/ppermute | solution.py:20
  283.2 4.3 %select_maximum_fusion = f32[34,130,130]{2,1,0:T(8,128)} fusion(f32[1,128,128]{2,1,0:T(8,128)S(1)} %collective-permute-done.18, f32[32,128,128]{2,1,0:T(8,128)S(1)} %copy-done.9, f32[1,128,128]{2,1,0:T(8,128)S(1)} %collective-permute-done.19), kind=kLoop, calls=%fused_computation.4 | loop fusion | flops 8619000 | bytes 4526624 | tf_op jit(solution)/shard_map/concatenate | solution.py:24
  287.5 11.1 %fusion.19 = f32[128,128]{1,0:T(8,128)S(1)} fusion(f32[32,128,128]{2,1,0:T(8,128)S(1)} %bitcast.33, f32[32,128,128]{2,1,0:T(8,128)S(1)} %copy-done.7, f32[32,128,128]{2,1,0:T(8,128)} %fusion.37, f32[34,130,130]{2,1,0:T(8,128)} %select_maximum_fusion, f32[32,128,128]{2,1,0:T(8,128)S(1)} %copy-done.6, f32[32,128,128]{2,1,0:T(8,128)S(1)} %copy-done.4, ...), kind=kLoop, calls=%fused_computation.42 | loop fusion | flops 14663680 | bytes 23396352 | tf_op jit(solution)/shard_map/reduce_sum | solution.py:113
  306.4 8.0 %collective-permute-done.21 = f32[1,256,256]{2,1,0:T(8,128)S(1)} collective-permute-done((f32[1,256,256]{2,1,0:T(8,128)S(1)}, f32[1,256,256]{2,1,0:T(8,128)S(1)}, u32[]{:S(2)}, u32[]{:S(2)}) %collective-permute-start.21) | collective-permute-done | bytes 262176 | tf_op jit(solution)/shard_map/ppermute | solution.py:20
  317.7 2.7 collective-permute-start.23
  321.6 8.0 %collective-permute-done.23 = f32[1,256,256]{2,1,0:T(8,128)S(1)} collective-permute-done((f32[1,256,256]{2,1,0:T(8,128)S(1)}, f32[1,256,256]{2,1,0:T(8,128)S(1)}, u32[]{:S(2)}, u32[]{:S(2)}) %collective-permute-start.23) | collective-permute-done | bytes 262176 | tf_op jit(solution)/shard_map/ppermute | solution.py:20
  336.8 8.0 %collective-permute-done.25 = f32[1,256,256]{2,1,0:T(8,128)S(1)} collective-permute-done((f32[1,256,256]{2,1,0:T(8,128)S(1)}, f32[1,256,256]{2,1,0:T(8,128)S(1)}, u32[]{:S(2)}, u32[]{:S(2)}) %collective-permute-start.25) | collective-permute-done | bytes 262176 | tf_op jit(solution)/shard_map/ppermute | solution.py:20
  (134 shorter events, 69.8 us)
Async XLA Ops:
  7.2 123.2 %all-gather.5.cloned.1.call-start = ((), (), s32[]{:S(2)}) async-start(), calls=%async_computation | async-start | bytes 2162688 | tf_op jit(solution)/shard_map/all_gather | solution.py:96
  8.3 19.5 %collective-permute-start = (f32[1,256,256]{2,1,0:T(8,128)S(1)}, f32[1,256,256]{2,1,0:T(8,128)S(1)}, u32[]{:S(2)}, u32[]{:S(2)}) collective-permute-start(f32[1,256,256]{2,1,0:T(8,128)S(1)} %get-tuple-element.44), channel_id=1, source_target_pairs={{1,0},{2,1},{3,2},{4,3},{5,4},{6,5},{7,6},{8,7},{9,8},{10,9},{11,1... | collective-permute-start | bytes 786440 | tf_op jit(solution)/shard_map/ppermute | solution.py:23
  16.0 11.9 %collective-permute-start.1 = (f32[1,256,256]{2,1,0:T(8,128)S(1)}, f32[1,256,256]{2,1,0:T(8,128)S(1)}, u32[]{:S(2)}, u32[]{:S(2)}) collective-permute-start(f32[1,256,256]{2,1,0:T(8,128)S(1)} %get-tuple-element.43), channel_id=1, source_target_pairs={{0,1},{1,2},{2,3},{3,4},{4,5},{5,6},{6,7},{7,8},{8,9},{9,10},{10,1... | collective-permute-start | bytes 786440 | tf_op jit(solution)/shard_map/ppermute | solution.py:20
  18.0 11.7 %collective-permute-start.2 = (f32[1,256,256]{2,1,0:T(8,128)S(1)}, f32[1,256,256]{2,1,0:T(8,128)S(1)}, u32[]{:S(2)}, u32[]{:S(2)}) collective-permute-start(f32[1,256,256]{2,1,0:T(8,128)S(1)} %broadcast.95), channel_id=1, source_target_pairs={{1,0},{2,1},{3,2},{4,3},{5,4},{6,5},{7,6},{8,7},{9,8},{10,9},{11,1... | collective-permute-start | bytes 786440 | tf_op jit(solution)/shard_map/ppermute | solution.py:23
  25.9 11.9 %collective-permute-start.3 = (f32[1,256,256]{2,1,0:T(8,128)S(1)}, f32[1,256,256]{2,1,0:T(8,128)S(1)}, u32[]{:S(2)}, u32[]{:S(2)}) collective-permute-start(f32[1,256,256]{2,1,0:T(8,128)S(1)} %broadcast.95), channel_id=1, source_target_pairs={{0,1},{1,2},{2,3},{3,4},{4,5},{5,6},{6,7},{7,8},{8,9},{9,10},{10,1... | collective-permute-start | bytes 786440 | tf_op jit(solution)/shard_map/ppermute | solution.py:20
  40.6 58.7 %copy-start.11 = (f32[2,256,256]{2,1,0:T(8,128)}, f32[2,256,256]{2,1,0:T(8,128)S(1)}, u32[]{:S(2)}) copy-start(f32[2,256,256]{2,1,0:T(8,128)S(1)} %get-tuple-element.16) | copy-start | bytes 1572868
  40.6 58.7 %copy-start.13 = (f32[2,256,256]{2,1,0:T(8,128)}, f32[2,256,256]{2,1,0:T(8,128)S(1)}, u32[]{:S(2)}) copy-start(f32[2,256,256]{2,1,0:T(8,128)S(1)} %get-tuple-element.17) | copy-start | bytes 1572868
  40.6 58.7 %copy-start.15 = (f32[2,256,256]{2,1,0:T(8,128)}, f32[2,256,256]{2,1,0:T(8,128)S(1)}, u32[]{:S(2)}) copy-start(f32[2,256,256]{2,1,0:T(8,128)S(1)} %get-tuple-element.18) | copy-start | bytes 1572868
  40.6 58.7 %copy-start.17 = (f32[2,256,256]{2,1,0:T(8,128)}, f32[2,256,256]{2,1,0:T(8,128)S(1)}, u32[]{:S(2)}) copy-start(f32[2,256,256]{2,1,0:T(8,128)S(1)} %get-tuple-element.19) | copy-start | bytes 1572868
  67.3 99.5 %all-gather.7.cloned.1.call-start = ((), (), s32[]{:S(2)}) async-start(), calls=%async_computation.1 | async-start | bytes 2162688 | tf_op jit(solution)/shard_map/all_gather | solution.py:109
  67.4 5.9 %collective-permute-start.4 = (f32[1,256,256]{2,1,0:T(8,128)S(1)}, f32[1,256,256]{2,1,0:T(8,128)S(1)}, u32[]{:S(2)}, u32[]{:S(2)}) collective-permute-start(f32[1,256,256]{2,1,0:T(8,128)S(1)} %get-tuple-element.42), channel_id=1, source_target_pairs={{1,0},{2,1},{3,2},{4,3},{5,4},{6,5},{7,6},{8,7},{9,8},{10,9},{11,1... | collective-permute-start | bytes 786440 | tf_op jit(solution)/shard_map/ppermute | solution.py:23
  69.5 12.3 %collective-permute-start.5 = (f32[1,256,256]{2,1,0:T(8,128)S(1)}, f32[1,256,256]{2,1,0:T(8,128)S(1)}, u32[]{:S(2)}, u32[]{:S(2)}) collective-permute-start(f32[1,256,256]{2,1,0:T(8,128)S(1)} %get-tuple-element.41), channel_id=1, source_target_pairs={{0,1},{1,2},{2,3},{3,4},{4,5},{5,6},{6,7},{7,8},{8,9},{9,10},{10,1... | collective-permute-start | bytes 786440 | tf_op jit(solution)/shard_map/ppermute | solution.py:20
  84.7 5.9 %collective-permute-start.8 = (f32[1,256,256]{2,1,0:T(8,128)S(1)}, f32[1,256,256]{2,1,0:T(8,128)S(1)}, u32[]{:S(2)}, u32[]{:S(2)}) collective-permute-start(f32[1,256,256]{2,1,0:T(8,128)S(1)} %get-tuple-element.40), channel_id=1, source_target_pairs={{1,0},{2,1},{3,2},{4,3},{5,4},{6,5},{7,6},{8,7},{9,8},{10,9},{11,1... | collective-permute-start | bytes 786440 | tf_op jit(solution)/shard_map/ppermute | solution.py:23
  86.8 12.0 %collective-permute-start.9 = (f32[1,256,256]{2,1,0:T(8,128)S(1)}, f32[1,256,256]{2,1,0:T(8,128)S(1)}, u32[]{:S(2)}, u32[]{:S(2)}) collective-permute-start(f32[1,256,256]{2,1,0:T(8,128)S(1)} %get-tuple-element.39), channel_id=1, source_target_pairs={{0,1},{1,2},{2,3},{3,4},{4,5},{5,6},{6,7},{7,8},{8,9},{9,10},{10,1... | collective-permute-start | bytes 786440 | tf_op jit(solution)/shard_map/ppermute | solution.py:20
  126.7 11.0 %collective-permute-start.10 = (f32[1,128,128]{2,1,0:T(8,128)S(1)}, f32[1,128,128]{2,1,0:T(8,128)S(1)}, u32[]{:S(2)}, u32[]{:S(2)}) collective-permute-start(f32[1,128,128]{2,1,0:T(8,128)S(1)} %broadcast.101), channel_id=1, source_target_pairs={{32,0},{64,32},{96,64},{33,1},{65,33},{97,65},{34,2},{66,34},{98,6... | collective-permute-start | bytes 196616 | tf_op jit(solution)/shard_map/ppermute | solution.py:23
  129.0 8.7 %collective-permute-start.11 = (f32[1,128,128]{2,1,0:T(8,128)S(1)}, f32[1,128,128]{2,1,0:T(8,128)S(1)}, u32[]{:S(2)}, u32[]{:S(2)}) collective-permute-start(f32[1,128,128]{2,1,0:T(8,128)S(1)} %broadcast.101), channel_id=1, source_target_pairs={{0,32},{32,64},{64,96},{1,33},{33,65},{65,97},{2,34},{34,66},{66,9... | collective-permute-start | bytes 196616 | tf_op jit(solution)/shard_map/ppermute | solution.py:20
  131.2 11.1 %collective-permute-start.7 = (f32[1,128,128]{2,1,0:T(8,128)S(1)}, f32[1,128,128]{2,1,0:T(8,128)S(1)}, u32[]{:S(2)}, u32[]{:S(2)}) collective-permute-start(f32[1,128,128]{2,1,0:T(8,128)S(1)} %get-tuple-element.31), channel_id=1, source_target_pairs={{0,32},{32,64},{64,96},{1,33},{33,65},{65,97},{2,34},{34,66},{66,9... | collective-permute-start | bytes 196616 | tf_op jit(solution)/shard_map/ppermute | solution.py:20
  132.5 9.8 %collective-permute-start.6 = (f32[1,128,128]{2,1,0:T(8,128)S(1)}, f32[1,128,128]{2,1,0:T(8,128)S(1)}, u32[]{:S(2)}, u32[]{:S(2)}) collective-permute-start(f32[1,128,128]{2,1,0:T(8,128)S(1)} %get-tuple-element.30), channel_id=1, source_target_pairs={{32,0},{64,32},{96,64},{33,1},{65,33},{97,65},{34,2},{66,34},{98,6... | collective-permute-start | bytes 196616 | tf_op jit(solution)/shard_map/ppermute | solution.py:23
  186.4 4.6 %collective-permute-start.12 = (f32[1,128,128]{2,1,0:T(8,128)S(1)}, f32[1,128,128]{2,1,0:T(8,128)S(1)}, u32[]{:S(2)}, u32[]{:S(2)}) collective-permute-start(f32[1,128,128]{2,1,0:T(8,128)S(1)} %get-tuple-element.29), channel_id=1, source_target_pairs={{32,0},{64,32},{96,64},{33,1},{65,33},{97,65},{34,2},{66,34},{98,6... | collective-permute-start | bytes 196616 | tf_op jit(solution)/shard_map/ppermute | solution.py:23
  189.2 6.4 %collective-permute-start.13 = (f32[1,128,128]{2,1,0:T(8,128)S(1)}, f32[1,128,128]{2,1,0:T(8,128)S(1)}, u32[]{:S(2)}, u32[]{:S(2)}) collective-permute-start(f32[1,128,128]{2,1,0:T(8,128)S(1)} %get-tuple-element.28), channel_id=1, source_target_pairs={{0,32},{32,64},{64,96},{1,33},{33,65},{65,97},{2,34},{34,66},{66,9... | collective-permute-start | bytes 196616 | tf_op jit(solution)/shard_map/ppermute | solution.py:20
  216.4 4.3 %collective-permute-start.14 = (f32[1,128,128]{2,1,0:T(8,128)S(1)}, f32[1,128,128]{2,1,0:T(8,128)S(1)}, u32[]{:S(2)}, u32[]{:S(2)}) collective-permute-start(f32[1,128,128]{2,1,0:T(8,128)S(1)} %get-tuple-element.27), channel_id=1, source_target_pairs={{32,0},{64,32},{96,64},{33,1},{65,33},{97,65},{34,2},{66,34},{98,6... | collective-permute-start | bytes 196616 | tf_op jit(solution)/shard_map/ppermute | solution.py:23
  218.8 6.2 %collective-permute-start.15 = (f32[1,128,128]{2,1,0:T(8,128)S(1)}, f32[1,128,128]{2,1,0:T(8,128)S(1)}, u32[]{:S(2)}, u32[]{:S(2)}) collective-permute-start(f32[1,128,128]{2,1,0:T(8,128)S(1)} %get-tuple-element.26), channel_id=1, source_target_pairs={{0,32},{32,64},{64,96},{1,33},{33,65},{65,97},{2,34},{34,66},{66,9... | collective-permute-start | bytes 196616 | tf_op jit(solution)/shard_map/ppermute | solution.py:20
  246.6 4.3 %collective-permute-start.16 = (f32[1,128,128]{2,1,0:T(8,128)S(1)}, f32[1,128,128]{2,1,0:T(8,128)S(1)}, u32[]{:S(2)}, u32[]{:S(2)}) collective-permute-start(f32[1,128,128]{2,1,0:T(8,128)S(1)} %get-tuple-element.25), channel_id=1, source_target_pairs={{32,0},{64,32},{96,64},{33,1},{65,33},{97,65},{34,2},{66,34},{98,6... | collective-permute-start | bytes 196616 | tf_op jit(solution)/shard_map/ppermute | solution.py:23
  249.1 6.2 %collective-permute-start.17 = (f32[1,128,128]{2,1,0:T(8,128)S(1)}, f32[1,128,128]{2,1,0:T(8,128)S(1)}, u32[]{:S(2)}, u32[]{:S(2)}) collective-permute-start(f32[1,128,128]{2,1,0:T(8,128)S(1)} %get-tuple-element.24), channel_id=1, source_target_pairs={{0,32},{32,64},{64,96},{1,33},{33,65},{65,97},{2,34},{34,66},{66,9... | collective-permute-start | bytes 196616 | tf_op jit(solution)/shard_map/ppermute | solution.py:20
  274.9 4.6 %collective-permute-start.18 = (f32[1,128,128]{2,1,0:T(8,128)S(1)}, f32[1,128,128]{2,1,0:T(8,128)S(1)}, u32[]{:S(2)}, u32[]{:S(2)}) collective-permute-start(f32[1,128,128]{2,1,0:T(8,128)S(1)} %get-tuple-element.23), channel_id=1, source_target_pairs={{32,0},{64,32},{96,64},{33,1},{65,33},{97,65},{34,2},{66,34},{98,6... | collective-permute-start | bytes 196616 | tf_op jit(solution)/shard_map/ppermute | solution.py:23
  276.9 6.3 %collective-permute-start.19 = (f32[1,128,128]{2,1,0:T(8,128)S(1)}, f32[1,128,128]{2,1,0:T(8,128)S(1)}, u32[]{:S(2)}, u32[]{:S(2)}) collective-permute-start(f32[1,128,128]{2,1,0:T(8,128)S(1)} %get-tuple-element.22), channel_id=1, source_target_pairs={{0,32},{32,64},{64,96},{1,33},{33,65},{65,97},{2,34},{34,66},{66,9... | collective-permute-start | bytes 196616 | tf_op jit(solution)/shard_map/ppermute | solution.py:20
  300.3 6.1 %collective-permute-start.20 = (f32[1,256,256]{2,1,0:T(8,128)S(1)}, f32[1,256,256]{2,1,0:T(8,128)S(1)}, u32[]{:S(2)}, u32[]{:S(2)}) collective-permute-start(f32[1,256,256]{2,1,0:T(8,128)S(1)} %get-tuple-element.37), channel_id=1, source_target_pairs={{1,0},{2,1},{3,2},{4,3},{5,4},{6,5},{7,6},{8,7},{9,8},{10,9},{11,1... | collective-permute-start | bytes 786440 | tf_op jit(solution)/shard_map/ppermute | solution.py:23
  302.5 11.9 %collective-permute-start.21 = (f32[1,256,256]{2,1,0:T(8,128)S(1)}, f32[1,256,256]{2,1,0:T(8,128)S(1)}, u32[]{:S(2)}, u32[]{:S(2)}) collective-permute-start(f32[1,256,256]{2,1,0:T(8,128)S(1)} %get-tuple-element.36), channel_id=1, source_target_pairs={{0,1},{1,2},{2,3},{3,4},{4,5},{5,6},{6,7},{7,8},{8,9},{9,10},{10,1... | collective-permute-start | bytes 786440 | tf_op jit(solution)/shard_map/ppermute | solution.py:20
  315.8 5.8 %collective-permute-start.22 = (f32[1,256,256]{2,1,0:T(8,128)S(1)}, f32[1,256,256]{2,1,0:T(8,128)S(1)}, u32[]{:S(2)}, u32[]{:S(2)}) collective-permute-start(f32[1,256,256]{2,1,0:T(8,128)S(1)} %get-tuple-element.35), channel_id=1, source_target_pairs={{1,0},{2,1},{3,2},{4,3},{5,4},{6,5},{7,6},{8,7},{9,8},{10,9},{11,1... | collective-permute-start | bytes 786440 | tf_op jit(solution)/shard_map/ppermute | solution.py:23
  317.7 11.9 %collective-permute-start.23 = (f32[1,256,256]{2,1,0:T(8,128)S(1)}, f32[1,256,256]{2,1,0:T(8,128)S(1)}, u32[]{:S(2)}, u32[]{:S(2)}) collective-permute-start(f32[1,256,256]{2,1,0:T(8,128)S(1)} %get-tuple-element.34), channel_id=1, source_target_pairs={{0,1},{1,2},{2,3},{3,4},{4,5},{5,6},{6,7},{7,8},{8,9},{9,10},{10,1... | collective-permute-start | bytes 786440 | tf_op jit(solution)/shard_map/ppermute | solution.py:20
  331.0 5.8 %collective-permute-start.24 = (f32[1,256,256]{2,1,0:T(8,128)S(1)}, f32[1,256,256]{2,1,0:T(8,128)S(1)}, u32[]{:S(2)}, u32[]{:S(2)}) collective-permute-start(f32[1,256,256]{2,1,0:T(8,128)S(1)} %get-tuple-element.33), channel_id=1, source_target_pairs={{1,0},{2,1},{3,2},{4,3},{5,4},{6,5},{7,6},{8,7},{9,8},{10,9},{11,1... | collective-permute-start | bytes 786440 | tf_op jit(solution)/shard_map/ppermute | solution.py:23
  332.9 11.9 %collective-permute-start.25 = (f32[1,256,256]{2,1,0:T(8,128)S(1)}, f32[1,256,256]{2,1,0:T(8,128)S(1)}, u32[]{:S(2)}, u32[]{:S(2)}) collective-permute-start(f32[1,256,256]{2,1,0:T(8,128)S(1)} %get-tuple-element.32), channel_id=1, source_target_pairs={{0,1},{1,2},{2,3},{3,4},{4,5},{5,6},{6,7},{7,8},{8,9},{9,10},{10,1... | collective-permute-start | bytes 786440 | tf_op jit(solution)/shard_map/ppermute | solution.py:20
  (23 other events, 309.8 us)
Sparse Core Ops, SparseCore 0:
  67.5 41.4 all-gather.4
  126.8 39.9 all-gather.6
where the time goes:
time: 361 us; the launch traced here: 354 us
  other arithmetic  134 us (37%)
  waiting for transfers between devices  93.8 us (26%)
  starting transfers between devices  67.8 us (19%)
  local copies, waits for them, and re-layouts  42.8 us (12%)
  between operations  15.3 us (4%)
    ppermute x13, waiting for transfers between devices, extended(): lax.ppermute(lax.slice_in_dim(block, block.shape[dim] - width, None, axis...  65.7 us
    add x6, other arithmetic, chebyshev(): current = current + update  46.7 us
    ppermute x13, starting transfers between devices, extended(): lax.ppermute(lax.slice_in_dim(block, 0, width, axis=dim), axis, backward)  42.8 us
    reduce_sum x2, local copies, waits for them, and re-layouts, restrict(): jnp.mean(field.reshape(planes // 2, 2, rows // 2, 2, cols // 2, 2), axis=...  36.2 us
    concatenate x13, other arithmetic, extended(): block = jnp.concatenate([low, block, high], axis=dim)  34.2 us
    ppermute x13, starting transfers between devices, extended(): lax.ppermute(lax.slice_in_dim(block, block.shape[dim] - width, None, axis...  24.9 us
    div x2, other arithmetic, chebyshev(): update = inv_diag * (source - apply_op(current)) / center_val  20.9 us
    all_gather x1, waiting for transfers between devices, local(): group_rhs = lax.all_gather(restrict(defect), 'slab', axis=0, tiled=True)  20.1 us
  transfers between devices with their start and end apart: 28, of which 21 were waited for; matrix products, arithmetic and copies ran while one was open for 12% of the time, Pallas kernels for 0%

commit v1 on v0

v1 whole, which is shorter than its diff:
```python
import functools

import jax
import jax.numpy as jnp
from jax import lax
from jax.experimental import pallas as pl
from jax.experimental.pallas import tpu as pltpu
from jax.sharding import PartitionSpec as P

KF = 2
KC = 4

LOWER = 0.25
UPPER = 2.0
CENTER = (UPPER + LOWER) / 2.0
HALF = (UPPER - LOWER) / 2.0
RATIO = CENTER / HALF

AXES = ("grp", "slab")
N = 256
NC = 128
PAD = 8
CH = 128
VM = pl.BlockSpec(memory_space=pltpu.VMEM)
ANY = pl.BlockSpec(memory_space=pl.ANY)
HBM = pl.BlockSpec(memory_space=pltpu.HBM)


def chebyshev_factors(count):
    rho = 1.0 / RATIO
    found = []
    for _ in range(count - 1):
        new = 1.0 / (2.0 * RATIO - rho)
        found.append((new * rho, 2.0 * new / HALF))
        rho = new
    return found


FINE = chebyshev_factors(KF)
COARSE = chebyshev_factors(KC)


def position():
    grp, slab = lax.axis_index("grp"), lax.axis_index("slab")
    slabs = lax.axis_size("slab")
    total = lax.axis_size("grp") * slabs
    index = grp * slabs + slab
    return index, lax.rem(slab, 2), total


def outer_mask():
    index, _, total = position()
    return jnp.where((index == 0) | (index == total - 1), 0.0, 1.0).astype(jnp.float32)


def lane_iota(shape):
    return lax.broadcasted_iota(jnp.int32, shape, len(shape) - 1)


def rows_of(chunk):
    return pl.multiple_of(chunk * CH, CH)


def at(ref, plane, row):
    return ref[plane, pl.ds(row + PAD, CH), :]


def window(ref, plane, row):
    return ref[plane, pl.ds(row, CH + 2 * PAD), :]


def shifted(win, by):
    return pltpu.roll(win, (-by) % win.shape[0], 0)[PAD : PAD + CH]


def put(ref, plane, row, value):
    ref[plane, pl.ds(row + PAD, CH), :] = value


def clear_pads(ref, planes):
    for p in planes:
        ref[p, 0:PAD, :] = jnp.zeros((PAD, N), jnp.float32)
        ref[p, PAD + N : 2 * PAD + N, :] = jnp.zeros((PAD, N), jnp.float32)


def left(v):
    return pltpu.roll(v, v.shape[-1] - 1, v.ndim - 1)


def right(v):
    return pltpu.roll(v, 1, v.ndim - 1)


class Copies:
    def __init__(self, sems):
        self.sems, self.used = sems, 0

    def start(self, source, target):
        copy = pltpu.make_async_copy(source, target, self.sems.at[self.used])
        self.used += 1
        copy.start()
        return copy


def clear_outside(refs):
    @pl.when(outer_mask() == 0.0)
    def _():
        for ref, plane in refs:
            ref[plane] = jnp.zeros(ref.shape[1:], jnp.float32)


def fill(copies, source, ref, plane):
    return copies.start(source, ref.at[plane, PAD : PAD + N, :])


def off_diagonal(row, here, below, above, fx, fy, fz_below, fz_above):
    v = window(*here, row)
    f = window(*fx, row)
    mid = v[PAD : PAD + CH]
    g = at(*fy, row)
    total = f[PAD : PAD + CH] * shifted(v, 1) + shifted(f * v, -1)
    total = total + (g * left(mid) + right(g * mid))
    return total + (at(*fz_below, row) * at(*below, row) + at(*fz_above, row) * at(*above, row))


def prepare(coef, p, row):
    win = window(coef, p, row)
    b = win[PAD : PAD + CH]
    down = shifted(win, 1)
    lane = lane_iota(b.shape)
    nxt = jnp.where(lane == N - 1, 0.0, left(b))
    prv = jnp.where(lane == 0, 0.0, right(b))
    over = at(coef, p + 1, row)
    around = (down + shifted(win, -1)) + (nxt + prv) + (at(coef, p - 1, row) + over)
    fy = jnp.where(lane == N - 1, 0.0, 0.5 * (b + nxt))
    return 3.0 * b + 0.5 * around, 0.5 * (b + down), fy, 0.5 * (b + over)


def pair_matrix(rows, cols):
    i = lax.broadcasted_iota(jnp.int32, (rows, cols), 0)
    j = lax.broadcasted_iota(jnp.int32, (rows, cols), 1)
    same = i // 2 == j if rows > cols else j // 2 == i
    return jnp.where(same, 1.0, 0.0).astype(jnp.bfloat16)


def dot(x, y):
    total = None
    for _ in range(3):
        part = x.astype(jnp.bfloat16)
        x = x - part.astype(jnp.float32)
        term = jnp.dot(part, y, preferred_element_type=jnp.float32)
        total = term if total is None else total + term
    return total


def first_kernel(g, b, bs, out, coef, sems):
    _, par, _ = position()
    inner = 1 - par
    copies = Copies(sems)
    started = [fill(copies, bs.at[par], coef, 2), fill(copies, b.at[inner], coef, 1), fill(copies, b.at[par], coef, 0)]
    clear_pads(coef, [1])
    for copy in started:
        copy.wait()

    @pl.loop(0, N // CH)
    def _(chunk):
        row = rows_of(chunk)
        diag = prepare(coef, 1, row)[0]
        out[0, pl.ds(row, CH), :] = g[par, pl.ds(row, CH), :]
        out[1, pl.ds(row, CH), :] = g[inner, pl.ds(row, CH), :] / (CENTER * diag)


FXS, FYS, IVS, FZS, XS, DGS, COARSE_AT, STATE = 0, 4, 8, 12, 17, 20, 22, 23


def make_state(g, gs, b, bs, bx, state, coef, rhs, copies, also):
    _, par, _ = position()
    inner = 1 - par
    alive = outer_mask()
    O2, O1, A, B, I1, I2 = range(6)
    source = {O2: bx.at[par], O1: bx.at[inner], A: b.at[par], B: b.at[inner], I1: bs.at[par], I2: bs.at[inner]}
    given = [g.at[par], g.at[inner], gs.at[par]]
    started = [fill(copies, ref, coef, p) for p, ref in source.items()]
    started += [copies.start(ref, rhs.at[k + 1]) for k, ref in enumerate(given)]
    clear_pads(coef, range(6))
    clear_pads(state, range(FXS, FXS + 4))
    clear_pads(state, range(XS, XS + 3))
    for copy in started:
        copy.wait()
    clear_outside([(coef, O2), (coef, O1)])

    @pl.loop(0, N // CH)
    def _(chunk):
        row = rows_of(chunk)
        put(state, FZS, row, 0.5 * (at(coef, O2, row) + at(coef, O1, row)))
        for k, p in enumerate((O1, A, B, I1)):
            diag, fx, fy, fz = prepare(coef, p, row)
            inv = 1.0 / diag
            if p == O1:
                inv = inv * alive
            else:
                put(state, XS + k - 1, row, rhs[k, pl.ds(row, CH), :] * inv * (1.0 / CENTER))
            if p in (A, B):
                put(state, DGS + k - 1, row, diag)
            put(state, FXS + k, row, fx)
            put(state, FYS + k, row, fy)
            put(state, FZS + 1 + k, row, fz)
            put(state, IVS + k, row, inv)
        also(row)


def ready_kernel(g, gs, b, bs, bx, sent, state, xa, coef, rhs, red, cpl, sems):
    del sent
    O2, O1, A, B, I1, I2 = range(6)

    def also(row):
        xa[pl.ds(row, CH), :] = at(state, XS, row)
        for k, (p, q) in enumerate(((A, B), (O1, O2), (I1, I2))):
            red[pl.ds(k * N + row, CH), :] = at(coef, p, row) + at(coef, q, row)

    make_state(g, gs, b, bs, bx, state, coef, rhs, Copies(sems), also)
    cpl[...] = dot(red[...], pair_matrix(N, NC))
    bc, bo, bi = (
        0.125 * (cpl[pl.ds(k * N, NC, 2), :] + cpl[pl.ds(k * N + 1, NC, 2), :]) for k in range(3)
    )
    row_at = lax.broadcasted_iota(jnp.int32, (NC, NC), 0)
    lane = lane_iota((NC, NC))
    around = (
        jnp.where(lane == NC - 1, 0.0, left(bc))
        + jnp.where(lane == 0, 0.0, right(bc))
        + jnp.where(row_at == NC - 1, 0.0, pltpu.roll(bc, NC - 1, 0))
        + jnp.where(row_at == 0, 0.0, pltpu.roll(bc, 1, 0))
    )
    diag = 0.25 * (3.0 * bc + 0.5 * (around + bo + bi))
    state[COARSE_AT, 0:NC, 0:NC] = bc
    state[COARSE_AT, 0:NC, NC:N] = 1.0 / (CENTER * diag)


def pre_smooth(state, rhs, x1, e2, r1, x2, done):
    O1, A, B, I1 = range(4)

    @pl.loop(0, N // CH)
    def _(chunk):
        row = rows_of(chunk)
        put(x1, 1, row, rhs[O1, pl.ds(row, CH), :] * at(state, IVS + O1, row) * (1.0 / CENTER))

    step_a, step_b = FINE[0]
    first = [(x1, 0), (x1, 1), (state, XS), (state, XS + 1), (state, XS + 2), (x1, 2)]

    def faces(k):
        return (state, FXS + k), (state, FYS + k), (state, FZS + k), (state, FZS + k + 1)

    @pl.loop(0, N // CH)
    def _(chunk):
        row = rows_of(chunk)
        for k in (O1, A, B, I1):
            res = off_diagonal(row, first[k + 1], first[k], first[k + 2], *faces(k))
            res = res + (1.0 - 1.0 / CENTER) * rhs[k, pl.ds(row, CH), :]
            here = at(*first[k + 1], row)
            move = step_a * here + step_b * (at(state, IVS + k, row) * res)
            put(e2, k, row, move)
            if k in (A, B):
                r1[k - A, pl.ds(row, CH), :] = res
                if x2 is not None:
                    x2[3 + k - A, pl.ds(row, CH), :] = here + move

    @pl.loop(0, N // CH)
    def _(chunk):
        row = rows_of(chunk)
        found = []
        for k in (A, B):
            res = r1[k - A, pl.ds(row, CH), :] - at(state, DGS + k - A, row) * at(e2, k, row)
            found.append(res + off_diagonal(row, (e2, k), (e2, k - 1), (e2, k + 1), *faces(k)))
        done(row, *found)


SPLIT = 2
HELD = 5


def pre_kernel(g, gs, bs, bx, state, sx, xi, pack, over, side, rhs, x1, e2, r1, red, cpl, packed, sems):
    _, par, _ = position()
    inner = 1 - par
    copies = Copies(sems)
    started = [copies.start(ref, rhs.at[k]) for k, ref in enumerate((sx.at[0], g.at[par], g.at[inner], gs.at[par]))]
    started += [fill(copies, sx.at[1], x1, 0), fill(copies, xi, x1, 2)]
    leaving = [copies.start(bs.at[par], over.at[2]), copies.start(bx.at[inner], side.at[2])]
    clear_pads(x1, range(3))
    clear_pads(e2, range(4))
    for copy in started:
        copy.wait()

    def done(row, ra, rb):
        red[pl.ds(row, CH), :] = ra + rb
        for ref in (over, side):
            ref[0, pl.ds(row, CH), :] = ra
            ref[1, pl.ds(row, CH), :] = rb

    pre_smooth(state, rhs, x1, e2, r1, side, done)
    cpl[0:N, :] = dot(red[...], pair_matrix(N, NC))
    rc = 0.125 * (cpl[pl.ds(0, NC, 2), :] + cpl[pl.ds(1, NC, 2), :])
    fields = (rc * state[COARSE_AT, 0:NC, NC:N], state[COARSE_AT, 0:NC, 0:NC])
    for k, field in enumerate(fields):
        base = k * (NC + 16)
        cpl[base : base + 8, :] = jnp.zeros((8, NC), jnp.float32)
        cpl[base + NC + 8 : base + NC + 16, :] = jnp.zeros((8, NC), jnp.float32)
        cpl[base + 8 : base + NC + 8, :] = field
    each = NC // 2 // SPLIT
    for part in range(SPLIT):
        for odd, first in ((0, 4), (1, 9)):
            for k in range(2):
                for j in range(HELD):
                    rows = cpl[pl.ds(k * (NC + 16) + first + j + part * each * 2, each, 2), :]
                    packed[pl.ds(part * each * 4 * HELD + (odd * 2 + k) * HELD + j, each, 4 * HELD), :] = rows
        piece = pl.ds(part * each * 4 * HELD, each * 4 * HELD)
        leaving.append(copies.start(packed.at[piece], pack.at[piece]))
    for copy in leaving:
        copy.wait()
    clear_outside([(side, 2)])


def coarse_kernel(recv, other, over, pack, cpl, packed, sems):
    del over
    index, par, _ = position()
    rows = 2 * HELD
    planes = recv.shape[0] // rows
    plane_at = lax.broadcasted_iota(jnp.int32, (planes, NC), 0)
    lane = lane_iota((planes, NC))

    def up(v):
        return pltpu.roll(v, planes - 1, 0)

    def down(v):
        return pltpu.roll(v, 1, 0)

    def row_of(field, n):
        if n >= 0:
            return recv[pl.ds(field * HELD + jnp.where(par == 0, 4 - n, n), planes, rows), :]
        return other[pl.ds(field * HELD + jnp.where(par == 0, -n - 1, 5 + n), planes, rows), :]

    u1 = {j: row_of(0, j) for j in range(-4, 5)}
    bc = {j: row_of(1, j) for j in range(-4, 5)}
    fr = {j: 0.125 * (bc[j] + bc[j + 1]) for j in range(-4, 4)}
    fz, fy, dg, iv = {}, {}, {}, {}
    for j in range(-3, 4):
        zn = jnp.where(plane_at == planes - 1, 0.0, up(bc[j]))
        zp = jnp.where(plane_at == 0, 0.0, down(bc[j]))
        yn = jnp.where(lane == NC - 1, 0.0, left(bc[j]))
        yp = jnp.where(lane == 0, 0.0, right(bc[j]))
        fz[j] = jnp.where(plane_at == planes - 1, 0.0, 0.125 * (bc[j] + zn))
        fy[j] = jnp.where(lane == NC - 1, 0.0, 0.125 * (bc[j] + yn))
        dg[j] = 0.75 * bc[j] + 0.125 * (zn + zp + yn + yp + bc[j - 1] + bc[j + 1])
        row = index + jnp.where(par == 0, -j, j)
        inside = (row >= 0) & (row < NC)
        iv[j] = jnp.where(inside, 1.0 / jnp.where(inside, dg[j], 1.0), 0.0)

    def off(v, j):
        total = fr[j] * v[j + 1] + fr[j - 1] * v[j - 1]
        total = total + fz[j] * up(v[j]) + down(fz[j] * v[j])
        return total + fy[j] * left(v[j]) + right(fy[j] * v[j])

    reach = 3
    res = {j: (CENTER - 1.0) * dg[j] * u1[j] + off(u1, j) for j in range(-reach, reach + 1)}
    step = u1
    total = u1[0]
    for k, (step_a, step_b) in enumerate(COARSE):
        step = {j: step_a * step[j] + step_b * iv[j] * res[j] for j in range(-reach, reach + 1)}
        total = total + step[0]
        reach -= 1
        res = {j: res[j] - dg[j] * step[j] + off(step, j) for j in range(-reach, reach + 1)}
    groups = lax.axis_size("grp")
    each = planes // groups
    column = jnp.sum(res[0].reshape(groups, each, NC), axis=1, keepdims=True)
    weight = jnp.sum(dg[0].reshape(groups, each, NC), axis=1, keepdims=True)
    lift = jnp.broadcast_to(column / weight, (groups, each, NC)).reshape(planes, NC)
    cpl[0:8, :] = jnp.zeros((8, NC), jnp.float32)
    cpl[planes + 8 : planes + 16, :] = jnp.zeros((8, NC), jnp.float32)
    cpl[8 : planes + 8, :] = total + lift
    for k in range(5):
        packed[pl.ds(k, planes, 5), :] = cpl[pl.ds(6 + k, planes), :]
    Copies(sems).start(packed, pack).wait()


def post_kernel(
    b, bs, bx, own, over, side, w, x5, r5,
    coef, fx, fy, fz, iv, dg, before, x2v, pw, r3, e4, r4, e5, half, wide, x5v, r5v, sems,
):
    _, par, _ = position()
    inner = 1 - par
    order = (par, inner)
    alive = outer_mask()
    copies = Copies(sems)
    source = (over.at[2], bx.at[par], bx.at[inner], b.at[par], b.at[inner], bs.at[par], bs.at[inner], side.at[2])
    started = [fill(copies, ref, coef, p) for p, ref in enumerate(source)]
    source = (over.at[1], over.at[0], own.at[0], own.at[1], side.at[1], side.at[0])
    started += [copies.start(ref, before.at[k]) for k, ref in enumerate(source)]
    started.append(copies.start(own.at[3:5], x2v))
    clear_pads(coef, range(8))
    clear_pads(fx, range(4))
    clear_pads(pw, range(8))
    clear_pads(e4, range(6))
    clear_pads(e5, range(4))
    spread = dot(w[...], pair_matrix(NC, N))
    for side in (0, 1):
        wide[side] = spread[:, side * NC : (side + 1) * NC]
    for k, planes in enumerate(((0,), (1, 2), (3, 4), (5, 6), (7,))):
        z = jnp.where(par == 0, k, 4 - k)
        for side in (0, 1):
            part = wide[side, pl.ds(z, NC, 5), :]
            half[pl.ds(0, NC, 2), :] = part
            half[pl.ds(1, NC, 2), :] = part
            for p in planes:
                pw[p, PAD : PAD + N, side * NC : (side + 1) * NC] = half[...]
    for copy in started:
        copy.wait()
    clear_outside([(coef, 0), (coef, 1), (coef, 2)])

    @pl.loop(0, N // CH)
    def _(chunk):
        row = rows_of(chunk)
        for k in range(6):
            p = k + 1
            win = window(coef, p, row)
            ahead = pltpu.roll(win, win.shape[0] - 1, 0)
            mid = win[PAD : PAD + CH]
            lane = lane_iota(mid.shape)
            nxt = jnp.where(lane == N - 1, 0.0, left(mid))
            prv = jnp.where(lane == 0, 0.0, right(mid))
            under, over = at(coef, p - 1, row), at(coef, p + 1, row)
            around = (ahead[PAD : PAD + CH] + shifted(win, -1)) + (nxt + prv) + (under + over)
            diag = 3.0 * mid + 0.5 * around
            if k < 2:
                inv = alive / jnp.where(diag > 0.0, diag, 1.0)
            else:
                inv = 1.0 / diag
            fxw = 0.5 * (win + ahead)
            fyc = jnp.where(lane == N - 1, 0.0, 0.5 * (mid + nxt))
            below, above = 0.5 * (mid + under), 0.5 * (mid + over)
            if 1 <= k <= 4:
                put(fx, k - 1, row, fxw[PAD : PAD + CH])
                fy[k - 1, pl.ds(row, CH), :] = fyc
                fz[k - 1, pl.ds(row, CH), :] = below
                iv[k - 1, pl.ds(row, CH), :] = inv
                if k == 4:
                    fz[4, pl.ds(row, CH), :] = above
            if k in (2, 3):
                dg[k - 2, pl.ds(row, CH), :] = diag
            v = window(pw, p, row)
            here = v[PAD : PAD + CH]
            total = fxw[PAD : PAD + CH] * shifted(v, 1) + shifted(fxw * v, -1)
            total = total + (fyc * left(here) + right(fyc * here))
            total = total + (below * at(pw, p - 1, row) + above * at(pw, p + 1, row))
            res = (before[k, pl.ds(row, CH), :] - diag * here) + total
            if 1 <= k <= 4:
                r3[k - 1, pl.ds(row, CH), :] = res
            put(e4, k, row, (1.0 / CENTER) * (inv * res))

    step_a, step_b = FINE[0]

    def off(v, k, shift, row):
        win, f = window(v, k + shift, row), window(fx, k, row)
        here = win[PAD : PAD + CH]
        g = fy[k, pl.ds(row, CH), :]
        total = f[PAD : PAD + CH] * shifted(win, 1) + shifted(f * win, -1)
        total = total + (g * left(here) + right(g * here))
        total = total + fz[k, pl.ds(row, CH), :] * at(v, k + shift - 1, row)
        return total + fz[k + 1, pl.ds(row, CH), :] * at(v, k + shift + 1, row)

    @pl.loop(0, N // CH)
    def _(chunk):
        row = rows_of(chunk)
        for k in range(4):
            res = off(e4, k, 1, row) + (1.0 - 1.0 / CENTER) * r3[k, pl.ds(row, CH), :]
            here = at(e4, k + 1, row)
            move = step_a * here + step_b * (iv[k, pl.ds(row, CH), :] * res)
            put(e5, k, row, move)
            if k in (1, 2):
                r4[k - 1, pl.ds(row, CH), :] = res
                x5v[k - 1, pl.ds(row, CH), :] = (x2v[k - 1, pl.ds(row, CH), :] + at(pw, k + 2, row)) + (here + move)

    leaving = [copies.start(x5v.at[k], x5.at[order[k]]) for k in range(2)]

    @pl.loop(0, N // CH)
    def _(chunk):
        row = rows_of(chunk)
        for k in (1, 2):
            res = r4[k - 1, pl.ds(row, CH), :] - dg[k - 1, pl.ds(row, CH), :] * at(e5, k, row)
            r5v[k - 1, pl.ds(row, CH), :] = res + off(e5, k, 0, row)

    leaving += [copies.start(r5v.at[k], r5.at[order[k]]) for k in range(2)]
    for copy in leaving:
        copy.wait()


def call(kernel, outs, scratch, sems, cost, *operands, limit=24):
    return pl.pallas_call(
        kernel,
        out_shape=[jax.ShapeDtypeStruct(s, jnp.float32) for s, _ in outs],
        in_specs=[spec for _, spec in operands],
        out_specs=[spec for _, spec in outs],
        scratch_shapes=[pltpu.VMEM(s, jnp.float32) for s in scratch] + [pltpu.SemaphoreType.DMA((sems,))],
        compiler_params=pltpu.CompilerParams(vmem_limit_bytes=limit * 1024 * 1024),
        cost_estimate=pl.CostEstimate(flops=cost, bytes_accessed=cost, transcendentals=0),
    )(*(array for array, _ in operands))


def local(right_side, conductivity):
    total = lax.axis_size("grp") * lax.axis_size("slab")
    inside = [(i, i ^ 1) for i in range(total)]
    across = [(i, (i + 1) % total) for i in range(1, total, 2)] + [((i + 1) % total, i) for i in range(1, total, 2)]

    def swap(v):
        return lax.ppermute(v, AXES, inside)

    def cross(v):
        return lax.ppermute(v, AXES, across)

    def everywhere(v):
        rows = v.shape[0]
        return lax.all_to_all(v.reshape(rows, 1, NC), AXES, 0, 0, tiled=True).reshape(rows, NC)

    plane, padded = (N, N), (N + 2 * PAD, N)
    two = (2,) + plane
    g, b = right_side, conductivity
    bs = swap(b)
    bx = cross(b)
    gs = swap(g)
    (send,) = call(first_kernel, [(two, VM)], [(3,) + padded], 3, 1 << 20, (g, VM), (b, ANY), (bs, ANY))
    sx = cross(send)
    state, xa = call(
        ready_kernel,
        [((STATE,) + padded, VM), (plane, VM)],
        [(6,) + padded, (4,) + plane, (3 * N, N), (3 * N, NC)],
        9,
        6 << 20,
        (g, ANY), (gs, ANY), (b, ANY), (bs, ANY), (bx, ANY), (send, ANY),
    )
    xi = swap(xa)
    pack, over, side = call(
        pre_kernel,
        [((2 * HELD * total, NC), HBM), ((3,) + plane, VM), ((5,) + plane, VM)],
        [(4,) + plane, (3,) + padded, (4,) + padded, two, plane, (2 * (NC + 16), NC), (2 * HELD * total, NC)],
        8 + SPLIT,
        6 << 20,
        (g, ANY), (gs, ANY), (bs, ANY), (bx, ANY), (state, VM), (sx, ANY), (xi, ANY),
    )
    from_over = cross(over)
    from_side = swap(side)
    own = swap(from_side)
    got = everywhere(pack)
    (back,) = call(
        coarse_kernel,
        [((5 * NC, NC), HBM)],
        [(total + 16, NC), (5 * NC, NC)],
        1,
        4 << 20,
        (got, VM), (swap(got), VM), (from_over, ANY),
    )
    w = everywhere(back)
    x5, r5 = call(
        post_kernel,
        [(two, HBM), (two, HBM)],
        [(8,) + padded, (4,) + padded, (4,) + plane, (5,) + plane, (4,) + plane, two, (6,) + plane, two, (8,) + padded, (4,) + plane, (6,) + padded, two, (4,) + padded, (N, NC), (2, 5 * NC, NC), two, two],
        20,
        8 << 20,
        (b, ANY), (bs, ANY), (bx, ANY), (own, ANY), (from_over, ANY), (from_side, ANY), (w, VM),
    )
    return x5, r5


def solution(mesh):
    spec = P(AXES, None, None)
    return jax.shard_map(
        local, mesh=mesh, in_specs=(spec, spec), out_specs=(spec, spec), check_vma=False
    )
```

time: 361 us -> 84.9 us (0.24)
  the two profiles are of different devices: /device:TPU:24 before, /device:TPU:1 now
where the time goes in v1:
time: 84.9 us; the launch traced here: 84.6 us
  starting transfers between devices  26.7 us (31%)
  blocking collectives  19.6 us (23%)
  waiting for transfers between devices  19.5 us (23%)
  Pallas kernels  16 us (19%)
  local copies, waits for them, and re-layouts  2.09 us (2%)
    all_to_all x1, blocking collectives, everywhere(): lax.all_to_all(v.reshape(rows, 1, NC), AXES, 0, 0, tiled=True)  19.6 us
    ppermute x6, starting transfers between devices, swap(): return lax.ppermute(v, AXES, inside)  17.7 us
    pallas_call x5, Pallas kernels, call(): pl.pallas_call(kernel, out_shape=[jax.ShapeDtypeStruct(s, jnp.float32) fo...  16 us
    all_to_all x1, waiting for transfers between devices, everywhere(): lax.all_to_all(v.reshape(rows, 1, NC), AXES, 0, 0, tiled=True)  13.1 us
    ppermute x3, waiting for transfers between devices, cross(): return lax.ppermute(v, AXES, across)  5.21 us
    ppermute x3, starting transfers between devices, cross(): return lax.ppermute(v, AXES, across)  4.54 us
    all_to_all x1, starting transfers between devices, everywhere(): lax.all_to_all(v.reshape(rows, 1, NC), AXES, 0, 0, tiled=True)  4.45 us
    unnamed x6, local copies, waits for them, and re-layouts  2.09 us
  transfers between devices with their start and end apart: 10, of which 4 were waited for; matrix products, arithmetic and copies ran while one was open for 0% of the time, Pallas kernels for 5%

profile of v1, /device:TPU:1, one launch (start us, length us, event | category | flops | bytes accessed | tf_op | source)
XLA Modules:
  0.0 84.6 jit_solution(2047302610712159853)
XLA Ops:
  0.6 1.5 %collective-permute-start = (f32[2,256,256]{2,1,0:T(8,128)}, f32[2,256,256]{2,1,0:T(8,128)S(1)}, u32[]{:S(2)}, u32[]{:S(2)}) collective-permute-start(f32[2,256,256]{2,1,0:T(8,128)} %b.5), channel_id=1, source_target_pairs={{0,1},{1,0},{2,3},{3,2},{4,5},{5,4},{6,7},{7,6},{8,9},{9,8},{10,11... | collective-permute-start | bytes 1572872 | tf_op jit(solution)/shard_map/ppermute | solution.py:513
  2.1 0.1 collective-permute-start.2
  2.2 2.0 %collective-permute-start.1 = (f32[2,256,256]{2,1,0:T(8,128)}, f32[2,256,256]{2,1,0:T(8,128)S(1)}, u32[]{:S(2)}, u32[]{:S(2)}) collective-permute-start(f32[2,256,256]{2,1,0:T(8,128)} %b.5), channel_id=1, source_target_pairs={{1,2},{3,4},{5,6},{7,8},{9,10},{11,12},{13,14},{15,16},{17,18},{19... | collective-permute-start | bytes 1572872 | tf_op jit(solution)/shard_map/ppermute | solution.py:516
  4.2 0.0 collective-permute-done.bs
  4.2 0.0 copy-start
  4.3 1.0 %copy-done = f32[2,256,256]{2,1,0:T(8,128)S(1)} copy-done((f32[2,256,256]{2,1,0:T(8,128)S(1)}, f32[2,256,256]{2,1,0:T(8,128)}, u32[]{:S(2)}) %copy-start) | copy-done | bytes 524312
  5.3 0.0 copy-start.1
  5.3 1.0 %copy-done.1 = f32[2,256,256]{2,1,0:T(8,128)S(1)} copy-done((f32[2,256,256]{2,1,0:T(8,128)S(1)}, f32[2,256,256]{2,1,0:T(8,128)}, u32[]{:S(2)}) %copy-start.1) | copy-done | bytes 524312
  6.3 0.5 shard_map.41.sent
  6.8 1.7 %collective-permute-start.3 = (f32[2,256,256]{2,1,0:T(8,128)S(1)}, f32[2,256,256]{2,1,0:T(8,128)S(1)}, u32[]{:S(2)}, u32[]{:S(2)}) collective-permute-start(f32[2,256,256]{2,1,0:T(8,128)S(1)} %shard_map.41.sent), channel_id=1, source_target_pairs={{1,2},{3,4},{5,6},{7,8},{9,10},{11,12},{13,14},{15,16},{17,18},{19... | collective-permute-start | bytes 1572872 | tf_op jit(solution)/shard_map/ppermute | solution.py:516
  8.5 0.0 collective-permute-done.2.gs
  8.5 2.8 %collective-permute-done.1.bx = f32[2,256,256]{2,1,0:T(8,128)S(1)} collective-permute-done((f32[2,256,256]{2,1,0:T(8,128)}, f32[2,256,256]{2,1,0:T(8,128)S(1)}, u32[]{:S(2)}, u32[]{:S(2)}) %collective-permute-start.1) | collective-permute-done | bytes 524320 | tf_op jit(solution)/shard_map/ppermute | solution.py:516
  11.3 2.0 %shard_map.42 = (f32[23,272,256]{2,1,0:T(8,128)S(1)}, f32[256,256]{1,0:T(8,128)S(1)}) custom-call(f32[2,256,256]{2,1,0:T(8,128)S(1)} %copy-done, f32[2,256,256]{2,1,0:T(8,128)S(1)} %collective-permute-done.2.gs, f32[2,256,256]{2,1,0:T(8,128)S(1)} %copy-done.1, f32[2,256,256]{2,1,0:T(8,128)S(1)} %collective-permute-done.bs, ...), custom_call_target="tpu_custom_call" | custom-call | flops 6291456 | bytes 6291456 | tf_op jit(solution)/shard_map/pallas_call | solution.py:496
  13.3 7.0 %collective-permute-start.4 = (f32[256,256]{1,0:T(8,128)S(1)}, f32[256,256]{1,0:T(8,128)S(1)}, u32[]{:S(2)}, u32[]{:S(2)}) collective-permute-start(f32[256,256]{1,0:T(8,128)S(1)} %get-tuple-element.8), channel_id=1, source_target_pairs={{0,1},{1,0},{2,3},{3,2},{4,5},{5,4},{6,7},{7,6},{8,9},{9,8},{10,11... | collective-permute-start | bytes 786440 | tf_op jit(solution)/shard_map/ppermute | solution.py:513
  20.2 1.2 %collective-permute-done.4.xi = f32[256,256]{1,0:T(8,128)S(1)} collective-permute-done((f32[256,256]{1,0:T(8,128)S(1)}, f32[256,256]{1,0:T(8,128)S(1)}, u32[]{:S(2)}, u32[]{:S(2)}) %collective-permute-start.4) | collective-permute-done | bytes 262176 | tf_op jit(solution)/shard_map/ppermute | solution.py:513
  21.4 0.0 collective-permute-done.3.sx
  21.4 4.5 %shard_map.43 = (f32[1280,128]{1,0:T(8,128)}, f32[3,256,256]{2,1,0:T(8,128)S(1)}, f32[5,256,256]{2,1,0:T(8,128)}) custom-call(f32[2,256,256]{2,1,0:T(8,128)S(1)} %copy-done, f32[2,256,256]{2,1,0:T(8,128)S(1)} %collective-permute-done.2.gs, f32[2,256,256]{2,1,0:T(8,128)S(1)} %collective-permute-done.bs, f32[2,256,256]{2,1,0:T(8,128)S(1)} %collective-permute-done.1.bx, ...), custom_call_target="tpu_custom_call" | custom-call | flops 6291456 | bytes 6291456 | tf_op jit(solution)/shard_map/pallas_call | solution.py:496
  25.9 6.5 %collective-permute-start.5 = (f32[5,256,256]{2,1,0:T(8,128)}, f32[5,256,256]{2,1,0:T(8,128)}, u32[]{:S(2)}, u32[]{:S(2)}) collective-permute-start(f32[5,256,256]{2,1,0:T(8,128)} %get-tuple-element.9), channel_id=1, source_target_pairs={{0,1},{1,0},{2,3},{3,2},{4,5},{5,4},{6,7},{7,6},{8,9},{9,8},{10,11... | collective-permute-start | bytes 3932168 | tf_op jit(solution)/shard_map/ppermute | solution.py:513
  32.4 4.4 %all-to-all-start = ((f32[1280,1,128]{2,1,0:T(1,128)}), f32[1280,1,128]{2,1,0:T(1,128)S(1)}, u32[]{:S(2)}, u32[]{:S(2)}) async-start(f32[1280,1,128]{2,1,0:T(1,128)} %bitcast.1), calls=%async_computation | async-start | bytes 1310720 | tf_op jit(solution)/shard_map/all_to_all | solution.py:520
  36.8 0.0 collective-permute-done.5.side
  36.8 1.1 %collective-permute-start.6 = (f32[5,256,256]{2,1,0:T(8,128)}, f32[5,256,256]{2,1,0:T(8,128)}, u32[]{:S(2)}, u32[]{:S(2)}) collective-permute-start(f32[5,256,256]{2,1,0:T(8,128)} %collective-permute-done.5.side), channel_id=1, source_target_pairs={{0,1},{1,0},{2,3},{3,2},{4,5},{5,4},{6,7},{7,6},{8,9},{9,8},{10,11... | collective-permute-start | bytes 3932168 | tf_op jit(solution)/shard_map/ppermute | solution.py:513
  38.0 0.8 collective-permute-start.7
  38.8 13.1 %all-to-all-done = f32[1280,1,128]{2,1,0:T(1,128)S(1)} async-done(((f32[1280,1,128]{2,1,0:T(1,128)}), f32[1280,1,128]{2,1,0:T(1,128)S(1)}, u32[]{:S(2)}, u32[]{:S(2)}) %all-to-all-start) | async-done | bytes 655392 | tf_op jit(solution)/shard_map/all_to_all | solution.py:520
  51.9 0.0 copy-start.2
  51.9 1.5 %collective-permute-start.8 = (f32[1280,128]{1,0:T(8,128)S(1)}, f32[1280,128]{1,0:T(8,128)S(1)}, u32[]{:S(2)}, u32[]{:S(2)}) collective-permute-start(f32[1280,128]{1,0:T(8,128)S(1)} %bitcast.8), channel_id=1, source_target_pairs={{0,1},{1,0},{2,3},{3,2},{4,5},{5,4},{6,7},{7,6},{8,9},{9,8},{10,11... | collective-permute-start | bytes 1966088 | tf_op jit(solution)/shard_map/ppermute | solution.py:513
  53.5 2.4 %collective-permute-done.7.over = f32[3,256,256]{2,1,0:T(8,128)S(1)} collective-permute-done((f32[3,256,256]{2,1,0:T(8,128)S(1)}, f32[3,256,256]{2,1,0:T(8,128)S(1)}, u32[]{:S(2)}, u32[]{:S(2)}) %collective-permute-start.7) | collective-permute-done | bytes 786464 | tf_op jit(solution)/shard_map/ppermute | solution.py:516
  55.9 0.0 collective-permute-done.8.other
  55.9 1.5 %shard_map.44 = f32[640,128]{1,0:T(8,128)S(1)} custom-call(f32[1280,128]{1,0:T(8,128)S(1)} %bitcast.9, f32[1280,128]{1,0:T(8,128)S(1)} %collective-permute-done.8.other, f32[3,256,256]{2,1,0:T(8,128)S(1)} %collective-permute-done.7.over), custom_call_target="tpu_custom_call" | custom-call | flops 4194304 | bytes 4194304 | tf_op jit(solution)/shard_map/pallas_call | solution.py:496
  57.4 19.6 %all_to_all.10 = f32[640,1,128]{2,1,0:T(1,128)S(1)} all-to-all(f32[640,1,128]{2,1,0:T(1,128)S(1)} %bitcast.10), channel_id=1, replica_groups=mesh['grp'=4,'slab'=32] {'grp','slab'}, dimensions={0} | all-to-all | bytes 655360 | tf_op jit(solution)/shard_map/all_to_all | solution.py:520
  77.0 0.0 collective-permute-done.6.own
  77.0 0.0 copy-done.2
  77.0 7.6 %shard_map.45 = (f32[2,256,256]{2,1,0:T(8,128)}, f32[2,256,256]{2,1,0:T(8,128)}) custom-call(f32[2,256,256]{2,1,0:T(8,128)S(1)} %copy-done.2, f32[2,256,256]{2,1,0:T(8,128)S(1)} %collective-permute-done.bs, f32[2,256,256]{2,1,0:T(8,128)S(1)} %collective-permute-done.1.bx, f32[5,256,256]{2,1,0:T(8,128)} %collective-permute-done.6.own, ...), custom_call_target="tpu_custom_call" | custom-call | flops 8388608 | bytes 8388608 | tf_op jit(solution)/shard_map/pallas_call | solution.py:496
Async XLA Ops:
  0.6 3.6 %collective-permute-start = (f32[2,256,256]{2,1,0:T(8,128)}, f32[2,256,256]{2,1,0:T(8,128)S(1)}, u32[]{:S(2)}, u32[]{:S(2)}) collective-permute-start(f32[2,256,256]{2,1,0:T(8,128)} %b.5), channel_id=1, source_target_pairs={{0,1},{1,0},{2,3},{3,2},{4,5},{5,4},{6,7},{7,6},{8,9},{9,8},{10,11... | collective-permute-start | bytes 1572872 | tf_op jit(solution)/shard_map/ppermute | solution.py:513
  2.1 6.4 %collective-permute-start.2 = (f32[2,256,256]{2,1,0:T(8,128)}, f32[2,256,256]{2,1,0:T(8,128)S(1)}, u32[]{:S(2)}, u32[]{:S(2)}) collective-permute-start(f32[2,256,256]{2,1,0:T(8,128)} %g.5), channel_id=1, source_target_pairs={{0,1},{1,0},{2,3},{3,2},{4,5},{5,4},{6,7},{7,6},{8,9},{9,8},{10,11... | collective-permute-start | bytes 1572872 | tf_op jit(solution)/shard_map/ppermute | solution.py:513
  2.2 9.1 %collective-permute-start.1 = (f32[2,256,256]{2,1,0:T(8,128)}, f32[2,256,256]{2,1,0:T(8,128)S(1)}, u32[]{:S(2)}, u32[]{:S(2)}) collective-permute-start(f32[2,256,256]{2,1,0:T(8,128)} %b.5), channel_id=1, source_target_pairs={{1,2},{3,4},{5,6},{7,8},{9,10},{11,12},{13,14},{15,16},{17,18},{19... | collective-permute-start | bytes 1572872 | tf_op jit(solution)/shard_map/ppermute | solution.py:516
  4.2 1.0 %copy-start = (f32[2,256,256]{2,1,0:T(8,128)S(1)}, f32[2,256,256]{2,1,0:T(8,128)}, u32[]{:S(2)}) copy-start(f32[2,256,256]{2,1,0:T(8,128)} %g.5) | copy-start | bytes 1572868
  5.3 1.0 %copy-start.1 = (f32[2,256,256]{2,1,0:T(8,128)S(1)}, f32[2,256,256]{2,1,0:T(8,128)}, u32[]{:S(2)}) copy-start(f32[2,256,256]{2,1,0:T(8,128)} %b.5) | copy-start | bytes 1572868
  6.8 14.6 %collective-permute-start.3 = (f32[2,256,256]{2,1,0:T(8,128)S(1)}, f32[2,256,256]{2,1,0:T(8,128)S(1)}, u32[]{:S(2)}, u32[]{:S(2)}) collective-permute-start(f32[2,256,256]{2,1,0:T(8,128)S(1)} %shard_map.41.sent), channel_id=1, source_target_pairs={{1,2},{3,4},{5,6},{7,8},{9,10},{11,12},{13,14},{15,16},{17,18},{19... | collective-permute-start | bytes 1572872 | tf_op jit(solution)/shard_map/ppermute | solution.py:516
  13.3 8.1 %collective-permute-start.4 = (f32[256,256]{1,0:T(8,128)S(1)}, f32[256,256]{1,0:T(8,128)S(1)}, u32[]{:S(2)}, u32[]{:S(2)}) collective-permute-start(f32[256,256]{1,0:T(8,128)S(1)} %get-tuple-element.8), channel_id=1, source_target_pairs={{0,1},{1,0},{2,3},{3,2},{4,5},{5,4},{6,7},{7,6},{8,9},{9,8},{10,11... | collective-permute-start | bytes 786440 | tf_op jit(solution)/shard_map/ppermute | solution.py:513
  25.9 10.9 %collective-permute-start.5 = (f32[5,256,256]{2,1,0:T(8,128)}, f32[5,256,256]{2,1,0:T(8,128)}, u32[]{:S(2)}, u32[]{:S(2)}) collective-permute-start(f32[5,256,256]{2,1,0:T(8,128)} %get-tuple-element.9), channel_id=1, source_target_pairs={{0,1},{1,0},{2,3},{3,2},{4,5},{5,4},{6,7},{7,6},{8,9},{9,8},{10,11... | collective-permute-start | bytes 3932168 | tf_op jit(solution)/shard_map/ppermute | solution.py:513
  32.4 19.6 %all-to-all-start = ((f32[1280,1,128]{2,1,0:T(1,128)}), f32[1280,1,128]{2,1,0:T(1,128)S(1)}, u32[]{:S(2)}, u32[]{:S(2)}) async-start(f32[1280,1,128]{2,1,0:T(1,128)} %bitcast.1), calls=%async_computation | async-start | bytes 1310720 | tf_op jit(solution)/shard_map/all_to_all | solution.py:520
  36.8 40.2 %collective-permute-start.6 = (f32[5,256,256]{2,1,0:T(8,128)}, f32[5,256,256]{2,1,0:T(8,128)}, u32[]{:S(2)}, u32[]{:S(2)}) collective-permute-start(f32[5,256,256]{2,1,0:T(8,128)} %collective-permute-done.5.side), channel_id=1, source_target_pairs={{0,1},{1,0},{2,3},{3,2},{4,5},{5,4},{6,7},{7,6},{8,9},{9,8},{10,11... | collective-permute-start | bytes 3932168 | tf_op jit(solution)/shard_map/ppermute | solution.py:513
  38.0 17.9 %collective-permute-start.7 = (f32[3,256,256]{2,1,0:T(8,128)S(1)}, f32[3,256,256]{2,1,0:T(8,128)S(1)}, u32[]{:S(2)}, u32[]{:S(2)}) collective-permute-start(f32[3,256,256]{2,1,0:T(8,128)S(1)} %get-tuple-element.10), channel_id=1, source_target_pairs={{1,2},{3,4},{5,6},{7,8},{9,10},{11,12},{13,14},{15,16},{17,18},{19... | collective-permute-start | bytes 2359304 | tf_op jit(solution)/shard_map/ppermute | solution.py:516
  51.9 25.1 %copy-start.2 = (f32[2,256,256]{2,1,0:T(8,128)S(1)}, f32[2,256,256]{2,1,0:T(8,128)}, u32[]{:S(2)}) copy-start(f32[2,256,256]{2,1,0:T(8,128)} %b.5) | copy-start | bytes 1572868
  51.9 3.9 %collective-permute-start.8 = (f32[1280,128]{1,0:T(8,128)S(1)}, f32[1280,128]{1,0:T(8,128)S(1)}, u32[]{:S(2)}, u32[]{:S(2)}) collective-permute-start(f32[1280,128]{1,0:T(8,128)S(1)} %bitcast.8), channel_id=1, source_target_pairs={{0,1},{1,0},{2,3},{3,2},{4,5},{5,4},{6,7},{7,6},{8,9},{9,8},{10,11... | collective-permute-start | bytes 1966088 | tf_op jit(solution)/shard_map/ppermute | solution.py:513

commit v2 on v1

--- a/solution.py
+++ b/solution.py
@@ -20,7 +20,7 @@
 N = 256
 NC = 128
 PAD = 8
-CH = 128
+CH = 256
 VM = pl.BlockSpec(memory_space=pltpu.VMEM)
 ANY = pl.BlockSpec(memory_space=pl.ANY)
 HBM = pl.BlockSpec(memory_space=pltpu.HBM)
@@ -61,6 +61,11 @@
     return pl.multiple_of(chunk * CH, CH)
 
 
+def whole_planes(body):
+    assert CH == N
+    body(0)
+
+
 def at(ref, plane, row):
     return ref[plane, pl.ds(row + PAD, CH), :]
 
@@ -101,6 +106,14 @@
         copy.start()
         return copy
 
+    def again(self, source, target):
+        pltpu.make_async_copy(source, target, self.sems.at[self.used]).start()
+
+    def handle(self, source, target):
+        copy = pltpu.make_async_copy(source, target, self.sems.at[self.used])
+        self.used += 1
+        return copy
+
 
 def clear_outside(refs):
     @pl.when(outer_mask() == 0.0)
@@ -113,14 +126,17 @@
     return copies.start(source, ref.at[plane, PAD : PAD + N, :])
 
 
-def off_diagonal(row, here, below, above, fx, fy, fz_below, fz_above):
+def lateral(row, here, fx, fy):
     v = window(*here, row)
     f = window(*fx, row)
     mid = v[PAD : PAD + CH]
     g = at(*fy, row)
     total = f[PAD : PAD + CH] * shifted(v, 1) + shifted(f * v, -1)
-    total = total + (g * left(mid) + right(g * mid))
-    return total + (at(*fz_below, row) * at(*below, row) + at(*fz_above, row) * at(*above, row))
+    return total + (g * left(mid) + right(g * mid))
+
+
+def inverse(v):
+    return 1.0 / v
 
 
 def prepare(coef, p, row):
@@ -170,55 +186,81 @@
         out[1, pl.ds(row, CH), :] = g[inner, pl.ds(row, CH), :] / (CENTER * diag)
 
 
-FXS, FYS, IVS, FZS, XS, DGS, COARSE_AT, STATE = 0, 4, 8, 12, 17, 20, 22, 23
-
-
-def make_state(g, gs, b, bs, bx, state, coef, rhs, copies, also):
+(FXO, FXA, FYO, FYA, IVO, IVA, IVI, Z0, Z1, Z2, Z3, Z4, XA, XI, PA, PI, DA, EB, PB, X2B, COARSE_AT, STATE) = range(22)
+
+
+def ready_kernel(g, gs, b, bs, bx, sent, state, xa, coef, rhs, mine, red, cpl, sems):
+    del sent
     _, par, _ = position()
     inner = 1 - par
     alive = outer_mask()
     O2, O1, A, B, I1, I2 = range(6)
+    FXB, FXI, FYB, FYI, IVB, DB, XB, RB = range(8)
+    copies = Copies(sems)
     source = {O2: bx.at[par], O1: bx.at[inner], A: b.at[par], B: b.at[inner], I1: bs.at[par], I2: bs.at[inner]}
     given = [g.at[par], g.at[inner], gs.at[par]]
     started = [fill(copies, ref, coef, p) for p, ref in source.items()]
-    started += [copies.start(ref, rhs.at[k + 1]) for k, ref in enumerate(given)]
+    started += [copies.start(ref, rhs.at[k]) for k, ref in enumerate(given)]
     clear_pads(coef, range(6))
-    clear_pads(state, range(FXS, FXS + 4))
-    clear_pads(state, range(XS, XS + 3))
+    clear_pads(state, (FXO, FXA, XA, XI, EB))
+    clear_pads(mine, (FXB, FXI, XB))
     for copy in started:
         copy.wait()
     clear_outside([(coef, O2), (coef, O1)])
+    keep = {
+        O1: ((state, FXO), (state, FYO), (state, IVO), (state, Z1), None, None),
+        A: ((state, FXA), (state, FYA), (state, IVA), (state, Z2), (state, DA), (state, XA)),
+        B: ((mine, FXB), (mine, FYB), (mine, IVB), (state, Z3), (mine, DB), (mine, XB)),
+        I1: ((mine, FXI), (mine, FYI), (state, IVI), (state, Z4), None, (state, XI)),
+    }
 
     @pl.loop(0, N // CH)
     def _(chunk):
         row = rows_of(chunk)
-        put(state, FZS, row, 0.5 * (at(coef, O2, row) + at(coef, O1, row)))
+        put(state, Z0, row, 0.5 * (at(coef, O2, row) + at(coef, O1, row)))
         for k, p in enumerate((O1, A, B, I1)):
             diag, fx, fy, fz = prepare(coef, p, row)
+            to_fx, to_fy, to_iv, to_fz, to_dg, to_x = keep[p]
             inv = 1.0 / diag
             if p == O1:
                 inv = inv * alive
-            else:
-                put(state, XS + k - 1, row, rhs[k, pl.ds(row, CH), :] * inv * (1.0 / CENTER))
-            if p in (A, B):
-                put(state, DGS + k - 1, row, diag)
-            put(state, FXS + k, row, fx)
-            put(state, FYS + k, row, fy)
-            put(state, FZS + 1 + k, row, fz)
-            put(state, IVS + k, row, inv)
-        also(row)
-
-
-def ready_kernel(g, gs, b, bs, bx, sent, state, xa, coef, rhs, red, cpl, sems):
-    del sent
-    O2, O1, A, B, I1, I2 = range(6)
-
-    def also(row):
-        xa[pl.ds(row, CH), :] = at(state, XS, row)
+            put(*to_fx, row, fx)
+            put(*to_fy, row, fy)
+            put(*to_iv, row, inv)
+            put(*to_fz, row, fz)
+            if to_dg:
+                put(*to_dg, row, diag)
+            if to_x:
+                x1 = rhs[k - 1, pl.ds(row, CH), :] * inv * (1.0 / CENTER)
+                put(*to_x, row, x1)
+                if p == A:
+                    xa[pl.ds(row, CH), :] = x1
         for k, (p, q) in enumerate(((A, B), (O1, O2), (I1, I2))):
             red[pl.ds(k * N + row, CH), :] = at(coef, p, row) + at(coef, q, row)
 
-    make_state(g, gs, b, bs, bx, state, coef, rhs, Copies(sems), also)
+    step_a, step_b = FINE[0]
+    left_over = 1.0 - 1.0 / CENTER
+
+    @pl.loop(0, N // CH)
+    def _(chunk):
+        row = rows_of(chunk)
+        here = at(mine, XB, row)
+        part = lateral(row, (state, XA), (state, FXA), (state, FYA)) + at(state, Z2, row) * here
+        put(state, PA, row, part + left_over * rhs[0, pl.ds(row, CH), :])
+        part = lateral(row, (state, XI), (mine, FXI), (mine, FYI)) + at(state, Z3, row) * here
+        put(state, PI, row, part + left_over * rhs[2, pl.ds(row, CH), :])
+        res = lateral(row, (mine, XB), (mine, FXB), (mine, FYB)) + left_over * rhs[1, pl.ds(row, CH), :]
+        res = res + (at(state, Z2, row) * at(state, XA, row) + at(state, Z3, row) * at(state, XI, row))
+        move = step_a * here + step_b * (at(mine, IVB, row) * res)
+        put(state, EB, row, move)
+        put(state, X2B, row, here + move)
+        put(mine, RB, row, res - at(mine, DB, row) * move)
+
+    @pl.loop(0, N // CH)
+    def _(chunk):
+        row = rows_of(chunk)
+        put(state, PB, row, at(mine, RB, row) + lateral(row, (state, EB), (mine, FXB), (mine, FYB)))
+
     cpl[...] = dot(red[...], pair_matrix(N, NC))
     bc, bo, bi = (
         0.125 * (cpl[pl.ds(k * N, NC, 2), :] + cpl[pl.ds(k * N + 1, NC, 2), :]) for k in range(3)
@@ -236,67 +278,65 @@
     state[COARSE_AT, 0:NC, NC:N] = 1.0 / (CENTER * diag)
 
 
-def pre_smooth(state, rhs, x1, e2, r1, x2, done):
-    O1, A, B, I1 = range(4)
+SPLIT = 2
+HELD = 5
+
+
+def pre_kernel(bs, bx, state, sx, xi, pack, side, x1, e2, part, red, cpl, packed, own, zeros, sems):
+    _, par, _ = position()
+    inner = 1 - par
+    copies = Copies(sems)
+    leaving = [copies.start(bs.at[par], side.at[2])]
+    beyond = outer_mask() == 0.0
+
+    @pl.when(beyond)
+    def _():
+        zeros[...] = jnp.zeros((N, N), jnp.float32)
+        copies.again(zeros, side.at[3])
+
+    @pl.when(jnp.logical_not(beyond))
+    def _():
+        copies.again(bx.at[inner], side.at[3])
+
+    leaving.append(copies.handle(bx.at[inner], side.at[3]))
+    clear_pads(x1, [0])
+    clear_pads(e2, [0])
 
     @pl.loop(0, N // CH)
     def _(chunk):
         row = rows_of(chunk)
-        put(x1, 1, row, rhs[O1, pl.ds(row, CH), :] * at(state, IVS + O1, row) * (1.0 / CENTER))
+        put(x1, 0, row, sx[0, pl.ds(row, CH), :] * at(state, IVO, row) * (1.0 / CENTER))
 
     step_a, step_b = FINE[0]
-    first = [(x1, 0), (x1, 1), (state, XS), (state, XS + 1), (state, XS + 2), (x1, 2)]
-
-    def faces(k):
-        return (state, FXS + k), (state, FYS + k), (state, FZS + k), (state, FZS + k + 1)
 
     @pl.loop(0, N // CH)
     def _(chunk):
         row = rows_of(chunk)
-        for k in (O1, A, B, I1):
-            res = off_diagonal(row, first[k + 1], first[k], first[k + 2], *faces(k))
-            res = res + (1.0 - 1.0 / CENTER) * rhs[k, pl.ds(row, CH), :]
-            here = at(*first[k + 1], row)
-            move = step_a * here + step_b * (at(state, IVS + k, row) * res)
-            put(e2, k, row, move)
-            if k in (A, B):
-                r1[k - A, pl.ds(row, CH), :] = res
-                if x2 is not None:
-                    x2[3 + k - A, pl.ds(row, CH), :] = here + move
+        here = at(x1, 0, row)
+        res = lateral(row, (x1, 0), (state, FXO), (state, FYO)) + (1.0 - 1.0 / CENTER) * sx[0, pl.ds(row, CH), :]
+        res = res + (at(state, Z0, row) * sx[1, pl.ds(row, CH), :] + at(state, Z1, row) * at(state, XA, row))
+        e2o = step_a * here + step_b * (at(state, IVO, row) * res)
+        res = at(state, PA, row) + at(state, Z1, row) * here
+        e2a = step_a * at(state, XA, row) + step_b * (at(state, IVA, row) * res)
+        put(e2, 0, row, e2a)
+        own[2, pl.ds(row, CH), :] = at(state, XA, row) + e2a
+        own[3, pl.ds(row, CH), :] = at(state, X2B, row)
+        res = res - at(state, DA, row) * e2a
+        part[pl.ds(row, CH), :] = res + (at(state, Z1, row) * e2o + at(state, Z2, row) * at(state, EB, row))
+        res = at(state, PI, row) + at(state, Z4, row) * xi[pl.ds(row, CH), :]
+        e2i = step_a * at(state, XI, row) + step_b * (at(state, IVI, row) * res)
+        own[1, pl.ds(row, CH), :] = at(state, PB, row) + (at(state, Z2, row) * e2a + at(state, Z3, row) * e2i)
+
+    leaving += [copies.start(own.at[1], side.at[1]), copies.start(own.at[2:4], side.at[4:6])]
 
     @pl.loop(0, N // CH)
     def _(chunk):
         row = rows_of(chunk)
-        found = []
-        for k in (A, B):
-            res = r1[k - A, pl.ds(row, CH), :] - at(state, DGS + k - A, row) * at(e2, k, row)
-            found.append(res + off_diagonal(row, (e2, k), (e2, k - 1), (e2, k + 1), *faces(k)))
-        done(row, *found)
-
-
-SPLIT = 2
-HELD = 5
-
-
-def pre_kernel(g, gs, bs, bx, state, sx, xi, pack, over, side, rhs, x1, e2, r1, red, cpl, packed, sems):
-    _, par, _ = position()
-    inner = 1 - par
-    copies = Copies(sems)
-    started = [copies.start(ref, rhs.at[k]) for k, ref in enumerate((sx.at[0], g.at[par], g.at[inner], gs.at[par]))]
-    started += [fill(copies, sx.at[1], x1, 0), fill(copies, xi, x1, 2)]
-    leaving = [copies.start(bs.at[par], over.at[2]), copies.start(bx.at[inner], side.at[2])]
-    clear_pads(x1, range(3))
-    clear_pads(e2, range(4))
-    for copy in started:
-        copy.wait()
-
-    def done(row, ra, rb):
-        red[pl.ds(row, CH), :] = ra + rb
-        for ref in (over, side):
-            ref[0, pl.ds(row, CH), :] = ra
-            ref[1, pl.ds(row, CH), :] = rb
-
-    pre_smooth(state, rhs, x1, e2, r1, side, done)
+        res = part[pl.ds(row, CH), :] + lateral(row, (e2, 0), (state, FXA), (state, FYA))
+        own[0, pl.ds(row, CH), :] = res
+        red[pl.ds(row, CH), :] = res + own[1, pl.ds(row, CH), :]
+
+    leaving.append(copies.start(own.at[0], side.at[0]))
     cpl[0:N, :] = dot(red[...], pair_matrix(N, NC))
     rc = 0.125 * (cpl[pl.ds(0, NC, 2), :] + cpl[pl.ds(1, NC, 2), :])
     fields = (rc * state[COARSE_AT, 0:NC, NC:N], state[COARSE_AT, 0:NC, 0:NC])
@@ -316,11 +356,9 @@
         leaving.append(copies.start(packed.at[piece], pack.at[piece]))
     for copy in leaving:
         copy.wait()
-    clear_outside([(side, 2)])
-
-
-def coarse_kernel(recv, other, over, pack, cpl, packed, sems):
-    del over
+
+
+def coarse_kernel(recv, other, pack, cpl, packed, sems):
     index, par, _ = position()
     rows = 2 * HELD
     planes = recv.shape[0] // rows
@@ -390,17 +428,20 @@
     order = (par, inner)
     alive = outer_mask()
     copies = Copies(sems)
-    source = (over.at[2], bx.at[par], bx.at[inner], b.at[par], b.at[inner], bs.at[par], bs.at[inner], side.at[2])
-    started = [fill(copies, ref, coef, p) for p, ref in enumerate(source)]
-    source = (over.at[1], over.at[0], own.at[0], own.at[1], side.at[1], side.at[0])
-    started += [copies.start(ref, before.at[k]) for k, ref in enumerate(source)]
-    started.append(copies.start(own.at[3:5], x2v))
+    source = (over.at[2], bx.at[par], bx.at[inner], b.at[par], b.at[inner], bs.at[par], bs.at[inner], side.at[3])
+    earlier = (over.at[1], over.at[0], own.at[0], own.at[1], side.at[1], side.at[0])
+    started = {}
+    for p in range(8):
+        started[p] = [fill(copies, source[p], coef, p)]
+        if 1 <= p <= 6:
+            started[p].append(copies.start(earlier[p - 1], before.at[p - 1]))
+    x2_copy = copies.start(own.at[4:6], x2v)
     clear_pads(coef, range(8))
     clear_pads(fx, range(4))
     clear_pads(pw, range(8))
     clear_pads(e4, range(6))
     clear_pads(e5, range(4))
-    spread = dot(w[...], pair_matrix(NC, N))
+    spread = dot(w[...], 0.5 * pair_matrix(NC, N))
     for side in (0, 1):
         wide[side] = spread[:, side * NC : (side + 1) * NC]
     for k, planes in enumerate(((0,), (1, 2), (3, 4), (5, 6), (7,))):
@@ -411,15 +452,21 @@
             half[pl.ds(1, NC, 2), :] = part
             for p in planes:
                 pw[p, PAD : PAD + N, side * NC : (side + 1) * NC] = half[...]
-    for copy in started:
-        copy.wait()
+
+    def arrived(planes):
+        for p in planes:
+            for copy in started[p]:
+                copy.wait()
+
+    arrived(range(3))
     clear_outside([(coef, 0), (coef, 1), (coef, 2)])
 
-    @pl.loop(0, N // CH)
-    def _(chunk):
-        row = rows_of(chunk)
+    @whole_planes
+    def _(row):
         for k in range(6):
             p = k + 1
+            if k > 0:
+                arrived([p + 1])
             win = window(coef, p, row)
             ahead = pltpu.roll(win, win.shape[0] - 1, 0)
             mid = win[PAD : PAD + CH]
@@ -428,14 +475,14 @@
             prv = jnp.where(lane == 0, 0.0, right(mid))
             under, over = at(coef, p - 1, row), at(coef, p + 1, row)
             around = (ahead[PAD : PAD + CH] + shifted(win, -1)) + (nxt + prv) + (under + over)
-            diag = 3.0 * mid + 0.5 * around
+            diag = 6.0 * mid + around
             if k < 2:
-                inv = alive / jnp.where(diag > 0.0, diag, 1.0)
+                inv = alive * inverse(jnp.where(diag > 0.0, diag, 1.0))
             else:
-                inv = 1.0 / diag
-            fxw = 0.5 * (win + ahead)
-            fyc = jnp.where(lane == N - 1, 0.0, 0.5 * (mid + nxt))
-            below, above = 0.5 * (mid + under), 0.5 * (mid + over)
+                inv = inverse(diag)
+            fxw = win + ahead
+            fyc = jnp.where(lane == N - 1, 0.0, mid + nxt)
+            below, above = mid + under, mid + over
             if 1 <= k <= 4:
                 put(fx, k - 1, row, fxw[PAD : PAD + CH])
                 fy[k - 1, pl.ds(row, CH), :] = fyc
@@ -455,6 +502,7 @@
                 r3[k - 1, pl.ds(row, CH), :] = res
             put(e4, k, row, (1.0 / CENTER) * (inv * res))
 
+    x2_copy.wait()
     step_a, step_b = FINE[0]
 
     def off(v, k, shift, row):
@@ -466,9 +514,8 @@
         total = total + fz[k, pl.ds(row, CH), :] * at(v, k + shift - 1, row)
         return total + fz[k + 1, pl.ds(row, CH), :] * at(v, k + shift + 1, row)
 
-    @pl.loop(0, N // CH)
-    def _(chunk):
-        row = rows_of(chunk)
+    @whole_planes
+    def _(row):
         for k in range(4):
             res = off(e4, k, 1, row) + (1.0 - 1.0 / CENTER) * r3[k, pl.ds(row, CH), :]
             here = at(e4, k + 1, row)
@@ -476,18 +523,17 @@
             put(e5, k, row, move)
             if k in (1, 2):
                 r4[k - 1, pl.ds(row, CH), :] = res
-                x5v[k - 1, pl.ds(row, CH), :] = (x2v[k - 1, pl.ds(row, CH), :] + at(pw, k + 2, row)) + (here + move)
+                x5v[k - 1, pl.ds(row, CH), :] = x2v[k - 1, pl.ds(row, CH), :] + 2.0 * (at(pw, k + 2, row) + (here + move))
 
     leaving = [copies.start(x5v.at[k], x5.at[order[k]]) for k in range(2)]
 
-    @pl.loop(0, N // CH)
-    def _(chunk):
-        row = rows_of(chunk)
+    @whole_planes
+    def _(row):
         for k in (1, 2):
             res = r4[k - 1, pl.ds(row, CH), :] - dg[k - 1, pl.ds(row, CH), :] * at(e5, k, row)
             r5v[k - 1, pl.ds(row, CH), :] = res + off(e5, k, 0, row)
-
-    leaving += [copies.start(r5v.at[k], r5.at[order[k]]) for k in range(2)]
+            leaving.append(copies.start(r5v.at[k - 1], r5.at[order[k - 1]]))
+
     for copy in leaving:
         copy.wait()
 
@@ -512,8 +558,10 @@
     def swap(v):
         return lax.ppermute(v, AXES, inside)
 
-    def cross(v):
-        return lax.ppermute(v, AXES, across)
+    between = [pair for pair in across if abs(pair[0] - pair[1]) == 1]
+
+    def cross(v, ends=True):
+        return lax.ppermute(v, AXES, across if ends else between)
 
     def everywhere(v):
         rows = v.shape[0]
@@ -526,25 +574,25 @@
     bx = cross(b)
     gs = swap(g)
     (send,) = call(first_kernel, [(two, VM)], [(3,) + padded], 3, 1 << 20, (g, VM), (b, ANY), (bs, ANY))
-    sx = cross(send)
+    sx = cross(send, False)
     state, xa = call(
         ready_kernel,
         [((STATE,) + padded, VM), (plane, VM)],
-        [(6,) + padded, (4,) + plane, (3 * N, N), (3 * N, NC)],
+        [(6,) + padded, (3,) + plane, (8,) + padded, (3 * N, N), (3 * N, NC)],
         9,
         6 << 20,
         (g, ANY), (gs, ANY), (b, ANY), (bs, ANY), (bx, ANY), (send, ANY),
     )
     xi = swap(xa)
-    pack, over, side = call(
+    pack, side = call(
         pre_kernel,
-        [((2 * HELD * total, NC), HBM), ((3,) + plane, VM), ((5,) + plane, VM)],
-        [(4,) + plane, (3,) + padded, (4,) + padded, two, plane, (2 * (NC + 16), NC), (2 * HELD * total, NC)],
-        8 + SPLIT,
+        [((2 * HELD * total, NC), HBM), ((6,) + plane, HBM)],
+        [(1,) + padded, (1,) + padded, plane, plane, (2 * (NC + 16), NC), (2 * HELD * total, NC), (4,) + plane, plane],
+        5 + SPLIT,
         6 << 20,
-        (g, ANY), (gs, ANY), (bs, ANY), (bx, ANY), (state, VM), (sx, ANY), (xi, ANY),
+        (bs, ANY), (bx, ANY), (state, VM), (sx, VM), (xi, VM),
     )
-    from_over = cross(over)
+    from_over = cross(side, False)
     from_side = swap(side)
     own = swap(from_side)
     got = everywhere(pack)
@@ -554,7 +602,7 @@
         [(total + 16, NC), (5 * NC, NC)],
         1,
         4 << 20,
-        (got, VM), (swap(got), VM), (from_over, ANY),
+        (got, VM), (swap(got), VM),
     )
     w = everywhere(back)
     x5, r5 = call(

time: 84.9 us -> 76.7 us (0.903)
  blocking collectives: 19.6 us -> 0 us
  waiting for transfers between devices: 19.5 us -> 26.8 us
  starting transfers between devices: 26.7 us -> 32.7 us
  Pallas kernels: 16 us -> 13.8 us
    all_to_all x1 -> x0, blocking collectives: 19.6 us -> none  [everywhere(): lax.all_to_all(v.reshape(rows, 1, NC), AXES, 0, 0, tiled=True)]
    all_to_all x1 -> x2, starting transfers between devices: 4.45 us -> 12.8 us  [everywhere(): lax.all_to_all(v.reshape(rows, 1, NC), AXES, 0, 0, tiled=True)]
    ppermute x6, starting transfers between devices: 17.7 us -> 10.8 us  [swap(): return lax.ppermute(v, AXES, inside)]
    all_to_all x1 -> x2, waiting for transfers between devices: 13.1 us -> 19.4 us  [everywhere(): lax.all_to_all(v.reshape(rows, 1, NC), AXES, 0, 0, tiled=True)]
    ppermute x3, starting transfers between devices: 4.54 us -> 9.17 us  [cross(): return lax.ppermute(v, AXES, across if ends else between)]
    pallas_call x5, Pallas kernels: 16 us -> 13.8 us  [call(): pl.pallas_call(kernel, out_shape=[jax.ShapeDtypeStruct(s, jnp.float32) fo...]
    ppermute x6, waiting for transfers between devices: 1.18 us -> 2.9 us  [swap(): return lax.ppermute(v, AXES, inside)]
  transfers between devices with their start and end apart: 10 -> 11, of which waited for: 4 -> 6; matrix products, arithmetic and copies ran while one was open for 0% -> 0% of each run, Pallas kernels for 5% -> 7%
where the time goes in v2:
time: 76.7 us; the launch traced here: 76.3 us
  starting transfers between devices  32.7 us (43%)
  waiting for transfers between devices  26.8 us (35%)
  Pallas kernels  13.8 us (18%)
  local copies, waits for them, and re-layouts  2.12 us (3%)
  between operations  0.89 us (1%)
    all_to_all x2, waiting for transfers between devices, everywhere(): lax.all_to_all(v.reshape(rows, 1, NC), AXES, 0, 0, tiled=True)  19.4 us
    pallas_call x5, Pallas kernels, call(): pl.pallas_call(kernel, out_shape=[jax.ShapeDtypeStruct(s, jnp.float32) fo...  13.8 us
    all_to_all x2, starting transfers between devices, everywhere(): lax.all_to_all(v.reshape(rows, 1, NC), AXES, 0, 0, tiled=True)  12.8 us
    ppermute x6, starting transfers between devices, swap(): return lax.ppermute(v, AXES, inside)  10.8 us
    ppermute x3, starting transfers between devices, cross(): return lax.ppermute(v, AXES, across if ends else between)  9.17 us
    ppermute x3, waiting for transfers between devices, cross(): return lax.ppermute(v, AXES, across if ends else between)  4.49 us
    ppermute x6, waiting for transfers between devices, swap(): return lax.ppermute(v, AXES, inside)  2.9 us
    unnamed x6, local copies, waits for them, and re-layouts  2.12 us
  transfers between devices with their start and end apart: 11, of which 6 were waited for; matrix products, arithmetic and copies ran while one was open for 0% of the time, Pallas kernels for 7%

profile of v2, /device:TPU:1, one launch (start us, length us, event | category | flops | bytes accessed | tf_op | source)
XLA Modules:
  0.0 76.3 jit_solution(14804856297172067359)
XLA Ops:
  0.6 1.5 %collective-permute-start = (f32[2,256,256]{2,1,0:T(8,128)}, f32[2,256,256]{2,1,0:T(8,128)S(1)}, u32[]{:S(2)}, u32[]{:S(2)}) collective-permute-start(f32[2,256,256]{2,1,0:T(8,128)} %b.5), channel_id=1, source_target_pairs={{0,1},{1,0},{2,3},{3,2},{4,5},{5,4},{6,7},{7,6},{8,9},{9,8},{10,11... | collective-permute-start | bytes 1572872 | tf_op jit(solution)/shard_map/ppermute | solution.py:559
  2.1 0.1 collective-permute-start.2
  2.2 2.0 %collective-permute-start.1 = (f32[2,256,256]{2,1,0:T(8,128)}, f32[2,256,256]{2,1,0:T(8,128)S(1)}, u32[]{:S(2)}, u32[]{:S(2)}) collective-permute-start(f32[2,256,256]{2,1,0:T(8,128)} %b.5), channel_id=1, source_target_pairs={{1,2},{3,4},{5,6},{7,8},{9,10},{11,12},{13,14},{15,16},{17,18},{19... | collective-permute-start | bytes 1572872 | tf_op jit(solution)/shard_map/ppermute | solution.py:564
  4.2 0.0 collective-permute-done.bs
  4.2 0.0 copy-start
  4.3 1.1 %copy-done = f32[2,256,256]{2,1,0:T(8,128)S(1)} copy-done((f32[2,256,256]{2,1,0:T(8,128)S(1)}, f32[2,256,256]{2,1,0:T(8,128)}, u32[]{:S(2)}) %copy-start) | copy-done | bytes 524312
  5.3 0.0 copy-start.2
  5.3 1.0 %copy-done.2 = f32[2,256,256]{2,1,0:T(8,128)S(1)} copy-done((f32[2,256,256]{2,1,0:T(8,128)S(1)}, f32[2,256,256]{2,1,0:T(8,128)}, u32[]{:S(2)}) %copy-start.2) | copy-done | bytes 524312
  6.4 0.4 shard_map.41.sent
  6.8 3.5 %collective-permute-start.3 = (f32[2,256,256]{2,1,0:T(8,128)S(1)}, f32[2,256,256]{2,1,0:T(8,128)S(1)}, u32[]{:S(2)}, u32[]{:S(2)}) collective-permute-start(f32[2,256,256]{2,1,0:T(8,128)S(1)} %shard_map.41.sent), channel_id=1, source_target_pairs={{1,2},{3,4},{5,6},{7,8},{9,10},{11,12},{13,14},{15,16},{17,18},{19... | collective-permute-start | bytes 1572872 | tf_op jit(solution)/shard_map/ppermute | solution.py:564
  10.3 0.0 collective-permute-done.2.gs
  10.3 1.0 %collective-permute-done.1.bx = f32[2,256,256]{2,1,0:T(8,128)S(1)} collective-permute-done((f32[2,256,256]{2,1,0:T(8,128)}, f32[2,256,256]{2,1,0:T(8,128)S(1)}, u32[]{:S(2)}, u32[]{:S(2)}) %collective-permute-start.1) | collective-permute-done | bytes 524320 | tf_op jit(solution)/shard_map/ppermute | solution.py:564
  11.3 2.6 %shard_map.42 = (f32[21,272,256]{2,1,0:T(8,128)S(1)}, f32[256,256]{1,0:T(8,128)S(1)}) custom-call(f32[2,256,256]{2,1,0:T(8,128)S(1)} %copy-done.2, f32[2,256,256]{2,1,0:T(8,128)S(1)} %collective-permute-done.2.gs, f32[2,256,256]{2,1,0:T(8,128)S(1)} %copy-done, f32[2,256,256]{2,1,0:T(8,128)S(1)} %collective-permute-done.bs, ...), custom_call_target="tpu_custom_call" | custom-call | flops 6291456 | bytes 6291456 | tf_op jit(solution)/shard_map/pallas_call | solution.py:542
  13.9 7.0 %collective-permute-start.4 = (f32[256,256]{1,0:T(8,128)S(1)}, f32[256,256]{1,0:T(8,128)S(1)}, u32[]{:S(2)}, u32[]{:S(2)}) collective-permute-start(f32[256,256]{1,0:T(8,128)S(1)} %get-tuple-element.7), channel_id=1, source_target_pairs={{0,1},{1,0},{2,3},{3,2},{4,5},{5,4},{6,7},{7,6},{8,9},{9,8},{10,11... | collective-permute-start | bytes 786440 | tf_op jit(solution)/shard_map/ppermute | solution.py:559
  20.9 1.2 %collective-permute-done.4.xi = f32[256,256]{1,0:T(8,128)S(1)} collective-permute-done((f32[256,256]{1,0:T(8,128)S(1)}, f32[256,256]{1,0:T(8,128)S(1)}, u32[]{:S(2)}, u32[]{:S(2)}) %collective-permute-start.4) | collective-permute-done | bytes 262176 | tf_op jit(solution)/shard_map/ppermute | solution.py:559
  22.0 0.0 collective-permute-done.3.sx
  22.0 1.9 %shard_map.43 = (f32[1280,128]{1,0:T(8,128)}, f32[6,256,256]{2,1,0:T(8,128)}) custom-call(f32[2,256,256]{2,1,0:T(8,128)S(1)} %collective-permute-done.bs, f32[2,256,256]{2,1,0:T(8,128)S(1)} %collective-permute-done.1.bx, f32[21,272,256]{2,1,0:T(8,128)S(1)} %get-tuple-element.6.state, f32[2,256,256]{2,1,0:T(8,128)S(1)} %collective-permute-done.3.sx, ...), custom_call_target="tpu_custom_call" | custom-call | flops 6291456 | bytes 6291456 | tf_op jit(solution)/shard_map/pallas_call | solution.py:542
  23.9 0.5 collective-permute-start.5
  24.4 9.0 %all-to-all-start = ((f32[1280,1,128]{2,1,0:T(1,128)}), f32[1280,1,128]{2,1,0:T(1,128)S(1)}, u32[]{:S(2)}, u32[]{:S(2)}) async-start(f32[1280,1,128]{2,1,0:T(1,128)} %bitcast.1), calls=%async_computation | async-start | bytes 1310720 | tf_op jit(solution)/shard_map/all_to_all | solution.py:568
  33.4 3.7 %collective-permute-start.7 = (f32[6,256,256]{2,1,0:T(8,128)}, f32[6,256,256]{2,1,0:T(8,128)}, u32[]{:S(2)}, u32[]{:S(2)}) collective-permute-start(f32[6,256,256]{2,1,0:T(8,128)} %get-tuple-element.8), channel_id=1, source_target_pairs={{1,2},{3,4},{5,6},{7,8},{9,10},{11,12},{13,14},{15,16},{17,18},{19... | collective-permute-start | bytes 4718600 | tf_op jit(solution)/shard_map/ppermute | solution.py:564
  37.0 0.0 collective-permute-done.5.side
  37.0 0.1 collective-permute-start.6
  37.1 11.2 %all-to-all-done = f32[1280,1,128]{2,1,0:T(1,128)S(1)} async-done(((f32[1280,1,128]{2,1,0:T(1,128)}), f32[1280,1,128]{2,1,0:T(1,128)S(1)}, u32[]{:S(2)}, u32[]{:S(2)}) %all-to-all-start) | async-done | bytes 655392 | tf_op jit(solution)/shard_map/all_to_all | solution.py:568
  48.3 1.6 %collective-permute-start.8 = (f32[1280,128]{1,0:T(8,128)S(1)}, f32[1280,128]{1,0:T(8,128)S(1)}, u32[]{:S(2)}, u32[]{:S(2)}) collective-permute-start(f32[1280,128]{1,0:T(8,128)S(1)} %bitcast.8), channel_id=1, source_target_pairs={{0,1},{1,0},{2,3},{3,2},{4,5},{5,4},{6,7},{7,6},{8,9},{9,8},{10,11... | collective-permute-start | bytes 1966088 | tf_op jit(solution)/shard_map/ppermute | solution.py:559
  50.0 1.7 %collective-permute-done.8.other = f32[1280,128]{1,0:T(8,128)S(1)} collective-permute-done((f32[1280,128]{1,0:T(8,128)S(1)}, f32[1280,128]{1,0:T(8,128)S(1)}, u32[]{:S(2)}, u32[]{:S(2)}) %collective-permute-start.8) | collective-permute-done | bytes 655392 | tf_op jit(solution)/shard_map/ppermute | solution.py:559
  51.7 2.2 %shard_map.44 = f32[640,128]{1,0:T(8,128)} custom-call(f32[1280,128]{1,0:T(8,128)S(1)} %bitcast.9, f32[1280,128]{1,0:T(8,128)S(1)} %collective-permute-done.8.other), custom_call_target="tpu_custom_call" | custom-call | flops 4194304 | bytes 4194304 | tf_op jit(solution)/shard_map/pallas_call | solution.py:542
  53.8 3.8 %all-to-all-start.1 = ((f32[640,1,128]{2,1,0:T(1,128)}), f32[640,1,128]{2,1,0:T(1,128)S(1)}, u32[]{:S(2)}, u32[]{:S(2)}) async-start(f32[640,1,128]{2,1,0:T(1,128)} %bitcast.4), calls=%async_computation.1 | async-start | bytes 655360 | tf_op jit(solution)/shard_map/all_to_all | solution.py:568
  57.7 3.4 %collective-permute-done.7.over = f32[6,256,256]{2,1,0:T(8,128)} collective-permute-done((f32[6,256,256]{2,1,0:T(8,128)}, f32[6,256,256]{2,1,0:T(8,128)}, u32[]{:S(2)}, u32[]{:S(2)}) %collective-permute-start.7) | collective-permute-done | bytes 1572896 | tf_op jit(solution)/shard_map/ppermute | solution.py:564
  61.1 8.2 %all-to-all-done.1 = f32[640,1,128]{2,1,0:T(1,128)S(1)} async-done(((f32[640,1,128]{2,1,0:T(1,128)}), f32[640,1,128]{2,1,0:T(1,128)S(1)}, u32[]{:S(2)}, u32[]{:S(2)}) %all-to-all-start.1) | async-done | bytes 327712 | tf_op jit(solution)/shard_map/all_to_all | solution.py:568
  69.3 0.0 collective-permute-done.6.own
  69.3 0.0 copy-done.1
  69.3 6.9 %shard_map.45 = (f32[2,256,256]{2,1,0:T(8,128)}, f32[2,256,256]{2,1,0:T(8,128)}) custom-call(f32[2,256,256]{2,1,0:T(8,128)S(1)} %copy-done.1, f32[2,256,256]{2,1,0:T(8,128)S(1)} %collective-permute-done.bs, f32[2,256,256]{2,1,0:T(8,128)S(1)} %collective-permute-done.1.bx, f32[6,256,256]{2,1,0:T(8,128)} %collective-permute-done.6.own, ...), custom_call_target="tpu_custom_call" | custom-call | flops 8388608 | bytes 8388608 | tf_op jit(solution)/shard_map/pallas_call | solution.py:542
  (1 shorter events, 0.0 us)
Async XLA Ops:
  0.6 3.6 %collective-permute-start = (f32[2,256,256]{2,1,0:T(8,128)}, f32[2,256,256]{2,1,0:T(8,128)S(1)}, u32[]{:S(2)}, u32[]{:S(2)}) collective-permute-start(f32[2,256,256]{2,1,0:T(8,128)} %b.5), channel_id=1, source_target_pairs={{0,1},{1,0},{2,3},{3,2},{4,5},{5,4},{6,7},{7,6},{8,9},{9,8},{10,11... | collective-permute-start | bytes 1572872 | tf_op jit(solution)/shard_map/ppermute | solution.py:559
  2.1 8.1 %collective-permute-start.2 = (f32[2,256,256]{2,1,0:T(8,128)}, f32[2,256,256]{2,1,0:T(8,128)S(1)}, u32[]{:S(2)}, u32[]{:S(2)}) collective-permute-start(f32[2,256,256]{2,1,0:T(8,128)} %g.3), channel_id=1, source_target_pairs={{0,1},{1,0},{2,3},{3,2},{4,5},{5,4},{6,7},{7,6},{8,9},{9,8},{10,11... | collective-permute-start | bytes 1572872 | tf_op jit(solution)/shard_map/ppermute | solution.py:559
  2.2 9.1 %collective-permute-start.1 = (f32[2,256,256]{2,1,0:T(8,128)}, f32[2,256,256]{2,1,0:T(8,128)S(1)}, u32[]{:S(2)}, u32[]{:S(2)}) collective-permute-start(f32[2,256,256]{2,1,0:T(8,128)} %b.5), channel_id=1, source_target_pairs={{1,2},{3,4},{5,6},{7,8},{9,10},{11,12},{13,14},{15,16},{17,18},{19... | collective-permute-start | bytes 1572872 | tf_op jit(solution)/shard_map/ppermute | solution.py:564
  4.2 1.1 %copy-start = (f32[2,256,256]{2,1,0:T(8,128)S(1)}, f32[2,256,256]{2,1,0:T(8,128)}, u32[]{:S(2)}) copy-start(f32[2,256,256]{2,1,0:T(8,128)} %b.5) | copy-start | bytes 1572868
  5.3 1.0 %copy-start.2 = (f32[2,256,256]{2,1,0:T(8,128)S(1)}, f32[2,256,256]{2,1,0:T(8,128)}, u32[]{:S(2)}) copy-start(f32[2,256,256]{2,1,0:T(8,128)} %g.3) | copy-start | bytes 1572868
  6.8 15.3 %collective-permute-start.3 = (f32[2,256,256]{2,1,0:T(8,128)S(1)}, f32[2,256,256]{2,1,0:T(8,128)S(1)}, u32[]{:S(2)}, u32[]{:S(2)}) collective-permute-start(f32[2,256,256]{2,1,0:T(8,128)S(1)} %shard_map.41.sent), channel_id=1, source_target_pairs={{1,2},{3,4},{5,6},{7,8},{9,10},{11,12},{13,14},{15,16},{17,18},{19... | collective-permute-start | bytes 1572872 | tf_op jit(solution)/shard_map/ppermute | solution.py:564
  13.9 8.1 %collective-permute-start.4 = (f32[256,256]{1,0:T(8,128)S(1)}, f32[256,256]{1,0:T(8,128)S(1)}, u32[]{:S(2)}, u32[]{:S(2)}) collective-permute-start(f32[256,256]{1,0:T(8,128)S(1)} %get-tuple-element.7), channel_id=1, source_target_pairs={{0,1},{1,0},{2,3},{3,2},{4,5},{5,4},{6,7},{7,6},{8,9},{9,8},{10,11... | collective-permute-start | bytes 786440 | tf_op jit(solution)/shard_map/ppermute | solution.py:559
  23.9 13.1 %collective-permute-start.5 = (f32[6,256,256]{2,1,0:T(8,128)}, f32[6,256,256]{2,1,0:T(8,128)}, u32[]{:S(2)}, u32[]{:S(2)}) collective-permute-start(f32[6,256,256]{2,1,0:T(8,128)} %get-tuple-element.8), channel_id=1, source_target_pairs={{0,1},{1,0},{2,3},{3,2},{4,5},{5,4},{6,7},{7,6},{8,9},{9,8},{10,11... | collective-permute-start | bytes 4718600 | tf_op jit(solution)/shard_map/ppermute | solution.py:559
  24.4 44.9 %copy-start.1 = (f32[2,256,256]{2,1,0:T(8,128)S(1)}, f32[2,256,256]{2,1,0:T(8,128)}, u32[]{:S(2)}) copy-start(f32[2,256,256]{2,1,0:T(8,128)} %b.5) | copy-start | bytes 1572868
  24.4 23.9 %all-to-all-start = ((f32[1280,1,128]{2,1,0:T(1,128)}), f32[1280,1,128]{2,1,0:T(1,128)S(1)}, u32[]{:S(2)}, u32[]{:S(2)}) async-start(f32[1280,1,128]{2,1,0:T(1,128)} %bitcast.1), calls=%async_computation | async-start | bytes 1310720 | tf_op jit(solution)/shard_map/all_to_all | solution.py:568
  33.4 27.7 %collective-permute-start.7 = (f32[6,256,256]{2,1,0:T(8,128)}, f32[6,256,256]{2,1,0:T(8,128)}, u32[]{:S(2)}, u32[]{:S(2)}) collective-permute-start(f32[6,256,256]{2,1,0:T(8,128)} %get-tuple-element.8), channel_id=1, source_target_pairs={{1,2},{3,4},{5,6},{7,8},{9,10},{11,12},{13,14},{15,16},{17,18},{19... | collective-permute-start | bytes 4718600 | tf_op jit(solution)/shard_map/ppermute | solution.py:564
  37.0 32.3 %collective-permute-start.6 = (f32[6,256,256]{2,1,0:T(8,128)}, f32[6,256,256]{2,1,0:T(8,128)}, u32[]{:S(2)}, u32[]{:S(2)}) collective-permute-start(f32[6,256,256]{2,1,0:T(8,128)} %collective-permute-done.5.side), channel_id=1, source_target_pairs={{0,1},{1,0},{2,3},{3,2},{4,5},{5,4},{6,7},{7,6},{8,9},{9,8},{10,11... | collective-permute-start | bytes 4718600 | tf_op jit(solution)/shard_map/ppermute | solution.py:559
  48.3 3.4 %collective-permute-start.8 = (f32[1280,128]{1,0:T(8,128)S(1)}, f32[1280,128]{1,0:T(8,128)S(1)}, u32[]{:S(2)}, u32[]{:S(2)}) collective-permute-start(f32[1280,128]{1,0:T(8,128)S(1)} %bitcast.8), channel_id=1, source_target_pairs={{0,1},{1,0},{2,3},{3,2},{4,5},{5,4},{6,7},{7,6},{8,9},{9,8},{10,11... | collective-permute-start | bytes 1966088 | tf_op jit(solution)/shard_map/ppermute | solution.py:559
  53.8 15.5 %all-to-all-start.1 = ((f32[640,1,128]{2,1,0:T(1,128)}), f32[640,1,128]{2,1,0:T(1,128)S(1)}, u32[]{:S(2)}, u32[]{:S(2)}) async-start(f32[640,1,128]{2,1,0:T(1,128)} %bitcast.4), calls=%async_computation.1 | async-start | bytes 655360 | tf_op jit(solution)/shard_map/all_to_all | solution.py:568

commit v3 on v2

--- a/solution.py
+++ b/solution.py
@@ -438,20 +438,20 @@
     x2_copy = copies.start(own.at[4:6], x2v)
     clear_pads(coef, range(8))
     clear_pads(fx, range(4))
-    clear_pads(pw, range(8))
+    clear_pads(pw, range(5))
     clear_pads(e4, range(6))
     clear_pads(e5, range(4))
     spread = dot(w[...], 0.5 * pair_matrix(NC, N))
     for side in (0, 1):
         wide[side] = spread[:, side * NC : (side + 1) * NC]
-    for k, planes in enumerate(((0,), (1, 2), (3, 4), (5, 6), (7,))):
+    held = (0, 1, 1, 2, 2, 3, 3, 4)
+    for k in range(5):
         z = jnp.where(par == 0, k, 4 - k)
         for side in (0, 1):
             part = wide[side, pl.ds(z, NC, 5), :]
             half[pl.ds(0, NC, 2), :] = part
             half[pl.ds(1, NC, 2), :] = part
-            for p in planes:
-                pw[p, PAD : PAD + N, side * NC : (side + 1) * NC] = half[...]
+            pw[k, PAD : PAD + N, side * NC : (side + 1) * NC] = half[...]
 
     def arrived(planes):
         for p in planes:
@@ -492,11 +492,11 @@
                     fz[4, pl.ds(row, CH), :] = above
             if k in (2, 3):
                 dg[k - 2, pl.ds(row, CH), :] = diag
-            v = window(pw, p, row)
+            v = window(pw, held[p], row)
             here = v[PAD : PAD + CH]
             total = fxw[PAD : PAD + CH] * shifted(v, 1) + shifted(fxw * v, -1)
             total = total + (fyc * left(here) + right(fyc * here))
-            total = total + (below * at(pw, p - 1, row) + above * at(pw, p + 1, row))
+            total = total + (below * at(pw, held[p - 1], row) + above * at(pw, held[p + 1], row))
             res = (before[k, pl.ds(row, CH), :] - diag * here) + total
             if 1 <= k <= 4:
                 r3[k - 1, pl.ds(row, CH), :] = res
@@ -523,7 +523,7 @@
             put(e5, k, row, move)
             if k in (1, 2):
                 r4[k - 1, pl.ds(row, CH), :] = res
-                x5v[k - 1, pl.ds(row, CH), :] = x2v[k - 1, pl.ds(row, CH), :] + 2.0 * (at(pw, k + 2, row) + (here + move))
+                x5v[k - 1, pl.ds(row, CH), :] = x2v[k - 1, pl.ds(row, CH), :] + 2.0 * (at(pw, held[k + 2], row) + (here + move))
 
     leaving = [copies.start(x5v.at[k], x5.at[order[k]]) for k in range(2)]
 
@@ -608,7 +608,7 @@
     x5, r5 = call(
         post_kernel,
         [(two, HBM), (two, HBM)],
-        [(8,) + padded, (4,) + padded, (4,) + plane, (5,) + plane, (4,) + plane, two, (6,) + plane, two, (8,) + padded, (4,) + plane, (6,) + padded, two, (4,) + padded, (N, NC), (2, 5 * NC, NC), two, two],
+        [(8,) + padded, (4,) + padded, (4,) + plane, (5,) + plane, (4,) + plane, two, (6,) + plane, two, (5,) + padded, (4,) + plane, (6,) + padded, two, (4,) + padded, (N, NC), (2, 5 * NC, NC), two, two],
         20,
         8 << 20,
         (b, ANY), (bs, ANY), (bx, ANY), (own, ANY), (from_over, ANY), (from_side, ANY), (w, VM),

time: 76.7 us -> 76.6 us (level)
  no operation moved by 1% of the time
where the time goes in v3:
time: 76.6 us; the launch traced here: 76.3 us
  starting transfers between devices  32.7 us (43%)
  waiting for transfers between devices  26.8 us (35%)
  Pallas kernels  13.8 us (18%)
  local copies, waits for them, and re-layouts  2.12 us (3%)
  between operations  0.89 us (1%)
    all_to_all x2, waiting for transfers between devices, everywhere(): lax.all_to_all(v.reshape(rows, 1, NC), AXES, 0, 0, tiled=True)  19.4 us
    pallas_call x5, Pallas kernels, call(): pl.pallas_call(kernel, out_shape=[jax.ShapeDtypeStruct(s, jnp.float32) fo...  13.8 us
    all_to_all x2, starting transfers between devices, everywhere(): lax.all_to_all(v.reshape(rows, 1, NC), AXES, 0, 0, tiled=True)  12.8 us
    ppermute x6, starting transfers between devices, swap(): return lax.ppermute(v, AXES, inside)  10.8 us
    ppermute x3, starting transfers between devices, cross(): return lax.ppermute(v, AXES, across if ends else between)  9.17 us
    ppermute x3, waiting for transfers between devices, cross(): return lax.ppermute(v, AXES, across if ends else between)  4.49 us
    ppermute x6, waiting for transfers between devices, swap(): return lax.ppermute(v, AXES, inside)  2.9 us
    unnamed x6, local copies, waits for them, and re-layouts  2.12 us
  transfers between devices with their start and end apart: 11, of which 6 were waited for; matrix products, arithmetic and copies ran while one was open for 0% of the time, Pallas kernels for 7%

profile of v3, /device:TPU:1, one launch (start us, length us, event | category | flops | bytes accessed | tf_op | source)
XLA Modules:
  0.0 76.3 jit_solution(6981811422865086440)
XLA Ops:
  0.6 1.5 %collective-permute-start = (f32[2,256,256]{2,1,0:T(8,128)}, f32[2,256,256]{2,1,0:T(8,128)S(1)}, u32[]{:S(2)}, u32[]{:S(2)}) collective-permute-start(f32[2,256,256]{2,1,0:T(8,128)} %b.5), channel_id=1, source_target_pairs={{0,1},{1,0},{2,3},{3,2},{4,5},{5,4},{6,7},{7,6},{8,9},{9,8},{10,11... | collective-permute-start | bytes 1572872 | tf_op jit(solution)/shard_map/ppermute | solution.py:559
  2.1 0.1 collective-permute-start.2
  2.2 2.0 %collective-permute-start.1 = (f32[2,256,256]{2,1,0:T(8,128)}, f32[2,256,256]{2,1,0:T(8,128)S(1)}, u32[]{:S(2)}, u32[]{:S(2)}) collective-permute-start(f32[2,256,256]{2,1,0:T(8,128)} %b.5), channel_id=1, source_target_pairs={{1,2},{3,4},{5,6},{7,8},{9,10},{11,12},{13,14},{15,16},{17,18},{19... | collective-permute-start | bytes 1572872 | tf_op jit(solution)/shard_map/ppermute | solution.py:564
  4.2 0.0 collective-permute-done.bs
  4.2 0.0 copy-start
  4.3 1.1 %copy-done = f32[2,256,256]{2,1,0:T(8,128)S(1)} copy-done((f32[2,256,256]{2,1,0:T(8,128)S(1)}, f32[2,256,256]{2,1,0:T(8,128)}, u32[]{:S(2)}) %copy-start) | copy-done | bytes 524312
  5.3 0.0 copy-start.2
  5.3 1.0 %copy-done.2 = f32[2,256,256]{2,1,0:T(8,128)S(1)} copy-done((f32[2,256,256]{2,1,0:T(8,128)S(1)}, f32[2,256,256]{2,1,0:T(8,128)}, u32[]{:S(2)}) %copy-start.2) | copy-done | bytes 524312
  6.4 0.4 shard_map.41.sent
  6.8 3.5 %collective-permute-start.3 = (f32[2,256,256]{2,1,0:T(8,128)S(1)}, f32[2,256,256]{2,1,0:T(8,128)S(1)}, u32[]{:S(2)}, u32[]{:S(2)}) collective-permute-start(f32[2,256,256]{2,1,0:T(8,128)S(1)} %shard_map.41.sent), channel_id=1, source_target_pairs={{1,2},{3,4},{5,6},{7,8},{9,10},{11,12},{13,14},{15,16},{17,18},{19... | collective-permute-start | bytes 1572872 | tf_op jit(solution)/shard_map/ppermute | solution.py:564
  10.3 0.0 collective-permute-done.2.gs
  10.3 1.0 %collective-permute-done.1.bx = f32[2,256,256]{2,1,0:T(8,128)S(1)} collective-permute-done((f32[2,256,256]{2,1,0:T(8,128)}, f32[2,256,256]{2,1,0:T(8,128)S(1)}, u32[]{:S(2)}, u32[]{:S(2)}) %collective-permute-start.1) | collective-permute-done | bytes 524320 | tf_op jit(solution)/shard_map/ppermute | solution.py:564
  11.3 2.6 %shard_map.42 = (f32[21,272,256]{2,1,0:T(8,128)S(1)}, f32[256,256]{1,0:T(8,128)S(1)}) custom-call(f32[2,256,256]{2,1,0:T(8,128)S(1)} %copy-done.2, f32[2,256,256]{2,1,0:T(8,128)S(1)} %collective-permute-done.2.gs, f32[2,256,256]{2,1,0:T(8,128)S(1)} %copy-done, f32[2,256,256]{2,1,0:T(8,128)S(1)} %collective-permute-done.bs, ...), custom_call_target="tpu_custom_call" | custom-call | flops 6291456 | bytes 6291456 | tf_op jit(solution)/shard_map/pallas_call | solution.py:542
  13.9 7.0 %collective-permute-start.4 = (f32[256,256]{1,0:T(8,128)S(1)}, f32[256,256]{1,0:T(8,128)S(1)}, u32[]{:S(2)}, u32[]{:S(2)}) collective-permute-start(f32[256,256]{1,0:T(8,128)S(1)} %get-tuple-element.7), channel_id=1, source_target_pairs={{0,1},{1,0},{2,3},{3,2},{4,5},{5,4},{6,7},{7,6},{8,9},{9,8},{10,11... | collective-permute-start | bytes 786440 | tf_op jit(solution)/shard_map/ppermute | solution.py:559
  20.9 1.2 %collective-permute-done.4.xi = f32[256,256]{1,0:T(8,128)S(1)} collective-permute-done((f32[256,256]{1,0:T(8,128)S(1)}, f32[256,256]{1,0:T(8,128)S(1)}, u32[]{:S(2)}, u32[]{:S(2)}) %collective-permute-start.4) | collective-permute-done | bytes 262176 | tf_op jit(solution)/shard_map/ppermute | solution.py:559
  22.0 0.0 collective-permute-done.3.sx
  22.0 1.9 %shard_map.43 = (f32[1280,128]{1,0:T(8,128)}, f32[6,256,256]{2,1,0:T(8,128)}) custom-call(f32[2,256,256]{2,1,0:T(8,128)S(1)} %collective-permute-done.bs, f32[2,256,256]{2,1,0:T(8,128)S(1)} %collective-permute-done.1.bx, f32[21,272,256]{2,1,0:T(8,128)S(1)} %get-tuple-element.6.state, f32[2,256,256]{2,1,0:T(8,128)S(1)} %collective-permute-done.3.sx, ...), custom_call_target="tpu_custom_call" | custom-call | flops 6291456 | bytes 6291456 | tf_op jit(solution)/shard_map/pallas_call | solution.py:542
  23.9 0.5 collective-permute-start.5
  24.4 9.0 %all-to-all-start = ((f32[1280,1,128]{2,1,0:T(1,128)}), f32[1280,1,128]{2,1,0:T(1,128)S(1)}, u32[]{:S(2)}, u32[]{:S(2)}) async-start(f32[1280,1,128]{2,1,0:T(1,128)} %bitcast.1), calls=%async_computation | async-start | bytes 1310720 | tf_op jit(solution)/shard_map/all_to_all | solution.py:568
  33.4 3.7 %collective-permute-start.7 = (f32[6,256,256]{2,1,0:T(8,128)}, f32[6,256,256]{2,1,0:T(8,128)}, u32[]{:S(2)}, u32[]{:S(2)}) collective-permute-start(f32[6,256,256]{2,1,0:T(8,128)} %get-tuple-element.8), channel_id=1, source_target_pairs={{1,2},{3,4},{5,6},{7,8},{9,10},{11,12},{13,14},{15,16},{17,18},{19... | collective-permute-start | bytes 4718600 | tf_op jit(solution)/shard_map/ppermute | solution.py:564
  37.0 0.0 collective-permute-done.5.side
  37.0 0.1 collective-permute-start.6
  37.1 11.2 %all-to-all-done = f32[1280,1,128]{2,1,0:T(1,128)S(1)} async-done(((f32[1280,1,128]{2,1,0:T(1,128)}), f32[1280,1,128]{2,1,0:T(1,128)S(1)}, u32[]{:S(2)}, u32[]{:S(2)}) %all-to-all-start) | async-done | bytes 655392 | tf_op jit(solution)/shard_map/all_to_all | solution.py:568
  48.3 1.6 %collective-permute-start.8 = (f32[1280,128]{1,0:T(8,128)S(1)}, f32[1280,128]{1,0:T(8,128)S(1)}, u32[]{:S(2)}, u32[]{:S(2)}) collective-permute-start(f32[1280,128]{1,0:T(8,128)S(1)} %bitcast.8), channel_id=1, source_target_pairs={{0,1},{1,0},{2,3},{3,2},{4,5},{5,4},{6,7},{7,6},{8,9},{9,8},{10,11... | collective-permute-start | bytes 1966088 | tf_op jit(solution)/shard_map/ppermute | solution.py:559
  50.0 1.7 %collective-permute-done.8.other = f32[1280,128]{1,0:T(8,128)S(1)} collective-permute-done((f32[1280,128]{1,0:T(8,128)S(1)}, f32[1280,128]{1,0:T(8,128)S(1)}, u32[]{:S(2)}, u32[]{:S(2)}) %collective-permute-start.8) | collective-permute-done | bytes 655392 | tf_op jit(solution)/shard_map/ppermute | solution.py:559
  51.7 2.2 %shard_map.44 = f32[640,128]{1,0:T(8,128)} custom-call(f32[1280,128]{1,0:T(8,128)S(1)} %bitcast.9, f32[1280,128]{1,0:T(8,128)S(1)} %collective-permute-done.8.other), custom_call_target="tpu_custom_call" | custom-call | flops 4194304 | bytes 4194304 | tf_op jit(solution)/shard_map/pallas_call | solution.py:542
  53.8 3.8 %all-to-all-start.1 = ((f32[640,1,128]{2,1,0:T(1,128)}), f32[640,1,128]{2,1,0:T(1,128)S(1)}, u32[]{:S(2)}, u32[]{:S(2)}) async-start(f32[640,1,128]{2,1,0:T(1,128)} %bitcast.4), calls=%async_computation.1 | async-start | bytes 655360 | tf_op jit(solution)/shard_map/all_to_all | solution.py:568
  57.7 3.4 %collective-permute-done.7.over = f32[6,256,256]{2,1,0:T(8,128)} collective-permute-done((f32[6,256,256]{2,1,0:T(8,128)}, f32[6,256,256]{2,1,0:T(8,128)}, u32[]{:S(2)}, u32[]{:S(2)}) %collective-permute-start.7) | collective-permute-done | bytes 1572896 | tf_op jit(solution)/shard_map/ppermute | solution.py:564
  61.1 8.2 %all-to-all-done.1 = f32[640,1,128]{2,1,0:T(1,128)S(1)} async-done(((f32[640,1,128]{2,1,0:T(1,128)}), f32[640,1,128]{2,1,0:T(1,128)S(1)}, u32[]{:S(2)}, u32[]{:S(2)}) %all-to-all-start.1) | async-done | bytes 327712 | tf_op jit(solution)/shard_map/all_to_all | solution.py:568
  69.3 0.0 collective-permute-done.6.own
  69.3 0.0 copy-done.1
  69.3 6.8 %shard_map.45 = (f32[2,256,256]{2,1,0:T(8,128)}, f32[2,256,256]{2,1,0:T(8,128)}) custom-call(f32[2,256,256]{2,1,0:T(8,128)S(1)} %copy-done.1, f32[2,256,256]{2,1,0:T(8,128)S(1)} %collective-permute-done.bs, f32[2,256,256]{2,1,0:T(8,128)S(1)} %collective-permute-done.1.bx, f32[6,256,256]{2,1,0:T(8,128)} %collective-permute-done.6.own, ...), custom_call_target="tpu_custom_call" | custom-call | flops 8388608 | bytes 8388608 | tf_op jit(solution)/shard_map/pallas_call | solution.py:542
  (1 shorter events, 0.0 us)
Async XLA Ops:
  0.6 3.6 %collective-permute-start = (f32[2,256,256]{2,1,0:T(8,128)}, f32[2,256,256]{2,1,0:T(8,128)S(1)}, u32[]{:S(2)}, u32[]{:S(2)}) collective-permute-start(f32[2,256,256]{2,1,0:T(8,128)} %b.5), channel_id=1, source_target_pairs={{0,1},{1,0},{2,3},{3,2},{4,5},{5,4},{6,7},{7,6},{8,9},{9,8},{10,11... | collective-permute-start | bytes 1572872 | tf_op jit(solution)/shard_map/ppermute | solution.py:559
  2.1 8.1 %collective-permute-start.2 = (f32[2,256,256]{2,1,0:T(8,128)}, f32[2,256,256]{2,1,0:T(8,128)S(1)}, u32[]{:S(2)}, u32[]{:S(2)}) collective-permute-start(f32[2,256,256]{2,1,0:T(8,128)} %g.3), channel_id=1, source_target_pairs={{0,1},{1,0},{2,3},{3,2},{4,5},{5,4},{6,7},{7,6},{8,9},{9,8},{10,11... | collective-permute-start | bytes 1572872 | tf_op jit(solution)/shard_map/ppermute | solution.py:559
  2.2 9.1 %collective-permute-start.1 = (f32[2,256,256]{2,1,0:T(8,128)}, f32[2,256,256]{2,1,0:T(8,128)S(1)}, u32[]{:S(2)}, u32[]{:S(2)}) collective-permute-start(f32[2,256,256]{2,1,0:T(8,128)} %b.5), channel_id=1, source_target_pairs={{1,2},{3,4},{5,6},{7,8},{9,10},{11,12},{13,14},{15,16},{17,18},{19... | collective-permute-start | bytes 1572872 | tf_op jit(solution)/shard_map/ppermute | solution.py:564
  4.2 1.1 %copy-start = (f32[2,256,256]{2,1,0:T(8,128)S(1)}, f32[2,256,256]{2,1,0:T(8,128)}, u32[]{:S(2)}) copy-start(f32[2,256,256]{2,1,0:T(8,128)} %b.5) | copy-start | bytes 1572868
  5.3 1.0 %copy-start.2 = (f32[2,256,256]{2,1,0:T(8,128)S(1)}, f32[2,256,256]{2,1,0:T(8,128)}, u32[]{:S(2)}) copy-start(f32[2,256,256]{2,1,0:T(8,128)} %g.3) | copy-start | bytes 1572868
  6.8 15.3 %collective-permute-start.3 = (f32[2,256,256]{2,1,0:T(8,128)S(1)}, f32[2,256,256]{2,1,0:T(8,128)S(1)}, u32[]{:S(2)}, u32[]{:S(2)}) collective-permute-start(f32[2,256,256]{2,1,0:T(8,128)S(1)} %shard_map.41.sent), channel_id=1, source_target_pairs={{1,2},{3,4},{5,6},{7,8},{9,10},{11,12},{13,14},{15,16},{17,18},{19... | collective-permute-start | bytes 1572872 | tf_op jit(solution)/shard_map/ppermute | solution.py:564
  13.9 8.1 %collective-permute-start.4 = (f32[256,256]{1,0:T(8,128)S(1)}, f32[256,256]{1,0:T(8,128)S(1)}, u32[]{:S(2)}, u32[]{:S(2)}) collective-permute-start(f32[256,256]{1,0:T(8,128)S(1)} %get-tuple-element.7), channel_id=1, source_target_pairs={{0,1},{1,0},{2,3},{3,2},{4,5},{5,4},{6,7},{7,6},{8,9},{9,8},{10,11... | collective-permute-start | bytes 786440 | tf_op jit(solution)/shard_map/ppermute | solution.py:559
  23.9 13.1 %collective-permute-start.5 = (f32[6,256,256]{2,1,0:T(8,128)}, f32[6,256,256]{2,1,0:T(8,128)}, u32[]{:S(2)}, u32[]{:S(2)}) collective-permute-start(f32[6,256,256]{2,1,0:T(8,128)} %get-tuple-element.8), channel_id=1, source_target_pairs={{0,1},{1,0},{2,3},{3,2},{4,5},{5,4},{6,7},{7,6},{8,9},{9,8},{10,11... | collective-permute-start | bytes 4718600 | tf_op jit(solution)/shard_map/ppermute | solution.py:559
  24.4 44.9 %copy-start.1 = (f32[2,256,256]{2,1,0:T(8,128)S(1)}, f32[2,256,256]{2,1,0:T(8,128)}, u32[]{:S(2)}) copy-start(f32[2,256,256]{2,1,0:T(8,128)} %b.5) | copy-start | bytes 1572868
  24.4 23.9 %all-to-all-start = ((f32[1280,1,128]{2,1,0:T(1,128)}), f32[1280,1,128]{2,1,0:T(1,128)S(1)}, u32[]{:S(2)}, u32[]{:S(2)}) async-start(f32[1280,1,128]{2,1,0:T(1,128)} %bitcast.1), calls=%async_computation | async-start | bytes 1310720 | tf_op jit(solution)/shard_map/all_to_all | solution.py:568
  33.4 27.7 %collective-permute-start.7 = (f32[6,256,256]{2,1,0:T(8,128)}, f32[6,256,256]{2,1,0:T(8,128)}, u32[]{:S(2)}, u32[]{:S(2)}) collective-permute-start(f32[6,256,256]{2,1,0:T(8,128)} %get-tuple-element.8), channel_id=1, source_target_pairs={{1,2},{3,4},{5,6},{7,8},{9,10},{11,12},{13,14},{15,16},{17,18},{19... | collective-permute-start | bytes 4718600 | tf_op jit(solution)/shard_map/ppermute | solution.py:564
  37.0 32.3 %collective-permute-start.6 = (f32[6,256,256]{2,1,0:T(8,128)}, f32[6,256,256]{2,1,0:T(8,128)}, u32[]{:S(2)}, u32[]{:S(2)}) collective-permute-start(f32[6,256,256]{2,1,0:T(8,128)} %collective-permute-done.5.side), channel_id=1, source_target_pairs={{0,1},{1,0},{2,3},{3,2},{4,5},{5,4},{6,7},{7,6},{8,9},{9,8},{10,11... | collective-permute-start | bytes 4718600 | tf_op jit(solution)/shard_map/ppermute | solution.py:559
  48.3 3.4 %collective-permute-start.8 = (f32[1280,128]{1,0:T(8,128)S(1)}, f32[1280,128]{1,0:T(8,128)S(1)}, u32[]{:S(2)}, u32[]{:S(2)}) collective-permute-start(f32[1280,128]{1,0:T(8,128)S(1)} %bitcast.8), channel_id=1, source_target_pairs={{0,1},{1,0},{2,3},{3,2},{4,5},{5,4},{6,7},{7,6},{8,9},{9,8},{10,11... | collective-permute-start | bytes 1966088 | tf_op jit(solution)/shard_map/ppermute | solution.py:559
  53.8 15.5 %all-to-all-start.1 = ((f32[640,1,128]{2,1,0:T(1,128)}), f32[640,1,128]{2,1,0:T(1,128)S(1)}, u32[]{:S(2)}, u32[]{:S(2)}) async-start(f32[640,1,128]{2,1,0:T(1,128)} %bitcast.4), calls=%async_computation.1 | async-start | bytes 655360 | tf_op jit(solution)/shard_map/all_to_all | solution.py:568

commit v4 on v3

--- a/solution.py
+++ b/solution.py
@@ -414,9 +414,15 @@
     cpl[0:8, :] = jnp.zeros((8, NC), jnp.float32)
     cpl[planes + 8 : planes + 16, :] = jnp.zeros((8, NC), jnp.float32)
     cpl[8 : planes + 8, :] = total + lift
-    for k in range(5):
-        packed[pl.ds(k, planes, 5), :] = cpl[pl.ds(6 + k, planes), :]
-    Copies(sems).start(packed, pack).wait()
+    copies, leaving = Copies(sems), []
+    half = planes // 2
+    for part in range(2):
+        for k in range(5):
+            packed[pl.ds(part * half * 5 + k, half, 5), :] = cpl[pl.ds(6 + k + part * half, half), :]
+        piece = pl.ds(part * half * 5, half * 5)
+        leaving.append(copies.start(packed.at[piece], pack.at[piece]))
+    for copy in leaving:
+        copy.wait()
 
 
 def post_kernel(
@@ -592,7 +598,7 @@
         6 << 20,
         (bs, ANY), (bx, ANY), (state, VM), (sx, VM), (xi, VM),
     )
-    from_over = cross(side, False)
+    from_over = cross(side)
     from_side = swap(side)
     own = swap(from_side)
     got = everywhere(pack)
@@ -600,7 +606,7 @@
         coarse_kernel,
         [((5 * NC, NC), HBM)],
         [(total + 16, NC), (5 * NC, NC)],
-        1,
+        2,
         4 << 20,
         (got, VM), (swap(got), VM),
     )

time: 76.6 us -> 76.7 us (level)
  starting transfers between devices: 32.7 us -> 37 us
  waiting for transfers between devices: 26.8 us -> 22.6 us
    ppermute x6, starting transfers between devices: 10.8 us -> 16.8 us  [swap(): return lax.ppermute(v, AXES, inside)]
    all_to_all x2, waiting for transfers between devices: 19.4 us -> 16.1 us  [everywhere(): lax.all_to_all(v.reshape(rows, 1, NC), AXES, 0, 0, tiled=True)]
    ppermute x3, starting transfers between devices: 9.17 us -> 7.34 us  [cross(): return lax.ppermute(v, AXES, across if ends else between)]
    ppermute x3, waiting for transfers between devices: 4.49 us -> 3.63 us  [cross(): return lax.ppermute(v, AXES, across if ends else between)]
where the time goes in v4:
time: 76.7 us; the launch traced here: 76.3 us
  starting transfers between devices  37 us (48%)
  waiting for transfers between devices  22.6 us (29%)
  Pallas kernels  13.8 us (18%)
  local copies, waits for them, and re-layouts  2.12 us (3%)
  between operations  0.87 us (1%)
    ppermute x6, starting transfers between devices, swap(): return lax.ppermute(v, AXES, inside)  16.8 us
    all_to_all x2, waiting for transfers between devices, everywhere(): lax.all_to_all(v.reshape(rows, 1, NC), AXES, 0, 0, tiled=True)  16.1 us
    pallas_call x5, Pallas kernels, call(): pl.pallas_call(kernel, out_shape=[jax.ShapeDtypeStruct(s, jnp.float32) fo...  13.8 us
    all_to_all x2, starting transfers between devices, everywhere(): lax.all_to_all(v.reshape(rows, 1, NC), AXES, 0, 0, tiled=True)  12.8 us
    ppermute x3, starting transfers between devices, cross(): return lax.ppermute(v, AXES, across if ends else between)  7.34 us
    ppermute x3, waiting for transfers between devices, cross(): return lax.ppermute(v, AXES, across if ends else between)  3.63 us
    ppermute x6, waiting for transfers between devices, swap(): return lax.ppermute(v, AXES, inside)  2.9 us
    unnamed x6, local copies, waits for them, and re-layouts  2.12 us
  transfers between devices with their start and end apart: 11, of which 6 were waited for; matrix products, arithmetic and copies ran while one was open for 0% of the time, Pallas kernels for 7%

profile of v4, /device:TPU:1, one launch (start us, length us, event | category | flops | bytes accessed | tf_op | source)
XLA Modules:
  0.0 76.3 jit_solution(317956301036152602)
XLA Ops:
  0.6 1.5 %collective-permute-start = (f32[2,256,256]{2,1,0:T(8,128)}, f32[2,256,256]{2,1,0:T(8,128)S(1)}, u32[]{:S(2)}, u32[]{:S(2)}) collective-permute-start(f32[2,256,256]{2,1,0:T(8,128)} %b.5), channel_id=1, source_target_pairs={{0,1},{1,0},{2,3},{3,2},{4,5},{5,4},{6,7},{7,6},{8,9},{9,8},{10,11... | collective-permute-start | bytes 1572872 | tf_op jit(solution)/shard_map/ppermute | solution.py:565
  2.1 0.1 collective-permute-start.2
  2.2 2.0 %collective-permute-start.1 = (f32[2,256,256]{2,1,0:T(8,128)}, f32[2,256,256]{2,1,0:T(8,128)S(1)}, u32[]{:S(2)}, u32[]{:S(2)}) collective-permute-start(f32[2,256,256]{2,1,0:T(8,128)} %b.5), channel_id=1, source_target_pairs={{1,2},{3,4},{5,6},{7,8},{9,10},{11,12},{13,14},{15,16},{17,18},{19... | collective-permute-start | bytes 1572872 | tf_op jit(solution)/shard_map/ppermute | solution.py:570
  4.2 0.0 collective-permute-done.bs
  4.2 0.0 copy-start
  4.3 1.1 %copy-done = f32[2,256,256]{2,1,0:T(8,128)S(1)} copy-done((f32[2,256,256]{2,1,0:T(8,128)S(1)}, f32[2,256,256]{2,1,0:T(8,128)}, u32[]{:S(2)}) %copy-start) | copy-done | bytes 524312
  5.3 0.0 copy-start.2
  5.3 1.0 %copy-done.2 = f32[2,256,256]{2,1,0:T(8,128)S(1)} copy-done((f32[2,256,256]{2,1,0:T(8,128)S(1)}, f32[2,256,256]{2,1,0:T(8,128)}, u32[]{:S(2)}) %copy-start.2) | copy-done | bytes 524312
  6.4 0.4 shard_map.41.sent
  6.8 3.5 %collective-permute-start.3 = (f32[2,256,256]{2,1,0:T(8,128)S(1)}, f32[2,256,256]{2,1,0:T(8,128)S(1)}, u32[]{:S(2)}, u32[]{:S(2)}) collective-permute-start(f32[2,256,256]{2,1,0:T(8,128)S(1)} %shard_map.41.sent), channel_id=1, source_target_pairs={{1,2},{3,4},{5,6},{7,8},{9,10},{11,12},{13,14},{15,16},{17,18},{19... | collective-permute-start | bytes 1572872 | tf_op jit(solution)/shard_map/ppermute | solution.py:570
  10.3 0.0 collective-permute-done.2.gs
  10.3 1.0 %collective-permute-done.1.bx = f32[2,256,256]{2,1,0:T(8,128)S(1)} collective-permute-done((f32[2,256,256]{2,1,0:T(8,128)}, f32[2,256,256]{2,1,0:T(8,128)S(1)}, u32[]{:S(2)}, u32[]{:S(2)}) %collective-permute-start.1) | collective-permute-done | bytes 524320 | tf_op jit(solution)/shard_map/ppermute | solution.py:570
  11.3 2.6 %shard_map.42 = (f32[21,272,256]{2,1,0:T(8,128)S(1)}, f32[256,256]{1,0:T(8,128)S(1)}) custom-call(f32[2,256,256]{2,1,0:T(8,128)S(1)} %copy-done.2, f32[2,256,256]{2,1,0:T(8,128)S(1)} %collective-permute-done.2.gs, f32[2,256,256]{2,1,0:T(8,128)S(1)} %copy-done, f32[2,256,256]{2,1,0:T(8,128)S(1)} %collective-permute-done.bs, ...), custom_call_target="tpu_custom_call" | custom-call | flops 6291456 | bytes 6291456 | tf_op jit(solution)/shard_map/pallas_call | solution.py:548
  13.9 7.0 %collective-permute-start.4 = (f32[256,256]{1,0:T(8,128)S(1)}, f32[256,256]{1,0:T(8,128)S(1)}, u32[]{:S(2)}, u32[]{:S(2)}) collective-permute-start(f32[256,256]{1,0:T(8,128)S(1)} %get-tuple-element.7), channel_id=1, source_target_pairs={{0,1},{1,0},{2,3},{3,2},{4,5},{5,4},{6,7},{7,6},{8,9},{9,8},{10,11... | collective-permute-start | bytes 786440 | tf_op jit(solution)/shard_map/ppermute | solution.py:565
  20.9 1.2 %collective-permute-done.4.xi = f32[256,256]{1,0:T(8,128)S(1)} collective-permute-done((f32[256,256]{1,0:T(8,128)S(1)}, f32[256,256]{1,0:T(8,128)S(1)}, u32[]{:S(2)}, u32[]{:S(2)}) %collective-permute-start.4) | collective-permute-done | bytes 262176 | tf_op jit(solution)/shard_map/ppermute | solution.py:565
  22.0 0.0 collective-permute-done.3.sx
  22.0 1.9 %shard_map.43 = (f32[1280,128]{1,0:T(8,128)}, f32[6,256,256]{2,1,0:T(8,128)}) custom-call(f32[2,256,256]{2,1,0:T(8,128)S(1)} %collective-permute-done.bs, f32[2,256,256]{2,1,0:T(8,128)S(1)} %collective-permute-done.1.bx, f32[21,272,256]{2,1,0:T(8,128)S(1)} %get-tuple-element.6.state, f32[2,256,256]{2,1,0:T(8,128)S(1)} %collective-permute-done.3.sx, ...), custom_call_target="tpu_custom_call" | custom-call | flops 6291456 | bytes 6291456 | tf_op jit(solution)/shard_map/pallas_call | solution.py:548
  23.9 0.5 collective-permute-start.5
  24.4 9.0 %all-to-all-start = ((f32[1280,1,128]{2,1,0:T(1,128)}), f32[1280,1,128]{2,1,0:T(1,128)S(1)}, u32[]{:S(2)}, u32[]{:S(2)}) async-start(f32[1280,1,128]{2,1,0:T(1,128)} %bitcast.1), calls=%async_computation | async-start | bytes 1310720 | tf_op jit(solution)/shard_map/all_to_all | solution.py:574
  33.4 1.8 %collective-permute-start.7 = (f32[6,256,256]{2,1,0:T(8,128)}, f32[6,256,256]{2,1,0:T(8,128)}, u32[]{:S(2)}, u32[]{:S(2)}) collective-permute-start(f32[6,256,256]{2,1,0:T(8,128)} %get-tuple-element.8), channel_id=1, source_target_pairs={{1,2},{3,4},{5,6},{7,8},{9,10},{11,12},{13,14},{15,16},{17,18},{19... | collective-permute-start | bytes 4718600 | tf_op jit(solution)/shard_map/ppermute | solution.py:570
  35.2 0.0 collective-permute-done.5.side
  35.2 6.4 %collective-permute-start.6 = (f32[6,256,256]{2,1,0:T(8,128)}, f32[6,256,256]{2,1,0:T(8,128)}, u32[]{:S(2)}, u32[]{:S(2)}) collective-permute-start(f32[6,256,256]{2,1,0:T(8,128)} %collective-permute-done.5.side), channel_id=1, source_target_pairs={{0,1},{1,0},{2,3},{3,2},{4,5},{5,4},{6,7},{7,6},{8,9},{9,8},{10,11... | collective-permute-start | bytes 4718600 | tf_op jit(solution)/shard_map/ppermute | solution.py:565
  41.6 7.0 %all-to-all-done = f32[1280,1,128]{2,1,0:T(1,128)S(1)} async-done(((f32[1280,1,128]{2,1,0:T(1,128)}), f32[1280,1,128]{2,1,0:T(1,128)S(1)}, u32[]{:S(2)}, u32[]{:S(2)}) %all-to-all-start) | async-done | bytes 655392 | tf_op jit(solution)/shard_map/all_to_all | solution.py:574
  48.6 1.4 %collective-permute-start.8 = (f32[1280,128]{1,0:T(8,128)S(1)}, f32[1280,128]{1,0:T(8,128)S(1)}, u32[]{:S(2)}, u32[]{:S(2)}) collective-permute-start(f32[1280,128]{1,0:T(8,128)S(1)} %bitcast.8), channel_id=1, source_target_pairs={{0,1},{1,0},{2,3},{3,2},{4,5},{5,4},{6,7},{7,6},{8,9},{9,8},{10,11... | collective-permute-start | bytes 1966088 | tf_op jit(solution)/shard_map/ppermute | solution.py:565
  50.0 1.7 %collective-permute-done.8.other = f32[1280,128]{1,0:T(8,128)S(1)} collective-permute-done((f32[1280,128]{1,0:T(8,128)S(1)}, f32[1280,128]{1,0:T(8,128)S(1)}, u32[]{:S(2)}, u32[]{:S(2)}) %collective-permute-start.8) | collective-permute-done | bytes 655392 | tf_op jit(solution)/shard_map/ppermute | solution.py:565
  51.7 2.2 %shard_map.44 = f32[640,128]{1,0:T(8,128)} custom-call(f32[1280,128]{1,0:T(8,128)S(1)} %bitcast.9, f32[1280,128]{1,0:T(8,128)S(1)} %collective-permute-done.8.other), custom_call_target="tpu_custom_call" | custom-call | flops 4194304 | bytes 4194304 | tf_op jit(solution)/shard_map/pallas_call | solution.py:548
  53.9 3.8 %all-to-all-start.1 = ((f32[640,1,128]{2,1,0:T(1,128)}), f32[640,1,128]{2,1,0:T(1,128)S(1)}, u32[]{:S(2)}, u32[]{:S(2)}) async-start(f32[640,1,128]{2,1,0:T(1,128)} %bitcast.4), calls=%async_computation.1 | async-start | bytes 655360 | tf_op jit(solution)/shard_map/all_to_all | solution.py:574
  57.7 2.6 %collective-permute-done.7.over = f32[6,256,256]{2,1,0:T(8,128)} collective-permute-done((f32[6,256,256]{2,1,0:T(8,128)}, f32[6,256,256]{2,1,0:T(8,128)}, u32[]{:S(2)}, u32[]{:S(2)}) %collective-permute-start.7) | collective-permute-done | bytes 1572896 | tf_op jit(solution)/shard_map/ppermute | solution.py:570
  60.3 9.1 %all-to-all-done.1 = f32[640,1,128]{2,1,0:T(1,128)S(1)} async-done(((f32[640,1,128]{2,1,0:T(1,128)}), f32[640,1,128]{2,1,0:T(1,128)S(1)}, u32[]{:S(2)}, u32[]{:S(2)}) %all-to-all-start.1) | async-done | bytes 327712 | tf_op jit(solution)/shard_map/all_to_all | solution.py:574
  69.4 0.0 collective-permute-done.6.own
  69.4 0.0 copy-done.1
  69.4 6.8 %shard_map.45 = (f32[2,256,256]{2,1,0:T(8,128)}, f32[2,256,256]{2,1,0:T(8,128)}) custom-call(f32[2,256,256]{2,1,0:T(8,128)S(1)} %copy-done.1, f32[2,256,256]{2,1,0:T(8,128)S(1)} %collective-permute-done.bs, f32[2,256,256]{2,1,0:T(8,128)S(1)} %collective-permute-done.1.bx, f32[6,256,256]{2,1,0:T(8,128)} %collective-permute-done.6.own, ...), custom_call_target="tpu_custom_call" | custom-call | flops 8388608 | bytes 8388608 | tf_op jit(solution)/shard_map/pallas_call | solution.py:548
  (1 shorter events, 0.0 us)
Async XLA Ops:
  0.6 3.6 %collective-permute-start = (f32[2,256,256]{2,1,0:T(8,128)}, f32[2,256,256]{2,1,0:T(8,128)S(1)}, u32[]{:S(2)}, u32[]{:S(2)}) collective-permute-start(f32[2,256,256]{2,1,0:T(8,128)} %b.5), channel_id=1, source_target_pairs={{0,1},{1,0},{2,3},{3,2},{4,5},{5,4},{6,7},{7,6},{8,9},{9,8},{10,11... | collective-permute-start | bytes 1572872 | tf_op jit(solution)/shard_map/ppermute | solution.py:565
  2.1 8.1 %collective-permute-start.2 = (f32[2,256,256]{2,1,0:T(8,128)}, f32[2,256,256]{2,1,0:T(8,128)S(1)}, u32[]{:S(2)}, u32[]{:S(2)}) collective-permute-start(f32[2,256,256]{2,1,0:T(8,128)} %g.3), channel_id=1, source_target_pairs={{0,1},{1,0},{2,3},{3,2},{4,5},{5,4},{6,7},{7,6},{8,9},{9,8},{10,11... | collective-permute-start | bytes 1572872 | tf_op jit(solution)/shard_map/ppermute | solution.py:565
  2.2 9.1 %collective-permute-start.1 = (f32[2,256,256]{2,1,0:T(8,128)}, f32[2,256,256]{2,1,0:T(8,128)S(1)}, u32[]{:S(2)}, u32[]{:S(2)}) collective-permute-start(f32[2,256,256]{2,1,0:T(8,128)} %b.5), channel_id=1, source_target_pairs={{1,2},{3,4},{5,6},{7,8},{9,10},{11,12},{13,14},{15,16},{17,18},{19... | collective-permute-start | bytes 1572872 | tf_op jit(solution)/shard_map/ppermute | solution.py:570
  4.2 1.1 %copy-start = (f32[2,256,256]{2,1,0:T(8,128)S(1)}, f32[2,256,256]{2,1,0:T(8,128)}, u32[]{:S(2)}) copy-start(f32[2,256,256]{2,1,0:T(8,128)} %b.5) | copy-start | bytes 1572868
  5.3 1.0 %copy-start.2 = (f32[2,256,256]{2,1,0:T(8,128)S(1)}, f32[2,256,256]{2,1,0:T(8,128)}, u32[]{:S(2)}) copy-start(f32[2,256,256]{2,1,0:T(8,128)} %g.3) | copy-start | bytes 1572868
  6.8 15.3 %collective-permute-start.3 = (f32[2,256,256]{2,1,0:T(8,128)S(1)}, f32[2,256,256]{2,1,0:T(8,128)S(1)}, u32[]{:S(2)}, u32[]{:S(2)}) collective-permute-start(f32[2,256,256]{2,1,0:T(8,128)S(1)} %shard_map.41.sent), channel_id=1, source_target_pairs={{1,2},{3,4},{5,6},{7,8},{9,10},{11,12},{13,14},{15,16},{17,18},{19... | collective-permute-start | bytes 1572872 | tf_op jit(solution)/shard_map/ppermute | solution.py:570
  13.9 8.1 %collective-permute-start.4 = (f32[256,256]{1,0:T(8,128)S(1)}, f32[256,256]{1,0:T(8,128)S(1)}, u32[]{:S(2)}, u32[]{:S(2)}) collective-permute-start(f32[256,256]{1,0:T(8,128)S(1)} %get-tuple-element.7), channel_id=1, source_target_pairs={{0,1},{1,0},{2,3},{3,2},{4,5},{5,4},{6,7},{7,6},{8,9},{9,8},{10,11... | collective-permute-start | bytes 786440 | tf_op jit(solution)/shard_map/ppermute | solution.py:565
  23.9 11.3 %collective-permute-start.5 = (f32[6,256,256]{2,1,0:T(8,128)}, f32[6,256,256]{2,1,0:T(8,128)}, u32[]{:S(2)}, u32[]{:S(2)}) collective-permute-start(f32[6,256,256]{2,1,0:T(8,128)} %get-tuple-element.8), channel_id=1, source_target_pairs={{0,1},{1,0},{2,3},{3,2},{4,5},{5,4},{6,7},{7,6},{8,9},{9,8},{10,11... | collective-permute-start | bytes 4718600 | tf_op jit(solution)/shard_map/ppermute | solution.py:565
  24.4 45.0 %copy-start.1 = (f32[2,256,256]{2,1,0:T(8,128)S(1)}, f32[2,256,256]{2,1,0:T(8,128)}, u32[]{:S(2)}) copy-start(f32[2,256,256]{2,1,0:T(8,128)} %b.5) | copy-start | bytes 1572868
  24.4 24.2 %all-to-all-start = ((f32[1280,1,128]{2,1,0:T(1,128)}), f32[1280,1,128]{2,1,0:T(1,128)S(1)}, u32[]{:S(2)}, u32[]{:S(2)}) async-start(f32[1280,1,128]{2,1,0:T(1,128)} %bitcast.1), calls=%async_computation | async-start | bytes 1310720 | tf_op jit(solution)/shard_map/all_to_all | solution.py:574
  33.4 26.9 %collective-permute-start.7 = (f32[6,256,256]{2,1,0:T(8,128)}, f32[6,256,256]{2,1,0:T(8,128)}, u32[]{:S(2)}, u32[]{:S(2)}) collective-permute-start(f32[6,256,256]{2,1,0:T(8,128)} %get-tuple-element.8), channel_id=1, source_target_pairs={{1,2},{3,4},{5,6},{7,8},{9,10},{11,12},{13,14},{15,16},{17,18},{19... | collective-permute-start | bytes 4718600 | tf_op jit(solution)/shard_map/ppermute | solution.py:570
  35.2 34.2 %collective-permute-start.6 = (f32[6,256,256]{2,1,0:T(8,128)}, f32[6,256,256]{2,1,0:T(8,128)}, u32[]{:S(2)}, u32[]{:S(2)}) collective-permute-start(f32[6,256,256]{2,1,0:T(8,128)} %collective-permute-done.5.side), channel_id=1, source_target_pairs={{0,1},{1,0},{2,3},{3,2},{4,5},{5,4},{6,7},{7,6},{8,9},{9,8},{10,11... | collective-permute-start | bytes 4718600 | tf_op jit(solution)/shard_map/ppermute | solution.py:565
  48.6 3.2 %collective-permute-start.8 = (f32[1280,128]{1,0:T(8,128)S(1)}, f32[1280,128]{1,0:T(8,128)S(1)}, u32[]{:S(2)}, u32[]{:S(2)}) collective-permute-start(f32[1280,128]{1,0:T(8,128)S(1)} %bitcast.8), channel_id=1, source_target_pairs={{0,1},{1,0},{2,3},{3,2},{4,5},{5,4},{6,7},{7,6},{8,9},{9,8},{10,11... | collective-permute-start | bytes 1966088 | tf_op jit(solution)/shard_map/ppermute | solution.py:565
  53.9 15.5 %all-to-all-start.1 = ((f32[640,1,128]{2,1,0:T(1,128)}), f32[640,1,128]{2,1,0:T(1,128)S(1)}, u32[]{:S(2)}, u32[]{:S(2)}) async-start(f32[640,1,128]{2,1,0:T(1,128)} %bitcast.4), calls=%async_computation.1 | async-start | bytes 655360 | tf_op jit(solution)/shard_map/all_to_all | solution.py:574

commit v5 on v3

--- a/solution.py
+++ b/solution.py
@@ -358,58 +358,94 @@
         copy.wait()
 
 
-def coarse_kernel(recv, other, pack, cpl, packed, sems):
-    index, par, _ = position()
-    rows = 2 * HELD
-    planes = recv.shape[0] // rows
-    plane_at = lax.broadcasted_iota(jnp.int32, (planes, NC), 0)
-    lane = lane_iota((planes, NC))
-
-    def up(v):
-        return pltpu.roll(v, planes - 1, 0)
-
-    def down(v):
+class CoarseRows:
+    def __init__(self, planes):
+        self.index, self.par, _ = position()
+        self.planes = planes
+        self.plane_at = lax.broadcasted_iota(jnp.int32, (planes, NC), 0)
+        self.lane = lane_iota((planes, NC))
+        self.fr, self.fz, self.fy, self.dg, self.iv = {}, {}, {}, {}, {}
+
+    def load(self, ref, field, n, own):
+        at_n = jnp.where(self.par == 0, 4 - n, n) if own else jnp.where(self.par == 0, -n - 1, 5 + n)
+        return ref[pl.ds(field * HELD + at_n, self.planes, 2 * HELD), :]
+
+    def up(self, v):
+        return pltpu.roll(v, self.planes - 1, 0)
+
+    def down(self, v):
         return pltpu.roll(v, 1, 0)
 
-    def row_of(field, n):
-        if n >= 0:
-            return recv[pl.ds(field * HELD + jnp.where(par == 0, 4 - n, n), planes, rows), :]
-        return other[pl.ds(field * HELD + jnp.where(par == 0, -n - 1, 5 + n), planes, rows), :]
-
-    u1 = {j: row_of(0, j) for j in range(-4, 5)}
-    bc = {j: row_of(1, j) for j in range(-4, 5)}
-    fr = {j: 0.125 * (bc[j] + bc[j + 1]) for j in range(-4, 4)}
-    fz, fy, dg, iv = {}, {}, {}, {}
-    for j in range(-3, 4):
-        zn = jnp.where(plane_at == planes - 1, 0.0, up(bc[j]))
-        zp = jnp.where(plane_at == 0, 0.0, down(bc[j]))
-        yn = jnp.where(lane == NC - 1, 0.0, left(bc[j]))
-        yp = jnp.where(lane == 0, 0.0, right(bc[j]))
-        fz[j] = jnp.where(plane_at == planes - 1, 0.0, 0.125 * (bc[j] + zn))
-        fy[j] = jnp.where(lane == NC - 1, 0.0, 0.125 * (bc[j] + yn))
-        dg[j] = 0.75 * bc[j] + 0.125 * (zn + zp + yn + yp + bc[j - 1] + bc[j + 1])
-        row = index + jnp.where(par == 0, -j, j)
+    def prepare(self, bc, j):
+        last, end = self.plane_at == self.planes - 1, self.lane == NC - 1
+        zn = jnp.where(last, 0.0, self.up(bc[j]))
+        zp = jnp.where(self.plane_at == 0, 0.0, self.down(bc[j]))
+        yn = jnp.where(end, 0.0, left(bc[j]))
+        yp = jnp.where(self.lane == 0, 0.0, right(bc[j]))
+        self.fz[j] = jnp.where(last, 0.0, 0.125 * (bc[j] + zn))
+        self.fy[j] = jnp.where(end, 0.0, 0.125 * (bc[j] + yn))
+        self.dg[j] = 0.75 * bc[j] + 0.125 * (zn + zp + yn + yp + bc[j - 1] + bc[j + 1])
+        row = self.index + jnp.where(self.par == 0, -j, j)
         inside = (row >= 0) & (row < NC)
-        iv[j] = jnp.where(inside, 1.0 / jnp.where(inside, dg[j], 1.0), 0.0)
-
-    def off(v, j):
-        total = fr[j] * v[j + 1] + fr[j - 1] * v[j - 1]
-        total = total + fz[j] * up(v[j]) + down(fz[j] * v[j])
-        return total + fy[j] * left(v[j]) + right(fy[j] * v[j])
-
+        self.iv[j] = jnp.where(inside, 1.0 / jnp.where(inside, self.dg[j], 1.0), 0.0)
+
+    def off(self, v, j):
+        total = self.fr[j] * v[j + 1] + self.fr[j - 1] * v[j - 1]
+        total = total + self.fz[j] * self.up(v[j]) + self.down(self.fz[j] * v[j])
+        return total + self.fy[j] * left(v[j]) + right(self.fy[j] * v[j])
+
+
+HANDED = 12
+
+
+def coarse_first_kernel(recv, handed):
+    m = CoarseRows(recv.shape[0] // (2 * HELD))
+    u1 = {j: m.load(recv, 0, j, True) for j in range(5)}
+    bc = {j: m.load(recv, 1, j, True) for j in range(5)}
+    m.fr = {j: 0.125 * (bc[j] + bc[j + 1]) for j in range(4)}
+    for j in (1, 2, 3):
+        m.prepare(bc, j)
+    (a1, b1), (a2, b2) = COARSE[:2]
+    res = {j: (CENTER - 1.0) * m.dg[j] * u1[j] + m.off(u1, j) for j in (1, 2, 3)}
+    step = {j: a1 * u1[j] + b1 * m.iv[j] * res[j] for j in (1, 2, 3)}
+    second = res[2] - m.dg[2] * step[2] + m.off(step, 2)
+    later = a2 * step[2] + b2 * m.iv[2] * second
+    found = (m.fr[0], m.fr[1], m.fz[1], m.fy[1], m.dg[1], m.iv[1], res[1], step[1], step[2], later, u1[1], bc[1])
+    for k, value in enumerate(found):
+        handed[k] = value
+
+
+def coarse_kernel(recv, other, handed, pack, cpl, packed, sems):
+    planes = recv.shape[0] // (2 * HELD)
+    m = CoarseRows(planes)
+    u1 = {j: m.load(other, 0, j, False) for j in range(-4, 0)}
+    bc = {j: m.load(other, 1, j, False) for j in range(-4, 0)}
+    u1[0], bc[0] = m.load(recv, 0, 0, True), m.load(recv, 1, 0, True)
+    m.fr = {j: 0.125 * (bc[j] + bc[j + 1]) for j in range(-4, 0)}
+    m.fr[0], m.fr[1], m.fz[1], m.fy[1], m.dg[1], m.iv[1], near, second1, second2, third2, u1[1], bc[1] = (
+        handed[k] for k in range(HANDED)
+    )
+    for j in range(-3, 1):
+        m.prepare(bc, j)
     reach = 3
-    res = {j: (CENTER - 1.0) * dg[j] * u1[j] + off(u1, j) for j in range(-reach, reach + 1)}
+    res = {j: (CENTER - 1.0) * m.dg[j] * u1[j] + m.off(u1, j) for j in range(-reach, 1)}
+    res[1] = near
     step = u1
     total = u1[0]
-    for k, (step_a, step_b) in enumerate(COARSE):
-        step = {j: step_a * step[j] + step_b * iv[j] * res[j] for j in range(-reach, reach + 1)}
+    known = ({1: second1, 2: second2}, {2: third2}, {})
+    for (step_a, step_b), there in zip(COARSE, known, strict=True):
+        moved_by = dict(there)
+        for j in range(-reach, min(reach, 1) + 1):
+            if j not in moved_by:
+                moved_by[j] = step_a * step[j] + step_b * m.iv[j] * res[j]
+        step = moved_by
         total = total + step[0]
         reach -= 1
-        res = {j: res[j] - dg[j] * step[j] + off(step, j) for j in range(-reach, reach + 1)}
+        res = {j: res[j] - m.dg[j] * step[j] + m.off(step, j) for j in range(-reach, min(reach, 1) + 1)}
     groups = lax.axis_size("grp")
     each = planes // groups
     column = jnp.sum(res[0].reshape(groups, each, NC), axis=1, keepdims=True)
-    weight = jnp.sum(dg[0].reshape(groups, each, NC), axis=1, keepdims=True)
+    weight = jnp.sum(m.dg[0].reshape(groups, each, NC), axis=1, keepdims=True)
     lift = jnp.broadcast_to(column / weight, (groups, each, NC)).reshape(planes, NC)
     cpl[0:8, :] = jnp.zeros((8, NC), jnp.float32)
     cpl[planes + 8 : planes + 16, :] = jnp.zeros((8, NC), jnp.float32)
@@ -544,7 +580,7 @@
         out_shape=[jax.ShapeDtypeStruct(s, jnp.float32) for s, _ in outs],
         in_specs=[spec for _, spec in operands],
         out_specs=[spec for _, spec in outs],
-        scratch_shapes=[pltpu.VMEM(s, jnp.float32) for s in scratch] + [pltpu.SemaphoreType.DMA((sems,))],
+        scratch_shapes=[pltpu.VMEM(s, jnp.float32) for s in scratch] + [pltpu.SemaphoreType.DMA((sems,))] * (sems > 0),
         compiler_params=pltpu.CompilerParams(vmem_limit_bytes=limit * 1024 * 1024),
         cost_estimate=pl.CostEstimate(flops=cost, bytes_accessed=cost, transcendentals=0),
     )(*(array for array, _ in operands))
@@ -596,13 +632,14 @@
     from_side = swap(side)
     own = swap(from_side)
     got = everywhere(pack)
+    (handed,) = call(coarse_first_kernel, [((HANDED, total, NC), VM)], [], 0, 2 << 20, (got, VM))
     (back,) = call(
         coarse_kernel,
         [((5 * NC, NC), HBM)],
         [(total + 16, NC), (5 * NC, NC)],
         1,
         4 << 20,
-        (got, VM), (swap(got), VM),
+        (got, VM), (swap(got), VM), (handed, VM),
     )
     w = everywhere(back)
     x5, r5 = call(

time: 76.6 us -> 76.2 us (level)
    pallas_call x5 -> x6, Pallas kernels: 13.8 us -> 13.8 us  [call(): pl.pallas_call(kernel, out_shape=[jax.ShapeDtypeStruct(s, jnp.float32) fo...]
where the time goes in v5:
time: 76.2 us; the launch traced here: 75.8 us
  starting transfers between devices  32.7 us (43%)
  waiting for transfers between devices  26.3 us (35%)
  Pallas kernels  13.8 us (18%)
  local copies, waits for them, and re-layouts  2.12 us (3%)
  between operations  0.9 us (1%)
    all_to_all x2, waiting for transfers between devices, everywhere(): lax.all_to_all(v.reshape(rows, 1, NC), AXES, 0, 0, tiled=True)  18.8 us
    pallas_call x6, Pallas kernels, call(): pl.pallas_call(kernel, out_shape=[jax.ShapeDtypeStruct(s, jnp.float32) fo...  13.8 us
    all_to_all x2, starting transfers between devices, everywhere(): lax.all_to_all(v.reshape(rows, 1, NC), AXES, 0, 0, tiled=True)  12.8 us
    ppermute x6, starting transfers between devices, swap(): return lax.ppermute(v, AXES, inside)  10.8 us
    ppermute x3, starting transfers between devices, cross(): return lax.ppermute(v, AXES, across if ends else between)  9.17 us
    ppermute x3, waiting for transfers between devices, cross(): return lax.ppermute(v, AXES, across if ends else between)  5.1 us
    ppermute x6, waiting for transfers between devices, swap(): return lax.ppermute(v, AXES, inside)  2.44 us
    unnamed x6, local copies, waits for them, and re-layouts  2.12 us
  transfers between devices with their start and end apart: 11, of which 6 were waited for; matrix products, arithmetic and copies ran while one was open for 0% of the time, Pallas kernels for 7%

profile of v5, /device:TPU:1, one launch (start us, length us, event | category | flops | bytes accessed | tf_op | source)
XLA Modules:
  0.0 75.8 jit_solution(13615475591408887115)
XLA Ops:
  0.6 1.5 %collective-permute-start = (f32[2,256,256]{2,1,0:T(8,128)}, f32[2,256,256]{2,1,0:T(8,128)S(1)}, u32[]{:S(2)}, u32[]{:S(2)}) collective-permute-start(f32[2,256,256]{2,1,0:T(8,128)} %b.5), channel_id=1, source_target_pairs={{0,1},{1,0},{2,3},{3,2},{4,5},{5,4},{6,7},{7,6},{8,9},{9,8},{10,11... | collective-permute-start | bytes 1572872 | tf_op jit(solution)/shard_map/ppermute | solution.py:595
  2.1 0.1 collective-permute-start.2
  2.2 2.0 %collective-permute-start.1 = (f32[2,256,256]{2,1,0:T(8,128)}, f32[2,256,256]{2,1,0:T(8,128)S(1)}, u32[]{:S(2)}, u32[]{:S(2)}) collective-permute-start(f32[2,256,256]{2,1,0:T(8,128)} %b.5), channel_id=1, source_target_pairs={{1,2},{3,4},{5,6},{7,8},{9,10},{11,12},{13,14},{15,16},{17,18},{19... | collective-permute-start | bytes 1572872 | tf_op jit(solution)/shard_map/ppermute | solution.py:600
  4.2 0.0 collective-permute-done.bs
  4.3 1.1 %copy-done = f32[2,256,256]{2,1,0:T(8,128)S(1)} copy-done((f32[2,256,256]{2,1,0:T(8,128)S(1)}, f32[2,256,256]{2,1,0:T(8,128)}, u32[]{:S(2)}) %copy-start) | copy-done | bytes 524312
  5.3 1.0 %copy-done.2 = f32[2,256,256]{2,1,0:T(8,128)S(1)} copy-done((f32[2,256,256]{2,1,0:T(8,128)S(1)}, f32[2,256,256]{2,1,0:T(8,128)}, u32[]{:S(2)}) %copy-start.2) | copy-done | bytes 524312
  6.4 0.4 shard_map.41.sent
  6.8 3.5 %collective-permute-start.3 = (f32[2,256,256]{2,1,0:T(8,128)S(1)}, f32[2,256,256]{2,1,0:T(8,128)S(1)}, u32[]{:S(2)}, u32[]{:S(2)}) collective-permute-start(f32[2,256,256]{2,1,0:T(8,128)S(1)} %shard_map.41.sent), channel_id=1, source_target_pairs={{1,2},{3,4},{5,6},{7,8},{9,10},{11,12},{13,14},{15,16},{17,18},{19... | collective-permute-start | bytes 1572872 | tf_op jit(solution)/shard_map/ppermute | solution.py:600
  10.3 0.0 collective-permute-done.2.gs
  10.3 1.0 %collective-permute-done.1.bx = f32[2,256,256]{2,1,0:T(8,128)S(1)} collective-permute-done((f32[2,256,256]{2,1,0:T(8,128)}, f32[2,256,256]{2,1,0:T(8,128)S(1)}, u32[]{:S(2)}, u32[]{:S(2)}) %collective-permute-start.1) | collective-permute-done | bytes 524320 | tf_op jit(solution)/shard_map/ppermute | solution.py:600
  11.3 2.6 %shard_map.42 = (f32[21,272,256]{2,1,0:T(8,128)S(1)}, f32[256,256]{1,0:T(8,128)S(1)}) custom-call(f32[2,256,256]{2,1,0:T(8,128)S(1)} %copy-done.2, f32[2,256,256]{2,1,0:T(8,128)S(1)} %collective-permute-done.2.gs, f32[2,256,256]{2,1,0:T(8,128)S(1)} %copy-done, f32[2,256,256]{2,1,0:T(8,128)S(1)} %collective-permute-done.bs, ...), custom_call_target="tpu_custom_call" | custom-call | flops 6291456 | bytes 6291456 | tf_op jit(solution)/shard_map/pallas_call | solution.py:578
  13.9 7.0 %collective-permute-start.4 = (f32[256,256]{1,0:T(8,128)S(1)}, f32[256,256]{1,0:T(8,128)S(1)}, u32[]{:S(2)}, u32[]{:S(2)}) collective-permute-start(f32[256,256]{1,0:T(8,128)S(1)} %get-tuple-element.7), channel_id=1, source_target_pairs={{0,1},{1,0},{2,3},{3,2},{4,5},{5,4},{6,7},{7,6},{8,9},{9,8},{10,11... | collective-permute-start | bytes 786440 | tf_op jit(solution)/shard_map/ppermute | solution.py:595
  20.9 1.2 %collective-permute-done.4.xi = f32[256,256]{1,0:T(8,128)S(1)} collective-permute-done((f32[256,256]{1,0:T(8,128)S(1)}, f32[256,256]{1,0:T(8,128)S(1)}, u32[]{:S(2)}, u32[]{:S(2)}) %collective-permute-start.4) | collective-permute-done | bytes 262176 | tf_op jit(solution)/shard_map/ppermute | solution.py:595
  22.0 0.0 collective-permute-done.3.sx
  22.0 1.9 %shard_map.43 = (f32[1280,128]{1,0:T(8,128)}, f32[6,256,256]{2,1,0:T(8,128)}) custom-call(f32[2,256,256]{2,1,0:T(8,128)S(1)} %collective-permute-done.bs, f32[2,256,256]{2,1,0:T(8,128)S(1)} %collective-permute-done.1.bx, f32[21,272,256]{2,1,0:T(8,128)S(1)} %get-tuple-element.6.state, f32[2,256,256]{2,1,0:T(8,128)S(1)} %collective-permute-done.3.sx, ...), custom_call_target="tpu_custom_call" | custom-call | flops 6291456 | bytes 6291456 | tf_op jit(solution)/shard_map/pallas_call | solution.py:578
  23.9 0.5 collective-permute-start.5
  24.4 9.0 %all-to-all-start = ((f32[1280,1,128]{2,1,0:T(1,128)}), f32[1280,1,128]{2,1,0:T(1,128)S(1)}, u32[]{:S(2)}, u32[]{:S(2)}) async-start(f32[1280,1,128]{2,1,0:T(1,128)} %bitcast.1), calls=%async_computation | async-start | bytes 1310720 | tf_op jit(solution)/shard_map/all_to_all | solution.py:604
  33.4 3.7 %collective-permute-start.7 = (f32[6,256,256]{2,1,0:T(8,128)}, f32[6,256,256]{2,1,0:T(8,128)}, u32[]{:S(2)}, u32[]{:S(2)}) collective-permute-start(f32[6,256,256]{2,1,0:T(8,128)} %get-tuple-element.8), channel_id=1, source_target_pairs={{1,2},{3,4},{5,6},{7,8},{9,10},{11,12},{13,14},{15,16},{17,18},{19... | collective-permute-start | bytes 4718600 | tf_op jit(solution)/shard_map/ppermute | solution.py:600
  37.0 0.0 collective-permute-done.5.side
  37.0 0.1 collective-permute-start.6
  37.1 11.2 %all-to-all-done = f32[1280,1,128]{2,1,0:T(1,128)S(1)} async-done(((f32[1280,1,128]{2,1,0:T(1,128)}), f32[1280,1,128]{2,1,0:T(1,128)S(1)}, u32[]{:S(2)}, u32[]{:S(2)}) %all-to-all-start) | async-done | bytes 655392 | tf_op jit(solution)/shard_map/all_to_all | solution.py:604
  48.3 1.6 %collective-permute-start.8 = (f32[1280,128]{1,0:T(8,128)S(1)}, f32[1280,128]{1,0:T(8,128)S(1)}, u32[]{:S(2)}, u32[]{:S(2)}) collective-permute-start(f32[1280,128]{1,0:T(8,128)S(1)} %bitcast.8), channel_id=1, source_target_pairs={{0,1},{1,0},{2,3},{3,2},{4,5},{5,4},{6,7},{7,6},{8,9},{9,8},{10,11... | collective-permute-start | bytes 1966088 | tf_op jit(solution)/shard_map/ppermute | solution.py:595
  50.0 0.4 shard_map.44.handed
  50.4 0.0 copy-start.1
  50.4 1.3 %collective-permute-done.8.other = f32[1280,128]{1,0:T(8,128)S(1)} collective-permute-done((f32[1280,128]{1,0:T(8,128)S(1)}, f32[1280,128]{1,0:T(8,128)S(1)}, u32[]{:S(2)}, u32[]{:S(2)}) %collective-permute-start.8) | collective-permute-done | bytes 655392 | tf_op jit(solution)/shard_map/ppermute | solution.py:595
  51.7 1.7 %shard_map.45 = f32[640,128]{1,0:T(8,128)} custom-call(f32[1280,128]{1,0:T(8,128)S(1)} %bitcast.10, f32[1280,128]{1,0:T(8,128)S(1)} %collective-permute-done.8.other, f32[12,128,128]{2,1,0:T(8,128)S(1)} %shard_map.44.handed), custom_call_target="tpu_custom_call" | custom-call | flops 4194304 | bytes 4194304 | tf_op jit(solution)/shard_map/pallas_call | solution.py:578
  53.4 3.8 %all-to-all-start.1 = ((f32[640,1,128]{2,1,0:T(1,128)}), f32[640,1,128]{2,1,0:T(1,128)S(1)}, u32[]{:S(2)}, u32[]{:S(2)}) async-start(f32[640,1,128]{2,1,0:T(1,128)} %bitcast.4), calls=%async_computation.1 | async-start | bytes 655360 | tf_op jit(solution)/shard_map/all_to_all | solution.py:604
  57.2 4.1 %collective-permute-done.7.over = f32[6,256,256]{2,1,0:T(8,128)} collective-permute-done((f32[6,256,256]{2,1,0:T(8,128)}, f32[6,256,256]{2,1,0:T(8,128)}, u32[]{:S(2)}, u32[]{:S(2)}) %collective-permute-start.7) | collective-permute-done | bytes 1572896 | tf_op jit(solution)/shard_map/ppermute | solution.py:600
  61.3 7.6 %all-to-all-done.1 = f32[640,1,128]{2,1,0:T(1,128)S(1)} async-done(((f32[640,1,128]{2,1,0:T(1,128)}), f32[640,1,128]{2,1,0:T(1,128)S(1)}, u32[]{:S(2)}, u32[]{:S(2)}) %all-to-all-start.1) | async-done | bytes 327712 | tf_op jit(solution)/shard_map/all_to_all | solution.py:604
  68.9 0.0 collective-permute-done.6.own
  68.9 0.0 copy-done.1
  68.9 6.8 %shard_map.46 = (f32[2,256,256]{2,1,0:T(8,128)}, f32[2,256,256]{2,1,0:T(8,128)}) custom-call(f32[2,256,256]{2,1,0:T(8,128)S(1)} %copy-done.1, f32[2,256,256]{2,1,0:T(8,128)S(1)} %collective-permute-done.bs, f32[2,256,256]{2,1,0:T(8,128)S(1)} %collective-permute-done.1.bx, f32[6,256,256]{2,1,0:T(8,128)} %collective-permute-done.6.own, ...), custom_call_target="tpu_custom_call" | custom-call | flops 8388608 | bytes 8388608 | tf_op jit(solution)/shard_map/pallas_call | solution.py:578
  (2 shorter events, 0.0 us)
Async XLA Ops:
  0.6 3.6 %collective-permute-start = (f32[2,256,256]{2,1,0:T(8,128)}, f32[2,256,256]{2,1,0:T(8,128)S(1)}, u32[]{:S(2)}, u32[]{:S(2)}) collective-permute-start(f32[2,256,256]{2,1,0:T(8,128)} %b.5), channel_id=1, source_target_pairs={{0,1},{1,0},{2,3},{3,2},{4,5},{5,4},{6,7},{7,6},{8,9},{9,8},{10,11... | collective-permute-start | bytes 1572872 | tf_op jit(solution)/shard_map/ppermute | solution.py:595
  2.1 8.1 %collective-permute-start.2 = (f32[2,256,256]{2,1,0:T(8,128)}, f32[2,256,256]{2,1,0:T(8,128)S(1)}, u32[]{:S(2)}, u32[]{:S(2)}) collective-permute-start(f32[2,256,256]{2,1,0:T(8,128)} %g.3), channel_id=1, source_target_pairs={{0,1},{1,0},{2,3},{3,2},{4,5},{5,4},{6,7},{7,6},{8,9},{9,8},{10,11... | collective-permute-start | bytes 1572872 | tf_op jit(solution)/shard_map/ppermute | solution.py:595
  2.2 9.1 %collective-permute-start.1 = (f32[2,256,256]{2,1,0:T(8,128)}, f32[2,256,256]{2,1,0:T(8,128)S(1)}, u32[]{:S(2)}, u32[]{:S(2)}) collective-permute-start(f32[2,256,256]{2,1,0:T(8,128)} %b.5), channel_id=1, source_target_pairs={{1,2},{3,4},{5,6},{7,8},{9,10},{11,12},{13,14},{15,16},{17,18},{19... | collective-permute-start | bytes 1572872 | tf_op jit(solution)/shard_map/ppermute | solution.py:600
  4.2 1.1 %copy-start = (f32[2,256,256]{2,1,0:T(8,128)S(1)}, f32[2,256,256]{2,1,0:T(8,128)}, u32[]{:S(2)}) copy-start(f32[2,256,256]{2,1,0:T(8,128)} %b.5) | copy-start | bytes 1572868
  5.3 1.0 %copy-start.2 = (f32[2,256,256]{2,1,0:T(8,128)S(1)}, f32[2,256,256]{2,1,0:T(8,128)}, u32[]{:S(2)}) copy-start(f32[2,256,256]{2,1,0:T(8,128)} %g.3) | copy-start | bytes 1572868
  6.8 15.3 %collective-permute-start.3 = (f32[2,256,256]{2,1,0:T(8,128)S(1)}, f32[2,256,256]{2,1,0:T(8,128)S(1)}, u32[]{:S(2)}, u32[]{:S(2)}) collective-permute-start(f32[2,256,256]{2,1,0:T(8,128)S(1)} %shard_map.41.sent), channel_id=1, source_target_pairs={{1,2},{3,4},{5,6},{7,8},{9,10},{11,12},{13,14},{15,16},{17,18},{19... | collective-permute-start | bytes 1572872 | tf_op jit(solution)/shard_map/ppermute | solution.py:600
  13.9 8.1 %collective-permute-start.4 = (f32[256,256]{1,0:T(8,128)S(1)}, f32[256,256]{1,0:T(8,128)S(1)}, u32[]{:S(2)}, u32[]{:S(2)}) collective-permute-start(f32[256,256]{1,0:T(8,128)S(1)} %get-tuple-element.7), channel_id=1, source_target_pairs={{0,1},{1,0},{2,3},{3,2},{4,5},{5,4},{6,7},{7,6},{8,9},{9,8},{10,11... | collective-permute-start | bytes 786440 | tf_op jit(solution)/shard_map/ppermute | solution.py:595
  23.9 13.1 %collective-permute-start.5 = (f32[6,256,256]{2,1,0:T(8,128)}, f32[6,256,256]{2,1,0:T(8,128)}, u32[]{:S(2)}, u32[]{:S(2)}) collective-permute-start(f32[6,256,256]{2,1,0:T(8,128)} %get-tuple-element.8), channel_id=1, source_target_pairs={{0,1},{1,0},{2,3},{3,2},{4,5},{5,4},{6,7},{7,6},{8,9},{9,8},{10,11... | collective-permute-start | bytes 4718600 | tf_op jit(solution)/shard_map/ppermute | solution.py:595
  24.4 23.9 %all-to-all-start = ((f32[1280,1,128]{2,1,0:T(1,128)}), f32[1280,1,128]{2,1,0:T(1,128)S(1)}, u32[]{:S(2)}, u32[]{:S(2)}) async-start(f32[1280,1,128]{2,1,0:T(1,128)} %bitcast.1), calls=%async_computation | async-start | bytes 1310720 | tf_op jit(solution)/shard_map/all_to_all | solution.py:604
  33.4 27.9 %collective-permute-start.7 = (f32[6,256,256]{2,1,0:T(8,128)}, f32[6,256,256]{2,1,0:T(8,128)}, u32[]{:S(2)}, u32[]{:S(2)}) collective-permute-start(f32[6,256,256]{2,1,0:T(8,128)} %get-tuple-element.8), channel_id=1, source_target_pairs={{1,2},{3,4},{5,6},{7,8},{9,10},{11,12},{13,14},{15,16},{17,18},{19... | collective-permute-start | bytes 4718600 | tf_op jit(solution)/shard_map/ppermute | solution.py:600
  37.0 31.8 %collective-permute-start.6 = (f32[6,256,256]{2,1,0:T(8,128)}, f32[6,256,256]{2,1,0:T(8,128)}, u32[]{:S(2)}, u32[]{:S(2)}) collective-permute-start(f32[6,256,256]{2,1,0:T(8,128)} %collective-permute-done.5.side), channel_id=1, source_target_pairs={{0,1},{1,0},{2,3},{3,2},{4,5},{5,4},{6,7},{7,6},{8,9},{9,8},{10,11... | collective-permute-start | bytes 4718600 | tf_op jit(solution)/shard_map/ppermute | solution.py:595
  48.3 3.4 %collective-permute-start.8 = (f32[1280,128]{1,0:T(8,128)S(1)}, f32[1280,128]{1,0:T(8,128)S(1)}, u32[]{:S(2)}, u32[]{:S(2)}) collective-permute-start(f32[1280,128]{1,0:T(8,128)S(1)} %bitcast.8), channel_id=1, source_target_pairs={{0,1},{1,0},{2,3},{3,2},{4,5},{5,4},{6,7},{7,6},{8,9},{9,8},{10,11... | collective-permute-start | bytes 1966088 | tf_op jit(solution)/shard_map/ppermute | solution.py:595
  50.4 18.5 %copy-start.1 = (f32[2,256,256]{2,1,0:T(8,128)S(1)}, f32[2,256,256]{2,1,0:T(8,128)}, u32[]{:S(2)}) copy-start(f32[2,256,256]{2,1,0:T(8,128)} %b.5) | copy-start | bytes 1572868
  53.4 15.5 %all-to-all-start.1 = ((f32[640,1,128]{2,1,0:T(1,128)}), f32[640,1,128]{2,1,0:T(1,128)S(1)}, u32[]{:S(2)}, u32[]{:S(2)}) async-start(f32[640,1,128]{2,1,0:T(1,128)} %bitcast.4), calls=%async_computation.1 | async-start | bytes 655360 | tf_op jit(solution)/shard_map/all_to_all | solution.py:604

commit v6 on v5

--- a/solution.py
+++ b/solution.py
@@ -384,18 +384,23 @@
         yp = jnp.where(self.lane == 0, 0.0, right(bc[j]))
         self.fz[j] = jnp.where(last, 0.0, 0.125 * (bc[j] + zn))
         self.fy[j] = jnp.where(end, 0.0, 0.125 * (bc[j] + yn))
-        self.dg[j] = 0.75 * bc[j] + 0.125 * (zn + zp + yn + yp + bc[j - 1] + bc[j + 1])
+        self.dg[j] = 0.75 * bc[j] + 0.125 * (zn + zp + yn + yp + bc[j + 1])
+        if j == 0 and j - 1 not in bc:
+            return
+        self.dg[j] = self.dg[j] + 0.125 * bc[j - 1]
         row = self.index + jnp.where(self.par == 0, -j, j)
         inside = (row >= 0) & (row < NC)
         self.iv[j] = jnp.where(inside, 1.0 / jnp.where(inside, self.dg[j], 1.0), 0.0)
 
     def off(self, v, j):
-        total = self.fr[j] * v[j + 1] + self.fr[j - 1] * v[j - 1]
+        total = self.fr[j] * v[j + 1]
+        if j - 1 in v:
+            total = total + self.fr[j - 1] * v[j - 1]
         total = total + self.fz[j] * self.up(v[j]) + self.down(self.fz[j] * v[j])
         return total + self.fy[j] * left(v[j]) + right(self.fy[j] * v[j])
 
 
-HANDED = 12
+HANDED = 16
 
 
 def coarse_first_kernel(recv, handed):
@@ -403,7 +408,7 @@
     u1 = {j: m.load(recv, 0, j, True) for j in range(5)}
     bc = {j: m.load(recv, 1, j, True) for j in range(5)}
     m.fr = {j: 0.125 * (bc[j] + bc[j + 1]) for j in range(4)}
-    for j in (1, 2, 3):
+    for j in (0, 1, 2, 3):
         m.prepare(bc, j)
     (a1, b1), (a2, b2) = COARSE[:2]
     res = {j: (CENTER - 1.0) * m.dg[j] * u1[j] + m.off(u1, j) for j in (1, 2, 3)}
@@ -411,6 +416,7 @@
     second = res[2] - m.dg[2] * step[2] + m.off(step, 2)
     later = a2 * step[2] + b2 * m.iv[2] * second
     found = (m.fr[0], m.fr[1], m.fz[1], m.fy[1], m.dg[1], m.iv[1], res[1], step[1], step[2], later, u1[1], bc[1])
+    found += (m.fz[0], m.fy[0], m.dg[0], m.off(u1, 0))
     for k, value in enumerate(found):
         handed[k] = value
 
@@ -423,12 +429,16 @@
     u1[0], bc[0] = m.load(recv, 0, 0, True), m.load(recv, 1, 0, True)
     m.fr = {j: 0.125 * (bc[j] + bc[j + 1]) for j in range(-4, 0)}
     m.fr[0], m.fr[1], m.fz[1], m.fy[1], m.dg[1], m.iv[1], near, second1, second2, third2, u1[1], bc[1] = (
-        handed[k] for k in range(HANDED)
-    )
-    for j in range(-3, 1):
+        handed[k] for k in range(12)
+    )
+    m.fz[0], m.fy[0], m.dg[0], here = (handed[k] for k in range(12, HANDED))
+    m.dg[0] = m.dg[0] + 0.125 * bc[-1]
+    m.iv[0] = 1.0 / m.dg[0]
+    for j in range(-3, 0):
         m.prepare(bc, j)
     reach = 3
-    res = {j: (CENTER - 1.0) * m.dg[j] * u1[j] + m.off(u1, j) for j in range(-reach, 1)}
+    res = {j: (CENTER - 1.0) * m.dg[j] * u1[j] + m.off(u1, j) for j in range(-reach, 0)}
+    res[0] = (CENTER - 1.0) * m.dg[0] * u1[0] + (here + m.fr[-1] * u1[-1])
     res[1] = near
     step = u1
     total = u1[0]

time: 76.2 us -> 76.1 us (level)
  no operation moved by 1% of the time
where the time goes in v6:
time: 76.1 us; the launch traced here: 75.7 us
  starting transfers between devices  32.7 us (43%)
  waiting for transfers between devices  26.2 us (34%)
  Pallas kernels  13.8 us (18%)
  local copies, waits for them, and re-layouts  2.12 us (3%)
  between operations  0.9 us (1%)
    all_to_all x2, waiting for transfers between devices, everywhere(): lax.all_to_all(v.reshape(rows, 1, NC), AXES, 0, 0, tiled=True)  18.7 us
    pallas_call x6, Pallas kernels, call(): pl.pallas_call(kernel, out_shape=[jax.ShapeDtypeStruct(s, jnp.float32) fo...  13.8 us
    all_to_all x2, starting transfers between devices, everywhere(): lax.all_to_all(v.reshape(rows, 1, NC), AXES, 0, 0, tiled=True)  12.8 us
    ppermute x6, starting transfers between devices, swap(): return lax.ppermute(v, AXES, inside)  10.8 us
    ppermute x3, starting transfers between devices, cross(): return lax.ppermute(v, AXES, across if ends else between)  9.17 us
    ppermute x3, waiting for transfers between devices, cross(): return lax.ppermute(v, AXES, across if ends else between)  5.19 us
    ppermute x6, waiting for transfers between devices, swap(): return lax.ppermute(v, AXES, inside)  2.36 us
    unnamed x6, local copies, waits for them, and re-layouts  2.12 us
  transfers between devices with their start and end apart: 11, of which 6 were waited for; matrix products, arithmetic and copies ran while one was open for 0% of the time, Pallas kernels for 7%

profile of v6, /device:TPU:1, one launch (start us, length us, event | category | flops | bytes accessed | tf_op | source)
XLA Modules:
  0.0 75.7 jit_solution(17999951543885814739)
XLA Ops:
  0.6 1.5 %collective-permute-start = (f32[2,256,256]{2,1,0:T(8,128)}, f32[2,256,256]{2,1,0:T(8,128)S(1)}, u32[]{:S(2)}, u32[]{:S(2)}) collective-permute-start(f32[2,256,256]{2,1,0:T(8,128)} %b.5), channel_id=1, source_target_pairs={{0,1},{1,0},{2,3},{3,2},{4,5},{5,4},{6,7},{7,6},{8,9},{9,8},{10,11... | collective-permute-start | bytes 1572872 | tf_op jit(solution)/shard_map/ppermute | solution.py:605
  2.1 0.1 collective-permute-start.2
  2.2 2.0 %collective-permute-start.1 = (f32[2,256,256]{2,1,0:T(8,128)}, f32[2,256,256]{2,1,0:T(8,128)S(1)}, u32[]{:S(2)}, u32[]{:S(2)}) collective-permute-start(f32[2,256,256]{2,1,0:T(8,128)} %b.5), channel_id=1, source_target_pairs={{1,2},{3,4},{5,6},{7,8},{9,10},{11,12},{13,14},{15,16},{17,18},{19... | collective-permute-start | bytes 1572872 | tf_op jit(solution)/shard_map/ppermute | solution.py:610
  4.2 0.0 collective-permute-done.bs
  4.3 1.1 %copy-done = f32[2,256,256]{2,1,0:T(8,128)S(1)} copy-done((f32[2,256,256]{2,1,0:T(8,128)S(1)}, f32[2,256,256]{2,1,0:T(8,128)}, u32[]{:S(2)}) %copy-start) | copy-done | bytes 524312
  5.3 1.0 %copy-done.2 = f32[2,256,256]{2,1,0:T(8,128)S(1)} copy-done((f32[2,256,256]{2,1,0:T(8,128)S(1)}, f32[2,256,256]{2,1,0:T(8,128)}, u32[]{:S(2)}) %copy-start.2) | copy-done | bytes 524312
  6.4 0.4 shard_map.41.sent
  6.8 3.5 %collective-permute-start.3 = (f32[2,256,256]{2,1,0:T(8,128)S(1)}, f32[2,256,256]{2,1,0:T(8,128)S(1)}, u32[]{:S(2)}, u32[]{:S(2)}) collective-permute-start(f32[2,256,256]{2,1,0:T(8,128)S(1)} %shard_map.41.sent), channel_id=1, source_target_pairs={{1,2},{3,4},{5,6},{7,8},{9,10},{11,12},{13,14},{15,16},{17,18},{19... | collective-permute-start | bytes 1572872 | tf_op jit(solution)/shard_map/ppermute | solution.py:610
  10.3 0.0 collective-permute-done.2.gs
  10.3 1.0 %collective-permute-done.1.bx = f32[2,256,256]{2,1,0:T(8,128)S(1)} collective-permute-done((f32[2,256,256]{2,1,0:T(8,128)}, f32[2,256,256]{2,1,0:T(8,128)S(1)}, u32[]{:S(2)}, u32[]{:S(2)}) %collective-permute-start.1) | collective-permute-done | bytes 524320 | tf_op jit(solution)/shard_map/ppermute | solution.py:610
  11.3 2.6 %shard_map.42 = (f32[21,272,256]{2,1,0:T(8,128)S(1)}, f32[256,256]{1,0:T(8,128)S(1)}) custom-call(f32[2,256,256]{2,1,0:T(8,128)S(1)} %copy-done.2, f32[2,256,256]{2,1,0:T(8,128)S(1)} %collective-permute-done.2.gs, f32[2,256,256]{2,1,0:T(8,128)S(1)} %copy-done, f32[2,256,256]{2,1,0:T(8,128)S(1)} %collective-permute-done.bs, ...), custom_call_target="tpu_custom_call" | custom-call | flops 6291456 | bytes 6291456 | tf_op jit(solution)/shard_map/pallas_call | solution.py:588
  13.9 7.0 %collective-permute-start.4 = (f32[256,256]{1,0:T(8,128)S(1)}, f32[256,256]{1,0:T(8,128)S(1)}, u32[]{:S(2)}, u32[]{:S(2)}) collective-permute-start(f32[256,256]{1,0:T(8,128)S(1)} %get-tuple-element.7), channel_id=1, source_target_pairs={{0,1},{1,0},{2,3},{3,2},{4,5},{5,4},{6,7},{7,6},{8,9},{9,8},{10,11... | collective-permute-start | bytes 786440 | tf_op jit(solution)/shard_map/ppermute | solution.py:605
  20.9 1.2 %collective-permute-done.4.xi = f32[256,256]{1,0:T(8,128)S(1)} collective-permute-done((f32[256,256]{1,0:T(8,128)S(1)}, f32[256,256]{1,0:T(8,128)S(1)}, u32[]{:S(2)}, u32[]{:S(2)}) %collective-permute-start.4) | collective-permute-done | bytes 262176 | tf_op jit(solution)/shard_map/ppermute | solution.py:605
  22.0 0.0 collective-permute-done.3.sx
  22.0 1.9 %shard_map.43 = (f32[1280,128]{1,0:T(8,128)}, f32[6,256,256]{2,1,0:T(8,128)}) custom-call(f32[2,256,256]{2,1,0:T(8,128)S(1)} %collective-permute-done.bs, f32[2,256,256]{2,1,0:T(8,128)S(1)} %collective-permute-done.1.bx, f32[21,272,256]{2,1,0:T(8,128)S(1)} %get-tuple-element.6.state, f32[2,256,256]{2,1,0:T(8,128)S(1)} %collective-permute-done.3.sx, ...), custom_call_target="tpu_custom_call" | custom-call | flops 6291456 | bytes 6291456 | tf_op jit(solution)/shard_map/pallas_call | solution.py:588
  23.9 0.5 collective-permute-start.5
  24.4 9.0 %all-to-all-start = ((f32[1280,1,128]{2,1,0:T(1,128)}), f32[1280,1,128]{2,1,0:T(1,128)S(1)}, u32[]{:S(2)}, u32[]{:S(2)}) async-start(f32[1280,1,128]{2,1,0:T(1,128)} %bitcast.1), calls=%async_computation | async-start | bytes 1310720 | tf_op jit(solution)/shard_map/all_to_all | solution.py:614
  33.4 3.7 %collective-permute-start.7 = (f32[6,256,256]{2,1,0:T(8,128)}, f32[6,256,256]{2,1,0:T(8,128)}, u32[]{:S(2)}, u32[]{:S(2)}) collective-permute-start(f32[6,256,256]{2,1,0:T(8,128)} %get-tuple-element.8), channel_id=1, source_target_pairs={{1,2},{3,4},{5,6},{7,8},{9,10},{11,12},{13,14},{15,16},{17,18},{19... | collective-permute-start | bytes 4718600 | tf_op jit(solution)/shard_map/ppermute | solution.py:610
  37.0 0.0 collective-permute-done.5.side
  37.0 0.1 collective-permute-start.6
  37.1 11.2 %all-to-all-done = f32[1280,1,128]{2,1,0:T(1,128)S(1)} async-done(((f32[1280,1,128]{2,1,0:T(1,128)}), f32[1280,1,128]{2,1,0:T(1,128)S(1)}, u32[]{:S(2)}, u32[]{:S(2)}) %all-to-all-start) | async-done | bytes 655392 | tf_op jit(solution)/shard_map/all_to_all | solution.py:614
  48.3 1.6 %collective-permute-start.8 = (f32[1280,128]{1,0:T(8,128)S(1)}, f32[1280,128]{1,0:T(8,128)S(1)}, u32[]{:S(2)}, u32[]{:S(2)}) collective-permute-start(f32[1280,128]{1,0:T(8,128)S(1)} %bitcast.8), channel_id=1, source_target_pairs={{0,1},{1,0},{2,3},{3,2},{4,5},{5,4},{6,7},{7,6},{8,9},{9,8},{10,11... | collective-permute-start | bytes 1966088 | tf_op jit(solution)/shard_map/ppermute | solution.py:605
  50.0 0.5 shard_map.44.handed
  50.5 0.0 copy-start.1
  50.5 1.2 %collective-permute-done.8.other = f32[1280,128]{1,0:T(8,128)S(1)} collective-permute-done((f32[1280,128]{1,0:T(8,128)S(1)}, f32[1280,128]{1,0:T(8,128)S(1)}, u32[]{:S(2)}, u32[]{:S(2)}) %collective-permute-start.8) | collective-permute-done | bytes 655392 | tf_op jit(solution)/shard_map/ppermute | solution.py:605
  51.7 1.6 %shard_map.45 = f32[640,128]{1,0:T(8,128)} custom-call(f32[1280,128]{1,0:T(8,128)S(1)} %bitcast.10, f32[1280,128]{1,0:T(8,128)S(1)} %collective-permute-done.8.other, f32[16,128,128]{2,1,0:T(8,128)S(1)} %shard_map.44.handed), custom_call_target="tpu_custom_call" | custom-call | flops 4194304 | bytes 4194304 | tf_op jit(solution)/shard_map/pallas_call | solution.py:588
  53.3 3.8 %all-to-all-start.1 = ((f32[640,1,128]{2,1,0:T(1,128)}), f32[640,1,128]{2,1,0:T(1,128)S(1)}, u32[]{:S(2)}, u32[]{:S(2)}) async-start(f32[640,1,128]{2,1,0:T(1,128)} %bitcast.4), calls=%async_computation.1 | async-start | bytes 655360 | tf_op jit(solution)/shard_map/all_to_all | solution.py:614
  57.1 4.1 %collective-permute-done.7.over = f32[6,256,256]{2,1,0:T(8,128)} collective-permute-done((f32[6,256,256]{2,1,0:T(8,128)}, f32[6,256,256]{2,1,0:T(8,128)}, u32[]{:S(2)}, u32[]{:S(2)}) %collective-permute-start.7) | collective-permute-done | bytes 1572896 | tf_op jit(solution)/shard_map/ppermute | solution.py:610
  61.3 7.5 %all-to-all-done.1 = f32[640,1,128]{2,1,0:T(1,128)S(1)} async-done(((f32[640,1,128]{2,1,0:T(1,128)}), f32[640,1,128]{2,1,0:T(1,128)S(1)}, u32[]{:S(2)}, u32[]{:S(2)}) %all-to-all-start.1) | async-done | bytes 327712 | tf_op jit(solution)/shard_map/all_to_all | solution.py:614
  68.8 0.0 collective-permute-done.6.own
  68.8 0.0 copy-done.1
  68.8 6.8 %shard_map.46 = (f32[2,256,256]{2,1,0:T(8,128)}, f32[2,256,256]{2,1,0:T(8,128)}) custom-call(f32[2,256,256]{2,1,0:T(8,128)S(1)} %copy-done.1, f32[2,256,256]{2,1,0:T(8,128)S(1)} %collective-permute-done.bs, f32[2,256,256]{2,1,0:T(8,128)S(1)} %collective-permute-done.1.bx, f32[6,256,256]{2,1,0:T(8,128)} %collective-permute-done.6.own, ...), custom_call_target="tpu_custom_call" | custom-call | flops 8388608 | bytes 8388608 | tf_op jit(solution)/shard_map/pallas_call | solution.py:588
  (2 shorter events, 0.0 us)
Async XLA Ops:
  0.6 3.6 %collective-permute-start = (f32[2,256,256]{2,1,0:T(8,128)}, f32[2,256,256]{2,1,0:T(8,128)S(1)}, u32[]{:S(2)}, u32[]{:S(2)}) collective-permute-start(f32[2,256,256]{2,1,0:T(8,128)} %b.5), channel_id=1, source_target_pairs={{0,1},{1,0},{2,3},{3,2},{4,5},{5,4},{6,7},{7,6},{8,9},{9,8},{10,11... | collective-permute-start | bytes 1572872 | tf_op jit(solution)/shard_map/ppermute | solution.py:605
  2.1 8.1 %collective-permute-start.2 = (f32[2,256,256]{2,1,0:T(8,128)}, f32[2,256,256]{2,1,0:T(8,128)S(1)}, u32[]{:S(2)}, u32[]{:S(2)}) collective-permute-start(f32[2,256,256]{2,1,0:T(8,128)} %g.3), channel_id=1, source_target_pairs={{0,1},{1,0},{2,3},{3,2},{4,5},{5,4},{6,7},{7,6},{8,9},{9,8},{10,11... | collective-permute-start | bytes 1572872 | tf_op jit(solution)/shard_map/ppermute | solution.py:605
  2.2 9.1 %collective-permute-start.1 = (f32[2,256,256]{2,1,0:T(8,128)}, f32[2,256,256]{2,1,0:T(8,128)S(1)}, u32[]{:S(2)}, u32[]{:S(2)}) collective-permute-start(f32[2,256,256]{2,1,0:T(8,128)} %b.5), channel_id=1, source_target_pairs={{1,2},{3,4},{5,6},{7,8},{9,10},{11,12},{13,14},{15,16},{17,18},{19... | collective-permute-start | bytes 1572872 | tf_op jit(solution)/shard_map/ppermute | solution.py:610
  4.2 1.1 %copy-start = (f32[2,256,256]{2,1,0:T(8,128)S(1)}, f32[2,256,256]{2,1,0:T(8,128)}, u32[]{:S(2)}) copy-start(f32[2,256,256]{2,1,0:T(8,128)} %b.5) | copy-start | bytes 1572868
  5.3 1.0 %copy-start.2 = (f32[2,256,256]{2,1,0:T(8,128)S(1)}, f32[2,256,256]{2,1,0:T(8,128)}, u32[]{:S(2)}) copy-start(f32[2,256,256]{2,1,0:T(8,128)} %g.3) | copy-start | bytes 1572868
  6.8 15.3 %collective-permute-start.3 = (f32[2,256,256]{2,1,0:T(8,128)S(1)}, f32[2,256,256]{2,1,0:T(8,128)S(1)}, u32[]{:S(2)}, u32[]{:S(2)}) collective-permute-start(f32[2,256,256]{2,1,0:T(8,128)S(1)} %shard_map.41.sent), channel_id=1, source_target_pairs={{1,2},{3,4},{5,6},{7,8},{9,10},{11,12},{13,14},{15,16},{17,18},{19... | collective-permute-start | bytes 1572872 | tf_op jit(solution)/shard_map/ppermute | solution.py:610
  13.9 8.1 %collective-permute-start.4 = (f32[256,256]{1,0:T(8,128)S(1)}, f32[256,256]{1,0:T(8,128)S(1)}, u32[]{:S(2)}, u32[]{:S(2)}) collective-permute-start(f32[256,256]{1,0:T(8,128)S(1)} %get-tuple-element.7), channel_id=1, source_target_pairs={{0,1},{1,0},{2,3},{3,2},{4,5},{5,4},{6,7},{7,6},{8,9},{9,8},{10,11... | collective-permute-start | bytes 786440 | tf_op jit(solution)/shard_map/ppermute | solution.py:605
  23.9 13.1 %collective-permute-start.5 = (f32[6,256,256]{2,1,0:T(8,128)}, f32[6,256,256]{2,1,0:T(8,128)}, u32[]{:S(2)}, u32[]{:S(2)}) collective-permute-start(f32[6,256,256]{2,1,0:T(8,128)} %get-tuple-element.8), channel_id=1, source_target_pairs={{0,1},{1,0},{2,3},{3,2},{4,5},{5,4},{6,7},{7,6},{8,9},{9,8},{10,11... | collective-permute-start | bytes 4718600 | tf_op jit(solution)/shard_map/ppermute | solution.py:605
  24.4 23.9 %all-to-all-start = ((f32[1280,1,128]{2,1,0:T(1,128)}), f32[1280,1,128]{2,1,0:T(1,128)S(1)}, u32[]{:S(2)}, u32[]{:S(2)}) async-start(f32[1280,1,128]{2,1,0:T(1,128)} %bitcast.1), calls=%async_computation | async-start | bytes 1310720 | tf_op jit(solution)/shard_map/all_to_all | solution.py:614
  33.4 27.9 %collective-permute-start.7 = (f32[6,256,256]{2,1,0:T(8,128)}, f32[6,256,256]{2,1,0:T(8,128)}, u32[]{:S(2)}, u32[]{:S(2)}) collective-permute-start(f32[6,256,256]{2,1,0:T(8,128)} %get-tuple-element.8), channel_id=1, source_target_pairs={{1,2},{3,4},{5,6},{7,8},{9,10},{11,12},{13,14},{15,16},{17,18},{19... | collective-permute-start | bytes 4718600 | tf_op jit(solution)/shard_map/ppermute | solution.py:610
  37.0 31.7 %collective-permute-start.6 = (f32[6,256,256]{2,1,0:T(8,128)}, f32[6,256,256]{2,1,0:T(8,128)}, u32[]{:S(2)}, u32[]{:S(2)}) collective-permute-start(f32[6,256,256]{2,1,0:T(8,128)} %collective-permute-done.5.side), channel_id=1, source_target_pairs={{0,1},{1,0},{2,3},{3,2},{4,5},{5,4},{6,7},{7,6},{8,9},{9,8},{10,11... | collective-permute-start | bytes 4718600 | tf_op jit(solution)/shard_map/ppermute | solution.py:605
  48.3 3.4 %collective-permute-start.8 = (f32[1280,128]{1,0:T(8,128)S(1)}, f32[1280,128]{1,0:T(8,128)S(1)}, u32[]{:S(2)}, u32[]{:S(2)}) collective-permute-start(f32[1280,128]{1,0:T(8,128)S(1)} %bitcast.8), channel_id=1, source_target_pairs={{0,1},{1,0},{2,3},{3,2},{4,5},{5,4},{6,7},{7,6},{8,9},{9,8},{10,11... | collective-permute-start | bytes 1966088 | tf_op jit(solution)/shard_map/ppermute | solution.py:605
  50.5 18.3 %copy-start.1 = (f32[2,256,256]{2,1,0:T(8,128)S(1)}, f32[2,256,256]{2,1,0:T(8,128)}, u32[]{:S(2)}) copy-start(f32[2,256,256]{2,1,0:T(8,128)} %b.5) | copy-start | bytes 1572868
  53.3 15.5 %all-to-all-start.1 = ((f32[640,1,128]{2,1,0:T(1,128)}), f32[640,1,128]{2,1,0:T(1,128)S(1)}, u32[]{:S(2)}, u32[]{:S(2)}) async-start(f32[640,1,128]{2,1,0:T(1,128)} %bitcast.4), calls=%async_computation.1 | async-start | bytes 655360 | tf_op jit(solution)/shard_map/all_to_all | solution.py:614

commit v7 on v6

--- a/solution.py
+++ b/solution.py
@@ -278,7 +278,7 @@
     state[COARSE_AT, 0:NC, NC:N] = 1.0 / (CENTER * diag)
 
 
-SPLIT = 2
+SPLIT = 4
 HELD = 5
 
 

time: 76.1 us -> 76.1 us (level)
  no operation moved by 1% of the time
where the time goes in v7:
time: 76.1 us; the launch traced here: 75.7 us
  starting transfers between devices  32.7 us (43%)
  waiting for transfers between devices  26.2 us (34%)
  Pallas kernels  13.8 us (18%)
  local copies, waits for them, and re-layouts  2.12 us (3%)
  between operations  0.9 us (1%)
    all_to_all x2, waiting for transfers between devices, everywhere(): lax.all_to_all(v.reshape(rows, 1, NC), AXES, 0, 0, tiled=True)  18.7 us
    pallas_call x6, Pallas kernels, call(): pl.pallas_call(kernel, out_shape=[jax.ShapeDtypeStruct(s, jnp.float32) fo...  13.8 us
    all_to_all x2, starting transfers between devices, everywhere(): lax.all_to_all(v.reshape(rows, 1, NC), AXES, 0, 0, tiled=True)  12.8 us
    ppermute x6, starting transfers between devices, swap(): return lax.ppermute(v, AXES, inside)  10.8 us
    ppermute x3, starting transfers between devices, cross(): return lax.ppermute(v, AXES, across if ends else between)  9.17 us
    ppermute x3, waiting for transfers between devices, cross(): return lax.ppermute(v, AXES, across if ends else between)  5.19 us
    ppermute x6, waiting for transfers between devices, swap(): return lax.ppermute(v, AXES, inside)  2.36 us
    unnamed x6, local copies, waits for them, and re-layouts  2.12 us
  transfers between devices with their start and end apart: 11, of which 6 were waited for; matrix products, arithmetic and copies ran while one was open for 0% of the time, Pallas kernels for 7%

profile of v7, /device:TPU:1, one launch (start us, length us, event | category | flops | bytes accessed | tf_op | source)
XLA Modules:
  0.0 75.7 jit_solution(2428636370594976730)
XLA Ops:
  0.6 1.5 %collective-permute-start = (f32[2,256,256]{2,1,0:T(8,128)}, f32[2,256,256]{2,1,0:T(8,128)S(1)}, u32[]{:S(2)}, u32[]{:S(2)}) collective-permute-start(f32[2,256,256]{2,1,0:T(8,128)} %b.5), channel_id=1, source_target_pairs={{0,1},{1,0},{2,3},{3,2},{4,5},{5,4},{6,7},{7,6},{8,9},{9,8},{10,11... | collective-permute-start | bytes 1572872 | tf_op jit(solution)/shard_map/ppermute | solution.py:605
  2.1 0.1 collective-permute-start.2
  2.2 2.0 %collective-permute-start.1 = (f32[2,256,256]{2,1,0:T(8,128)}, f32[2,256,256]{2,1,0:T(8,128)S(1)}, u32[]{:S(2)}, u32[]{:S(2)}) collective-permute-start(f32[2,256,256]{2,1,0:T(8,128)} %b.5), channel_id=1, source_target_pairs={{1,2},{3,4},{5,6},{7,8},{9,10},{11,12},{13,14},{15,16},{17,18},{19... | collective-permute-start | bytes 1572872 | tf_op jit(solution)/shard_map/ppermute | solution.py:610
  4.2 0.0 collective-permute-done.bs
  4.3 1.1 %copy-done = f32[2,256,256]{2,1,0:T(8,128)S(1)} copy-done((f32[2,256,256]{2,1,0:T(8,128)S(1)}, f32[2,256,256]{2,1,0:T(8,128)}, u32[]{:S(2)}) %copy-start) | copy-done | bytes 524312
  5.3 1.0 %copy-done.2 = f32[2,256,256]{2,1,0:T(8,128)S(1)} copy-done((f32[2,256,256]{2,1,0:T(8,128)S(1)}, f32[2,256,256]{2,1,0:T(8,128)}, u32[]{:S(2)}) %copy-start.2) | copy-done | bytes 524312
  6.4 0.4 shard_map.41.sent
  6.8 3.5 %collective-permute-start.3 = (f32[2,256,256]{2,1,0:T(8,128)S(1)}, f32[2,256,256]{2,1,0:T(8,128)S(1)}, u32[]{:S(2)}, u32[]{:S(2)}) collective-permute-start(f32[2,256,256]{2,1,0:T(8,128)S(1)} %shard_map.41.sent), channel_id=1, source_target_pairs={{1,2},{3,4},{5,6},{7,8},{9,10},{11,12},{13,14},{15,16},{17,18},{19... | collective-permute-start | bytes 1572872 | tf_op jit(solution)/shard_map/ppermute | solution.py:610
  10.3 0.0 collective-permute-done.2.gs
  10.3 1.0 %collective-permute-done.1.bx = f32[2,256,256]{2,1,0:T(8,128)S(1)} collective-permute-done((f32[2,256,256]{2,1,0:T(8,128)}, f32[2,256,256]{2,1,0:T(8,128)S(1)}, u32[]{:S(2)}, u32[]{:S(2)}) %collective-permute-start.1) | collective-permute-done | bytes 524320 | tf_op jit(solution)/shard_map/ppermute | solution.py:610
  11.3 2.6 %shard_map.42 = (f32[21,272,256]{2,1,0:T(8,128)S(1)}, f32[256,256]{1,0:T(8,128)S(1)}) custom-call(f32[2,256,256]{2,1,0:T(8,128)S(1)} %copy-done.2, f32[2,256,256]{2,1,0:T(8,128)S(1)} %collective-permute-done.2.gs, f32[2,256,256]{2,1,0:T(8,128)S(1)} %copy-done, f32[2,256,256]{2,1,0:T(8,128)S(1)} %collective-permute-done.bs, ...), custom_call_target="tpu_custom_call" | custom-call | flops 6291456 | bytes 6291456 | tf_op jit(solution)/shard_map/pallas_call | solution.py:588
  13.9 7.0 %collective-permute-start.4 = (f32[256,256]{1,0:T(8,128)S(1)}, f32[256,256]{1,0:T(8,128)S(1)}, u32[]{:S(2)}, u32[]{:S(2)}) collective-permute-start(f32[256,256]{1,0:T(8,128)S(1)} %get-tuple-element.7), channel_id=1, source_target_pairs={{0,1},{1,0},{2,3},{3,2},{4,5},{5,4},{6,7},{7,6},{8,9},{9,8},{10,11... | collective-permute-start | bytes 786440 | tf_op jit(solution)/shard_map/ppermute | solution.py:605
  20.9 1.2 %collective-permute-done.4.xi = f32[256,256]{1,0:T(8,128)S(1)} collective-permute-done((f32[256,256]{1,0:T(8,128)S(1)}, f32[256,256]{1,0:T(8,128)S(1)}, u32[]{:S(2)}, u32[]{:S(2)}) %collective-permute-start.4) | collective-permute-done | bytes 262176 | tf_op jit(solution)/shard_map/ppermute | solution.py:605
  22.0 0.0 collective-permute-done.3.sx
  22.0 1.9 %shard_map.43 = (f32[1280,128]{1,0:T(8,128)}, f32[6,256,256]{2,1,0:T(8,128)}) custom-call(f32[2,256,256]{2,1,0:T(8,128)S(1)} %collective-permute-done.bs, f32[2,256,256]{2,1,0:T(8,128)S(1)} %collective-permute-done.1.bx, f32[21,272,256]{2,1,0:T(8,128)S(1)} %get-tuple-element.6.state, f32[2,256,256]{2,1,0:T(8,128)S(1)} %collective-permute-done.3.sx, ...), custom_call_target="tpu_custom_call" | custom-call | flops 6291456 | bytes 6291456 | tf_op jit(solution)/shard_map/pallas_call | solution.py:588
  23.9 0.5 collective-permute-start.5
  24.4 9.0 %all-to-all-start = ((f32[1280,1,128]{2,1,0:T(1,128)}), f32[1280,1,128]{2,1,0:T(1,128)S(1)}, u32[]{:S(2)}, u32[]{:S(2)}) async-start(f32[1280,1,128]{2,1,0:T(1,128)} %bitcast.1), calls=%async_computation | async-start | bytes 1310720 | tf_op jit(solution)/shard_map/all_to_all | solution.py:614
  33.4 3.7 %collective-permute-start.7 = (f32[6,256,256]{2,1,0:T(8,128)}, f32[6,256,256]{2,1,0:T(8,128)}, u32[]{:S(2)}, u32[]{:S(2)}) collective-permute-start(f32[6,256,256]{2,1,0:T(8,128)} %get-tuple-element.8), channel_id=1, source_target_pairs={{1,2},{3,4},{5,6},{7,8},{9,10},{11,12},{13,14},{15,16},{17,18},{19... | collective-permute-start | bytes 4718600 | tf_op jit(solution)/shard_map/ppermute | solution.py:610
  37.0 0.0 collective-permute-done.5.side
  37.0 0.1 collective-permute-start.6
  37.1 11.2 %all-to-all-done = f32[1280,1,128]{2,1,0:T(1,128)S(1)} async-done(((f32[1280,1,128]{2,1,0:T(1,128)}), f32[1280,1,128]{2,1,0:T(1,128)S(1)}, u32[]{:S(2)}, u32[]{:S(2)}) %all-to-all-start) | async-done | bytes 655392 | tf_op jit(solution)/shard_map/all_to_all | solution.py:614
  48.3 1.6 %collective-permute-start.8 = (f32[1280,128]{1,0:T(8,128)S(1)}, f32[1280,128]{1,0:T(8,128)S(1)}, u32[]{:S(2)}, u32[]{:S(2)}) collective-permute-start(f32[1280,128]{1,0:T(8,128)S(1)} %bitcast.8), channel_id=1, source_target_pairs={{0,1},{1,0},{2,3},{3,2},{4,5},{5,4},{6,7},{7,6},{8,9},{9,8},{10,11... | collective-permute-start | bytes 1966088 | tf_op jit(solution)/shard_map/ppermute | solution.py:605
  50.0 0.5 shard_map.44.handed
  50.5 0.0 copy-start.1
  50.5 1.2 %collective-permute-done.8.other = f32[1280,128]{1,0:T(8,128)S(1)} collective-permute-done((f32[1280,128]{1,0:T(8,128)S(1)}, f32[1280,128]{1,0:T(8,128)S(1)}, u32[]{:S(2)}, u32[]{:S(2)}) %collective-permute-start.8) | collective-permute-done | bytes 655392 | tf_op jit(solution)/shard_map/ppermute | solution.py:605
  51.7 1.6 %shard_map.45 = f32[640,128]{1,0:T(8,128)} custom-call(f32[1280,128]{1,0:T(8,128)S(1)} %bitcast.10, f32[1280,128]{1,0:T(8,128)S(1)} %collective-permute-done.8.other, f32[16,128,128]{2,1,0:T(8,128)S(1)} %shard_map.44.handed), custom_call_target="tpu_custom_call" | custom-call | flops 4194304 | bytes 4194304 | tf_op jit(solution)/shard_map/pallas_call | solution.py:588
  53.3 3.8 %all-to-all-start.1 = ((f32[640,1,128]{2,1,0:T(1,128)}), f32[640,1,128]{2,1,0:T(1,128)S(1)}, u32[]{:S(2)}, u32[]{:S(2)}) async-start(f32[640,1,128]{2,1,0:T(1,128)} %bitcast.4), calls=%async_computation.1 | async-start | bytes 655360 | tf_op jit(solution)/shard_map/all_to_all | solution.py:614
  57.1 4.1 %collective-permute-done.7.over = f32[6,256,256]{2,1,0:T(8,128)} collective-permute-done((f32[6,256,256]{2,1,0:T(8,128)}, f32[6,256,256]{2,1,0:T(8,128)}, u32[]{:S(2)}, u32[]{:S(2)}) %collective-permute-start.7) | collective-permute-done | bytes 1572896 | tf_op jit(solution)/shard_map/ppermute | solution.py:610
  61.3 7.5 %all-to-all-done.1 = f32[640,1,128]{2,1,0:T(1,128)S(1)} async-done(((f32[640,1,128]{2,1,0:T(1,128)}), f32[640,1,128]{2,1,0:T(1,128)S(1)}, u32[]{:S(2)}, u32[]{:S(2)}) %all-to-all-start.1) | async-done | bytes 327712 | tf_op jit(solution)/shard_map/all_to_all | solution.py:614
  68.8 0.0 collective-permute-done.6.own
  68.8 0.0 copy-done.1
  68.8 6.8 %shard_map.46 = (f32[2,256,256]{2,1,0:T(8,128)}, f32[2,256,256]{2,1,0:T(8,128)}) custom-call(f32[2,256,256]{2,1,0:T(8,128)S(1)} %copy-done.1, f32[2,256,256]{2,1,0:T(8,128)S(1)} %collective-permute-done.bs, f32[2,256,256]{2,1,0:T(8,128)S(1)} %collective-permute-done.1.bx, f32[6,256,256]{2,1,0:T(8,128)} %collective-permute-done.6.own, ...), custom_call_target="tpu_custom_call" | custom-call | flops 8388608 | bytes 8388608 | tf_op jit(solution)/shard_map/pallas_call | solution.py:588
  (2 shorter events, 0.0 us)
Async XLA Ops:
  0.6 3.6 %collective-permute-start = (f32[2,256,256]{2,1,0:T(8,128)}, f32[2,256,256]{2,1,0:T(8,128)S(1)}, u32[]{:S(2)}, u32[]{:S(2)}) collective-permute-start(f32[2,256,256]{2,1,0:T(8,128)} %b.5), channel_id=1, source_target_pairs={{0,1},{1,0},{2,3},{3,2},{4,5},{5,4},{6,7},{7,6},{8,9},{9,8},{10,11... | collective-permute-start | bytes 1572872 | tf_op jit(solution)/shard_map/ppermute | solution.py:605
  2.1 8.1 %collective-permute-start.2 = (f32[2,256,256]{2,1,0:T(8,128)}, f32[2,256,256]{2,1,0:T(8,128)S(1)}, u32[]{:S(2)}, u32[]{:S(2)}) collective-permute-start(f32[2,256,256]{2,1,0:T(8,128)} %g.3), channel_id=1, source_target_pairs={{0,1},{1,0},{2,3},{3,2},{4,5},{5,4},{6,7},{7,6},{8,9},{9,8},{10,11... | collective-permute-start | bytes 1572872 | tf_op jit(solution)/shard_map/ppermute | solution.py:605
  2.2 9.1 %collective-permute-start.1 = (f32[2,256,256]{2,1,0:T(8,128)}, f32[2,256,256]{2,1,0:T(8,128)S(1)}, u32[]{:S(2)}, u32[]{:S(2)}) collective-permute-start(f32[2,256,256]{2,1,0:T(8,128)} %b.5), channel_id=1, source_target_pairs={{1,2},{3,4},{5,6},{7,8},{9,10},{11,12},{13,14},{15,16},{17,18},{19... | collective-permute-start | bytes 1572872 | tf_op jit(solution)/shard_map/ppermute | solution.py:610
  4.2 1.1 %copy-start = (f32[2,256,256]{2,1,0:T(8,128)S(1)}, f32[2,256,256]{2,1,0:T(8,128)}, u32[]{:S(2)}) copy-start(f32[2,256,256]{2,1,0:T(8,128)} %b.5) | copy-start | bytes 1572868
  5.3 1.0 %copy-start.2 = (f32[2,256,256]{2,1,0:T(8,128)S(1)}, f32[2,256,256]{2,1,0:T(8,128)}, u32[]{:S(2)}) copy-start(f32[2,256,256]{2,1,0:T(8,128)} %g.3) | copy-start | bytes 1572868
  6.8 15.3 %collective-permute-start.3 = (f32[2,256,256]{2,1,0:T(8,128)S(1)}, f32[2,256,256]{2,1,0:T(8,128)S(1)}, u32[]{:S(2)}, u32[]{:S(2)}) collective-permute-start(f32[2,256,256]{2,1,0:T(8,128)S(1)} %shard_map.41.sent), channel_id=1, source_target_pairs={{1,2},{3,4},{5,6},{7,8},{9,10},{11,12},{13,14},{15,16},{17,18},{19... | collective-permute-start | bytes 1572872 | tf_op jit(solution)/shard_map/ppermute | solution.py:610
  13.9 8.1 %collective-permute-start.4 = (f32[256,256]{1,0:T(8,128)S(1)}, f32[256,256]{1,0:T(8,128)S(1)}, u32[]{:S(2)}, u32[]{:S(2)}) collective-permute-start(f32[256,256]{1,0:T(8,128)S(1)} %get-tuple-element.7), channel_id=1, source_target_pairs={{0,1},{1,0},{2,3},{3,2},{4,5},{5,4},{6,7},{7,6},{8,9},{9,8},{10,11... | collective-permute-start | bytes 786440 | tf_op jit(solution)/shard_map/ppermute | solution.py:605
  23.9 13.1 %collective-permute-start.5 = (f32[6,256,256]{2,1,0:T(8,128)}, f32[6,256,256]{2,1,0:T(8,128)}, u32[]{:S(2)}, u32[]{:S(2)}) collective-permute-start(f32[6,256,256]{2,1,0:T(8,128)} %get-tuple-element.8), channel_id=1, source_target_pairs={{0,1},{1,0},{2,3},{3,2},{4,5},{5,4},{6,7},{7,6},{8,9},{9,8},{10,11... | collective-permute-start | bytes 4718600 | tf_op jit(solution)/shard_map/ppermute | solution.py:605
  24.4 23.9 %all-to-all-start = ((f32[1280,1,128]{2,1,0:T(1,128)}), f32[1280,1,128]{2,1,0:T(1,128)S(1)}, u32[]{:S(2)}, u32[]{:S(2)}) async-start(f32[1280,1,128]{2,1,0:T(1,128)} %bitcast.1), calls=%async_computation | async-start | bytes 1310720 | tf_op jit(solution)/shard_map/all_to_all | solution.py:614
  33.4 27.9 %collective-permute-start.7 = (f32[6,256,256]{2,1,0:T(8,128)}, f32[6,256,256]{2,1,0:T(8,128)}, u32[]{:S(2)}, u32[]{:S(2)}) collective-permute-start(f32[6,256,256]{2,1,0:T(8,128)} %get-tuple-element.8), channel_id=1, source_target_pairs={{1,2},{3,4},{5,6},{7,8},{9,10},{11,12},{13,14},{15,16},{17,18},{19... | collective-permute-start | bytes 4718600 | tf_op jit(solution)/shard_map/ppermute | solution.py:610
  37.0 31.7 %collective-permute-start.6 = (f32[6,256,256]{2,1,0:T(8,128)}, f32[6,256,256]{2,1,0:T(8,128)}, u32[]{:S(2)}, u32[]{:S(2)}) collective-permute-start(f32[6,256,256]{2,1,0:T(8,128)} %collective-permute-done.5.side), channel_id=1, source_target_pairs={{0,1},{1,0},{2,3},{3,2},{4,5},{5,4},{6,7},{7,6},{8,9},{9,8},{10,11... | collective-permute-start | bytes 4718600 | tf_op jit(solution)/shard_map/ppermute | solution.py:605
  48.3 3.4 %collective-permute-start.8 = (f32[1280,128]{1,0:T(8,128)S(1)}, f32[1280,128]{1,0:T(8,128)S(1)}, u32[]{:S(2)}, u32[]{:S(2)}) collective-permute-start(f32[1280,128]{1,0:T(8,128)S(1)} %bitcast.8), channel_id=1, source_target_pairs={{0,1},{1,0},{2,3},{3,2},{4,5},{5,4},{6,7},{7,6},{8,9},{9,8},{10,11... | collective-permute-start | bytes 1966088 | tf_op jit(solution)/shard_map/ppermute | solution.py:605
  50.5 18.3 %copy-start.1 = (f32[2,256,256]{2,1,0:T(8,128)S(1)}, f32[2,256,256]{2,1,0:T(8,128)}, u32[]{:S(2)}) copy-start(f32[2,256,256]{2,1,0:T(8,128)} %b.5) | copy-start | bytes 1572868
  53.3 15.5 %all-to-all-start.1 = ((f32[640,1,128]{2,1,0:T(1,128)}), f32[640,1,128]{2,1,0:T(1,128)S(1)}, u32[]{:S(2)}, u32[]{:S(2)}) async-start(f32[640,1,128]{2,1,0:T(1,128)} %bitcast.4), calls=%async_computation.1 | async-start | bytes 655360 | tf_op jit(solution)/shard_map/all_to_all | solution.py:614
